TPU v7x, 256 devices: a whole 4x4x8 slice. The times are simulated.
256 devices in a mesh: src: 32 (over y, z), tgt: 8 (over x, core).
Axes of the slice: x: 4, y: 4, z: 8, core: 2. Of those that a mesh axis runs over, the one named last changes fastest.
Arguments:
- source_points: bfloat16 [32768, 128], P('src'), may hold values from -2 to 2
- target_points: bfloat16 [32768, 128], P(('tgt', 'src')), may hold values from -2 to 2
- initial_potential: float32 [32768], P('tgt'), may hold values from -4 to 4
- pair_list: int32 [32, 8, 16], P('src', 'tgt'), may hold values from -1 to 15, as said below
- pair_count: int32 [32, 8], P('src', 'tgt'), may hold values from 2 to 16, as said below
Outputs:
- source_potential: float32 [32768], P('src')
- target_potential: float32 [32768], P('tgt')
Inputs may be any that keep to these rules, and one draw needn't show every extreme that they name: `pair_count`: every source block and every target block is in at least one kept pair; the device with the most kept pairs holds all 16. `pair_list`: entries in slots below the device's pair_count are distinct local pair numbers b * 8 + c (b the source block, c the target block within the device's points); the other slots hold -1.
All inputs are finite; a program needn't handle non-finite values.
Results may differ from a plain program's by a relative error of at most 0.0003.
Values may be sent and summed in bfloat16 or wider, within the bound.
No kernel may reach another device: no remote copies, remote signals or barrier semaphores. Data moves between devices by JAX's collectives and lax.ppermute only.
A program may use at most 64 MiB of HBM per device.

v0:
```python
import math

import jax
import jax.numpy as jnp
from jax import lax
from jax.sharding import PartitionSpec as P

BLOCK = 512
TB_DEV = 8
ITERS = 2


NEG_START = -1e30
EPS_REG = 0.2


def joined(array, axis, combine):
    everything = jax.tree.map(lambda part: lax.all_gather(part, axis), array)
    initial = jax.tree.map(lambda part: part[0], everything)

    def turn(k, so_far):
        return combine(so_far, jax.tree.map(lambda part: part[k], everything))

    return lax.fori_loop(1, lax.axis_size(axis), turn, initial)


def pair_cost(sources, targets, source_sq, target_sq, src_start, tgt_start):
    rows = lax.dynamic_slice_in_dim(sources, src_start, BLOCK, 0)
    cols = lax.dynamic_slice_in_dim(targets, tgt_start, BLOCK, 0)
    inner = lax.dot_general(
        rows, cols, (((1,), (1,)), ((), ())), preferred_element_type=jnp.float32
    )
    row_sq = lax.dynamic_slice_in_dim(source_sq, src_start, BLOCK, 0)
    col_sq = lax.dynamic_slice_in_dim(target_sq, tgt_start, BLOCK, 0)
    return row_sq[:, None] + col_sq[None, :] - 2.0 * inner


def combine_stats(first, second):
    highest = jnp.maximum(first[0], second[0])
    return (
        highest,
        first[1] * jnp.exp(first[0] - highest) + second[1] * jnp.exp(second[0] - highest),
    )


def fold_block(running, place, block_max, block_sum):
    old_max = lax.dynamic_slice_in_dim(running[0], place, BLOCK, 0)
    old_sum = lax.dynamic_slice_in_dim(running[1], place, BLOCK, 0)
    highest = jnp.maximum(old_max, block_max)
    new_sum = old_sum * jnp.exp(old_max - highest) + block_sum * jnp.exp(block_max - highest)
    return (
        lax.dynamic_update_slice_in_dim(running[0], highest, place, 0),
        lax.dynamic_update_slice_in_dim(running[1], new_sum, place, 0),
    )


def per_device(source_points, target_points, initial_potential, pair_list, pair_count):
    targets = lax.all_gather(target_points, "src", axis=0, tiled=True)
    n_source = source_points.shape[0] * lax.axis_size("src")
    n_target = targets.shape[0] * lax.axis_size("tgt")
    src_rows = source_points.shape[0]
    tgt_rows = targets.shape[0]
    source_sq = jnp.sum(jnp.square(source_points.astype(jnp.float32)), axis=1)
    target_sq = jnp.sum(jnp.square(targets.astype(jnp.float32)), axis=1)
    pairs = pair_list.reshape(-1)
    total = pair_count.reshape(())

    def starts(number):
        local_pair = pairs[number]
        return (local_pair // TB_DEV * BLOCK, local_pair % TB_DEV * BLOCK)

    def row_scores(number, potential):
        src_start, tgt_start = starts(number)
        cost = pair_cost(source_points, targets, source_sq, target_sq, src_start, tgt_start)
        shift = lax.dynamic_slice_in_dim(potential, tgt_start, BLOCK, 0)
        return ((shift[None, :] - cost) / EPS_REG, src_start)

    def col_scores(number, potential):
        src_start, tgt_start = starts(number)
        cost = pair_cost(source_points, targets, source_sq, target_sq, src_start, tgt_start)
        shift = lax.dynamic_slice_in_dim(potential, src_start, BLOCK, 0)
        return ((shift[:, None] - cost) / EPS_REG, tgt_start)

    target_potential = initial_potential
    source_potential = jnp.zeros((src_rows,), jnp.float32)
    for iteration in range(ITERS):
        row_potential = target_potential

        def max_pass(number, highest):
            scores, place = row_scores(number, row_potential)
            old_max = lax.dynamic_slice_in_dim(highest, place, BLOCK, 0)
            return lax.dynamic_update_slice_in_dim(
                highest, jnp.maximum(old_max, jnp.max(scores, axis=1)), place, 0
            )

        local_max = lax.fori_loop(0, total, max_pass, jnp.full((src_rows,), NEG_START, jnp.float32))
        highest = lax.pmax(local_max, "tgt")

        def sum_pass(number, summed):
            scores, place = row_scores(number, row_potential)
            shift = lax.dynamic_slice_in_dim(highest, place, BLOCK, 0)
            block_sum = jnp.sum(jnp.exp(scores - shift[:, None]), axis=1)
            old_sum = lax.dynamic_slice_in_dim(summed, place, BLOCK, 0)
            return lax.dynamic_update_slice_in_dim(summed, old_sum + block_sum, place, 0)

        local_sum = lax.fori_loop(0, total, sum_pass, jnp.zeros((src_rows,), jnp.float32))
        summed = lax.psum(local_sum, "tgt")
        source_potential = EPS_REG * (-math.log(n_source) - (highest + jnp.log(summed)))
        col_potential = source_potential
        col_empty = (
            jnp.full((tgt_rows,), NEG_START, jnp.float32),
            jnp.zeros((tgt_rows,), jnp.float32),
        )

        def online_pass(number, running):
            scores, place = col_scores(number, col_potential)
            block_max = jnp.max(scores, axis=0)
            block_sum = jnp.sum(jnp.exp(scores - block_max[None, :]), axis=0)
            return fold_block(running, place, block_max, block_sum)

        local_stats = lax.fori_loop(0, total, online_pass, col_empty)
        col_highest, col_summed = joined((local_stats[0], local_stats[1]), "src", combine_stats)
        target_potential = EPS_REG * (-math.log(n_target) - (col_highest + jnp.log(col_summed)))
    return (source_potential, target_potential)


def solution(mesh):
    placed = (
        P("src", None),
        P(("tgt", "src"), None),
        P("tgt"),
        P("src", "tgt", None),
        P("src", "tgt"),
    )
    return jax.shard_map(
        per_device, mesh=mesh, in_specs=placed, out_specs=(P("src"), P("tgt")), check_vma=False
    )
```

profile of v0, /device:TPU:32, one launch (start us, length us, event | category | flops | bytes accessed | tf_op | source)
XLA Modules:
  0.0 850.9 jit_solution(7559814771760610560)
XLA Ops:
  7.2 0.7 all-gather.6.cloned.1.call-update
  7.9 1.2 multiply_reduce_fusion.1
  9.1 79.4 %all-gather.6.cloned.1.call-done = bf16[4096,128]{1,0:T(8,128)(2,1)} async-done(((bf16[128,128]{1,0:T(8,128)(2,1)}), bf16[4096,128]{1,0:T(8,128)(2,1)}) %all-gather.6.cloned.1.call-update) | async-done | bytes 1048592 | tf_op jit(solution)/shard_map/all_gather | solution.py:58
  88.5 1.9 multiply_reduce_fusion
  90.5 34.3 %while.110 = (s32[]{:T(128)}, f32[1024]{0:T(1024)S(1)}, s32[]{:T(128)}, s32[16]{0:T(128)S(1)}, f32[4096]{0:T(1024)}, /*index=5*/f32[1024]{0:T(1024)S(1)}, f32[40...) while((s32[]{:T(128)}, f32[1024]{0:T(1024)S(1)}, ...), condition=%wide.region_4.5_spmd, body=%wide.region_2.4_spmd.sunk | while | flops 68681760 | bytes 289298 | solution.py:96
  91.1 0.7 dynamic_slice.413
  94.7 0.8 dynamic_slice.416
  96.7 0.7 dynamic_slice.413
  100.4 0.8 dynamic_slice.416
  102.4 0.7 dynamic_slice.413
  106.0 0.8 dynamic_slice.416
  108.0 0.7 dynamic_slice.413
  111.6 0.8 dynamic_slice.416
  113.6 0.7 dynamic_slice.413
  117.2 0.8 dynamic_slice.416
  119.2 0.7 dynamic_slice.413
  122.8 0.8 dynamic_slice.416
  124.8 66.6 %pmax.14 = f32[1024]{0:T(1024)S(1)} all-reduce(f32[1024]{0:T(1024)S(1)} %get-tuple-element.1032), channel_id=1, replica_groups=mesh['src'=32,'tgt'=8] {'tgt'}, use_global_device_ids=true, to_apply=%region_5.6 | all-reduce | flops 1024 | bytes 8192 | tf_op jit(solution)/shard_map/pmax | solution.py:97
  191.4 35.4 %while.111 = (s32[]{:T(128)}, f32[1024]{0:T(1024)S(1)}, s32[]{:T(128)}, s32[16]{0:T(128)S(1)}, f32[4096]{0:T(1024)}, /*index=5*/f32[1024]{0:T(1024)S(1)}, f32[40...) while((s32[]{:T(128)}, f32[1024]{0:T(1024)S(1)}, ...), condition=%wide.region_8.9_spmd, body=%wide.region_6.8_spmd.sunk | while | flops 68943904 | bytes 295454 | solution.py:106
  192.1 0.7 dynamic_slice.420
  195.8 0.8 dynamic_slice.424
  197.9 0.7 dynamic_slice.420
  201.6 0.8 dynamic_slice.424
  203.7 0.7 dynamic_slice.420
  207.4 0.8 dynamic_slice.424
  209.5 0.7 dynamic_slice.420
  213.1 0.8 dynamic_slice.424
  215.3 0.7 dynamic_slice.420
  218.9 0.8 dynamic_slice.424
  221.1 0.7 dynamic_slice.420
  224.7 0.8 dynamic_slice.424
  226.8 68.2 %psum.14 = f32[1024]{0:T(1024)S(1)} all-reduce(f32[1024]{0:T(1024)S(1)} %get-tuple-element.1033), channel_id=1, replica_groups=mesh['src'=32,'tgt'=8] {'tgt'}, use_global_device_ids=true, to_apply=%region_9.10 | all-reduce | flops 1024 | bytes 8192 | tf_op jit(solution)/shard_map/psum | solution.py:107
  295.1 31.7 %while.112 = (s32[]{:T(128)}, f32[4096]{0:T(1024)S(1)}, f32[4096]{0:T(1024)S(1)}, s32[]{:T(128)}, s32[16]{0:T(128)S(1)}, /*index=5*/f32[1024]{0:T(1024)S(1)}, f3...) while((s32[]{:T(128)}, f32[4096]{0:T(1024)S(1)}, ...), condition=%wide.region_13.14_spmd, body=%wide.region_10.13_spmd.sunk | while | flops 69208096 | bytes 2396698 | solution.py:121
  295.8 0.7 dynamic_slice.429
  301.0 0.7 dynamic_slice.429
  306.1 0.7 dynamic_slice.429
  311.3 0.7 dynamic_slice.429
  316.5 0.7 dynamic_slice.429
  321.7 0.7 dynamic_slice.429
  326.8 100.8 %all-gather = f32[131072]{0:T(1024)S(1)} all-gather(f32[4096]{0:T(1024)S(1)} %get-tuple-element.1034), channel_id=2, replica_groups=mesh['src'=32,'tgt'=8] {'src'}, dimensions={0}, use_global_device_ids=true | all-gather | bytes 540672 | tf_op jit(solution)/shard_map/all_gather | solution.py:18
  427.8 49.3 %all-gather.1 = f32[131072]{0:T(1024)S(1)} all-gather(f32[4096]{0:T(1024)S(1)} %get-tuple-element.1035), channel_id=3, replica_groups=mesh['src'=32,'tgt'=8] {'src'}, dimensions={0}, use_global_device_ids=true | all-gather | bytes 540672 | tf_op jit(solution)/shard_map/all_gather | solution.py:18
  477.2 2.6 while.113
  479.9 30.3 %while.114 = (s32[]{:T(128)}, f32[1024]{0:T(1024)S(1)}, s32[]{:T(128)}, s32[16]{0:T(128)S(1)}, f32[4096]{0:T(1024)S(1)}, /*index=5*/f32[1024]{0:T(1024)S(1)}, f3...) while((s32[]{:T(128)}, f32[1024]{0:T(1024)S(1)}, ...), condition=%wide.region_18.19_spmd, body=%wide.region_16.18_spmd.sunk | while | flops 68681760 | bytes 289298 | solution.py:96
  480.6 0.7 dynamic_slice.437
  485.5 0.7 dynamic_slice.437
  490.4 0.7 dynamic_slice.437
  495.4 0.7 dynamic_slice.437
  500.3 0.7 dynamic_slice.437
  505.2 0.7 dynamic_slice.437
  510.1 56.2 %pmax.15 = f32[1024]{0:T(1024)S(1)} all-reduce(f32[1024]{0:T(1024)S(1)} %get-tuple-element.1038), channel_id=1, replica_groups=mesh['src'=32,'tgt'=8] {'tgt'}, use_global_device_ids=true, to_apply=%region_19.20 | all-reduce | flops 1024 | bytes 8192 | tf_op jit(solution)/shard_map/pmax | solution.py:97
  566.4 31.3 %while.115 = (s32[]{:T(128)}, f32[1024]{0:T(1024)S(1)}, s32[]{:T(128)}, s32[16]{0:T(128)S(1)}, f32[4096]{0:T(1024)S(1)}, /*index=5*/f32[1024]{0:T(1024)S(1)}, f3...) while((s32[]{:T(128)}, f32[1024]{0:T(1024)S(1)}, ...), condition=%wide.region_22.23_spmd, body=%wide.region_20.22_spmd.sunk | while | flops 68943904 | bytes 295454 | solution.py:106
  567.1 0.7 dynamic_slice.444
  572.2 0.7 dynamic_slice.444
  577.3 0.7 dynamic_slice.444
  582.4 0.7 dynamic_slice.444
  587.5 0.7 dynamic_slice.444
  592.6 0.7 dynamic_slice.444
  597.7 61.4 %psum.15 = f32[1024]{0:T(1024)S(1)} all-reduce(f32[1024]{0:T(1024)S(1)} %get-tuple-element.1039), channel_id=1, replica_groups=mesh['src'=32,'tgt'=8] {'tgt'}, use_global_device_ids=true, to_apply=%region_23.24 | all-reduce | flops 1024 | bytes 8192 | tf_op jit(solution)/shard_map/psum | solution.py:107
  659.1 30.2 %while.116 = (s32[]{:T(128)}, f32[4096]{0:T(1024)S(1)}, f32[4096]{0:T(1024)S(1)}, s32[]{:T(128)}, s32[16]{0:T(128)S(1)}, /*index=5*/f32[1024]{0:T(1024)S(1)}, f3...) while((s32[]{:T(128)}, f32[4096]{0:T(1024)S(1)}, ...), condition=%wide.region_27.28_spmd, body=%wide.region_24.27_spmd.sunk | while | flops 69208096 | bytes 2396698 | solution.py:121
  659.8 0.6 dynamic_slice.453
  689.4 102.0 %all-gather.2 = f32[131072]{0:T(1024)S(1)} all-gather(f32[4096]{0:T(1024)S(1)} %get-tuple-element.1040), channel_id=4, replica_groups=mesh['src'=32,'tgt'=8] {'src'}, dimensions={0}, use_global_device_ids=true | all-gather | bytes 540672 | tf_op jit(solution)/shard_map/all_gather | solution.py:18
  791.4 49.2 %all-gather.3 = f32[131072]{0:T(1024)S(1)} all-gather(f32[4096]{0:T(1024)S(1)} %get-tuple-element.1041), channel_id=5, replica_groups=mesh['src'=32,'tgt'=8] {'src'}, dimensions={0}, use_global_device_ids=true | all-gather | bytes 540672 | tf_op jit(solution)/shard_map/all_gather | solution.py:18
  840.8 2.6 while.117
  843.4 0.6 subtract_multiply_fusion
  (349 shorter events, 39.8 us)
Async XLA Ops:
  7.2 83.3 %copy-start.1 = (bf16[1024,128]{1,0:T(8,128)(2,1)S(1)}, bf16[1024,128]{1,0:T(8,128)(2,1)}, u32[]{:S(2)}) copy-start(bf16[1024,128]{1,0:T(8,128)(2,1)} %param.21) | copy-start | bytes 786436
  7.2 83.3 %copy-start.3 = (s32[1,1,16]{2,1,0:T(1,128)S(1)}, s32[1,1,16]{2,1,0:T(1,128)}, u32[]{:S(2)}) copy-start(s32[1,1,16]{2,1,0:T(1,128)} %param.24) | copy-start | bytes 196
  7.2 81.3 %all-gather.6.cloned.1.call-start = ((), (), s32[]{:S(2)}) async-start(), calls=%async_computation | async-start | bytes 1081344 | tf_op jit(solution)/shard_map/all_gather | solution.py:58
  88.5 2.0 copy-start
  689.3 151.3 %copy-start.2 = (f32[1024]{0:T(1024)}, f32[1024]{0:T(1024)S(1)}, u32[]{:S(2)}) copy-start(f32[1024]{0:T(1024)S(1)} %get-tuple-element.2077) | copy-start | bytes 12292
Sparse Core Ops, SparseCore 0:
  10.6 77.8 all-gather.5
where the time goes:
time: 857 us; the launch traced here: 851 us
  blocking collectives  554 us (65%)
  loops' own time  130 us (15%)
  waiting for transfers between devices  80.1 us (9%)
  local copies, waits for them, and re-layouts  43.1 us (5%)
  matrix products  15.3 us (2%)
  other arithmetic  14.7 us (2%)
  between operations  14.2 us (2%)
    all_gather x4, blocking collectives, joined(): everything = jax.tree.map(lambda part: lax.all_gather(part, axis), array)  301 us
    psum x2, blocking collectives, per_device(): summed = lax.psum(local_sum, 'tgt')  130 us
    pmax x2, blocking collectives, per_device(): highest = lax.pmax(local_max, 'tgt')  123 us
    all_gather x1, waiting for transfers between devices, per_device(): targets = lax.all_gather(target_points, 'src', axis=0, tiled=True)  79.4 us
    another operation x2, loops' own time, per_device(): lax.fori_loop(0, total, max_pass, jnp.full((src_rows,), NEG_START, jnp.fl...  42.9 us
    another operation x2, loops' own time, per_device(): lax.fori_loop(0, total, sum_pass, jnp.zeros((src_rows,), jnp.float32))  42.8 us
    another operation x2, loops' own time, per_device(): local_stats = lax.fori_loop(0, total, online_pass, col_empty)  41.9 us
    dynamic_slice x36, local copies, waits for them, and re-layouts, starts(): local_pair = pairs[number]  23.5 us
  transfers between devices with their start and end apart: 1, of which 1 were waited for; matrix products, arithmetic and copies ran while one was open for 0% of the time, Pallas kernels for 0%

commit v1 on v0

v1 whole, which is shorter than its diff:
```python
import functools
import math

import jax
import jax.numpy as jnp
from jax import lax
from jax.experimental import pallas as pl
from jax.experimental.pallas import tpu as pltpu
from jax.sharding import Mesh
from jax.sharding import PartitionSpec as P

BLOCK = 512
LANES = 128
EMB = 128
SB_DEV = 2
TB_DEV = 8
ITERS = 2
NEG_START = -1e30
EPS_REG = 0.2
LOG2E = math.log2(math.e)
SCALE = 2.0 * LOG2E / EPS_REG
GROUPS = BLOCK // LANES

bf16 = jnp.bfloat16
f32 = jnp.float32


def squares(points):
    values = points.astype(f32)
    sq = values * values
    high = sq.astype(bf16)
    low = (sq - high.astype(f32)).astype(bf16)
    parts = jnp.concatenate([high, low], axis=1)
    ones = jnp.ones((8, 2 * EMB), bf16)
    sums = lax.dot_general(ones, parts, (((1,), (1,)), ((), ())), preferred_element_type=f32)
    count = points.shape[0] // LANES
    return jnp.concatenate([sums[0:1, r * LANES:(r + 1) * LANES] for r in range(count)], axis=0)


def bias_columns(bias):
    high = bias.astype(bf16).astype(f32)
    rest = bias - high
    middle = rest.astype(bf16).astype(f32)
    low = rest - middle
    count = bias.shape[0]
    stacked = jnp.concatenate([high, middle, low, jnp.zeros((LANES - 3 * count, LANES), f32)], axis=0)
    return stacked.T.astype(bf16)


def combined(parts):
    highest = jnp.max(parts, axis=0)
    total = jnp.sum(jnp.exp2(parts - highest[None]), axis=0)
    return highest + jnp.log(total) * LOG2E


def half_bias(lse):
    return (-0.5 * EPS_REG / LOG2E) * (math.log2(32768) + lse)


def sweep(pairs_ref, count_ref, kept_ref, sum_ref, kept_bias, kept_count, acc_max, acc_sum, kept_first, out_ref):
    acc_max[...] = jnp.full(acc_max.shape, NEG_START, f32)
    acc_sum[...] = jnp.zeros(acc_sum.shape, f32)
    lane = lax.broadcasted_iota(jnp.int32, (LANES, LANES), 1) % kept_count
    ones = jnp.ones((BLOCK, LANES), bf16)

    def turn(number, carry):
        pair = pairs_ref[0, 0, number]
        first, second = pair // TB_DEV, pair % TB_DEV
        along, place = (first, second) if kept_first else (second, first)
        lhs = kept_ref[pl.ds(pl.multiple_of(along * BLOCK, BLOCK), BLOCK), :]
        bias = [jnp.where(lane == along * GROUPS + q, kept_bias, jnp.zeros_like(kept_bias)) for q in range(GROUPS)]
        lhs = jnp.concatenate([lhs, jnp.concatenate(bias, axis=0)], axis=1)
        rhs = sum_ref[pl.ds(pl.multiple_of(place * BLOCK, BLOCK), BLOCK), :]
        rhs = jnp.concatenate([rhs, ones], axis=1)
        scores = lax.dot_general(lhs, rhs, (((1,), (1,)), ((), ())), preferred_element_type=f32)
        old_max = acc_max[pl.ds(place, 1), :]
        highest = jnp.maximum(old_max, jnp.max(scores, axis=0, keepdims=True))
        block_sum = jnp.sum(jnp.exp2((scores - highest) * SCALE), axis=0, keepdims=True)
        acc_sum[pl.ds(place, 1), :] = acc_sum[pl.ds(place, 1), :] * jnp.exp2((old_max - highest) * SCALE) + block_sum
        acc_max[pl.ds(place, 1), :] = highest
        return carry

    lax.fori_loop(0, count_ref[0, 0], turn, 0)
    blocks = sum_ref.shape[0] // BLOCK
    total = acc_sum[...]
    lse = jnp.where(total > 0, acc_max[...] * SCALE + jnp.log(total) * LOG2E, NEG_START)
    dense = jnp.concatenate(
        [lse[b:b + 1, q * LANES:(q + 1) * LANES] for b in range(blocks) for q in range(GROUPS)], axis=0
    )
    for k in range(out_ref.shape[0]):
        out_ref[k] = dense


def first_rows(pairs_ref, count_ref, sources_ref, targets_ref, potential_ref, out_ref, acc_max, acc_sum):
    bias = 0.5 * (potential_ref[...] - squares(targets_ref[...]))
    sweep(pairs_ref, count_ref, targets_ref, sources_ref, bias_columns(bias), bias.shape[0], acc_max, acc_sum, False, out_ref)


def next_rows(pairs_ref, count_ref, sources_ref, targets_ref, parts_ref, out_ref, acc_max, acc_sum):
    bias = half_bias(combined(parts_ref[...]))
    sweep(pairs_ref, count_ref, targets_ref, sources_ref, bias_columns(bias), bias.shape[0], acc_max, acc_sum, False, out_ref)


def columns(pairs_ref, count_ref, sources_ref, targets_ref, parts_ref, out_ref, potential_ref, acc_max, acc_sum):
    bias = half_bias(combined(parts_ref[...]))
    potential_ref[...] = squares(sources_ref[...]) + 2.0 * bias
    sweep(pairs_ref, count_ref, sources_ref, targets_ref, bias_columns(bias), bias.shape[0], acc_max, acc_sum, True, out_ref)


def last_potential(targets_ref, parts_ref, potential_ref):
    potential_ref[...] = squares(targets_ref[...]) + 2.0 * half_bias(combined(parts_ref[...]))


SMEM = pl.BlockSpec(memory_space=pltpu.SMEM)
VMEM = pl.BlockSpec(memory_space=pltpu.VMEM)
PARAMS = pltpu.CompilerParams(vmem_limit_bytes=40 * 1024 * 1024)
STATS = [pltpu.VMEM((8, BLOCK), f32)] * 2


def spread(parts, axes):
    return lax.all_to_all(parts, axes, 0, 0, tiled=True)


def per_device(source_points, target_points, initial_potential, pair_list, pair_count):
    n_src = lax.axis_size(("y", "z"))
    n_tgt = lax.axis_size(("x", "c"))
    own = target_points.shape[0]
    targets = spread(jnp.broadcast_to(target_points[None], (n_src, own, EMB)), ("y", "z"))
    targets = targets.reshape(n_src * own, EMB)
    src_rows = source_points.shape[0] // LANES
    tgt_rows = targets.shape[0] // LANES

    def rows(kernel, operand):
        return pl.pallas_call(
            kernel,
            out_shape=jax.ShapeDtypeStruct((n_tgt, src_rows, LANES), f32),
            in_specs=[SMEM, SMEM, VMEM, VMEM, VMEM],
            out_specs=VMEM,
            scratch_shapes=STATS,
            compiler_params=PARAMS,
        )(pair_list, pair_count, source_points, targets, operand)

    col_parts = None
    for iteration in range(ITERS):
        if iteration == 0:
            row_parts = rows(first_rows, initial_potential.reshape(tgt_rows, LANES))
        else:
            row_parts = rows(next_rows, col_parts)
        row_parts = spread(row_parts, ("x", "c"))
        col_parts, source_potential = pl.pallas_call(
            columns,
            out_shape=[
                jax.ShapeDtypeStruct((n_src, tgt_rows, LANES), f32),
                jax.ShapeDtypeStruct((src_rows, LANES), f32),
            ],
            in_specs=[SMEM, SMEM, VMEM, VMEM, VMEM],
            out_specs=[VMEM, VMEM],
            scratch_shapes=STATS,
            compiler_params=PARAMS,
        )(pair_list, pair_count, source_points, targets, row_parts)
        col_parts = spread(col_parts, ("y", "z"))
    target_potential = pl.pallas_call(
        last_potential,
        out_shape=jax.ShapeDtypeStruct((tgt_rows, LANES), f32),
        in_specs=[VMEM, VMEM],
        out_specs=VMEM,
        compiler_params=PARAMS,
    )(targets, col_parts)
    return source_potential.reshape(-1), target_potential.reshape(-1)


def solution(mesh):
    fine = Mesh(mesh.devices.reshape(4, 8, 4, 2), ("y", "z", "x", "c"))
    src, tgt = ("y", "z"), ("x", "c")
    placed = (P(src, None), P(tgt + src, None), P(tgt), P(src, tgt, None), P(src, tgt))
    return jax.shard_map(
        per_device, mesh=fine, in_specs=placed, out_specs=(P(src), P(tgt)), check_vma=False
    )
```

time: 857 us -> 142 us (0.17)
  blocking collectives: 554 us -> 80.5 us
  loops' own time: 130 us -> 0 us
  waiting for transfers between devices: 80.1 us -> 27.9 us
  local copies, waits for them, and re-layouts: 43.1 us -> 2.62 us
  Pallas kernels: 0 us -> 18.5 us
  matrix products: 15.3 us -> 0 us
  other arithmetic: 14.7 us -> 0 us
  between operations: 14.2 us -> 1.31 us
  starting transfers between devices: 0.04 us -> 11.5 us
    all_gather x4 -> x0, blocking collectives: 301 us -> none  [joined(): everything = jax.tree.map(lambda part: lax.all_gather(part, axis), array)]
    psum x2 -> x0, blocking collectives: 130 us -> none  [per_device(): summed = lax.psum(local_sum, 'tgt')]
    another operation x8 -> x0, loops' own time: 130 us -> none  [the longest x2 42.9 us: per_device(): lax.fori_loop(0, total, max_pass, jnp.full((src_rows,), NEG_START, jnp.fl...]
    pmax x2 -> x0, blocking collectives: 123 us -> none  [per_device(): highest = lax.pmax(local_max, 'tgt')]
    all_to_all x0 -> x4, blocking collectives: none -> 80.5 us  [spread(): return lax.all_to_all(parts, axes, 0, 0, tiled=True)]
    all_gather x1 -> x0, waiting for transfers between devices: 79.4 us -> none  [per_device(): targets = lax.all_gather(target_points, 'src', axis=0, tiled=True)]
    dynamic_slice x218 -> x0, local copies, waits for them, and re-layouts: 42.7 us -> none  [the longest x36 23.5 us: starts(): local_pair = pairs[number]]
    all_to_all x0 -> x1, waiting for transfers between devices: none -> 27.9 us  [spread(): return lax.all_to_all(parts, axes, 0, 0, tiled=True)]
where the time goes in v1:
time: 142 us
  blocking collectives  80.5 us (57%)
  waiting for transfers between devices  27.9 us (20%)
  Pallas kernels  18.5 us (13%)
  starting transfers between devices  11.5 us (8%)
  local copies, waits for them, and re-layouts  2.62 us (2%)
    all_to_all x4, blocking collectives, spread(): return lax.all_to_all(parts, axes, 0, 0, tiled=True)  80.5 us
    all_to_all x1, waiting for transfers between devices, spread(): return lax.all_to_all(parts, axes, 0, 0, tiled=True)  27.9 us
    all_to_all x1, starting transfers between devices, spread(): return lax.all_to_all(parts, axes, 0, 0, tiled=True)  11.5 us
    pallas_call x2, Pallas kernels, per_device(): pl.pallas_call(columns, out_shape=[jax.ShapeDtypeStruct((n_src, tgt_rows,...  8.96 us
    pallas_call x2, Pallas kernels, rows(): pl.pallas_call(kernel, out_shape=jax.ShapeDtypeStruct((n_tgt, src_rows, L...  8.31 us
  transfers between devices with their start and end apart: 1, of which 1 were waited for; matrix products, arithmetic and copies ran while one was open for 0% of the time, Pallas kernels for 0%

profile of v1, /device:TPU:32, one launch (start us, length us, event | category | flops | bytes accessed | tf_op | source)
XLA Modules:
  0.0 142.3 jit_solution(10284687960276568422)
XLA Ops:
  0.6 2.0 %broadcast_in_dim.2 = bf16[32,128,128]{2,1,0:T(8,128)(2,1)} broadcast(bf16[128,128]{1,0:T(8,128)(2,1)} %param.6), dimensions={1,2} | broadcast | bytes 1081344 | tf_op jit(solution)/shard_map/broadcast_in_dim | solution.py:128
  2.6 0.0 copy-start
  2.6 0.0 copy-start.1
  2.6 11.5 %all-to-all-start = ((bf16[32,128,128]{2,1,0:T(8,128)(2,1)}), bf16[32,128,128]{2,1,0:T(8,128)(2,1)S(1)}, u32[]{:S(2)}, u32[]{:S(2)}) async-start(bf16[32,128,128]{2,1,0:T(8,128)(2,1)} %broadcast_in_dim.2), calls=%async_computation | async-start | bytes 2097152 | tf_op jit(solution)/shard_map/all_to_all | solution.py:121
  14.7 27.9 %all-to-all-done = bf16[32,128,128]{2,1,0:T(8,128)(2,1)S(1)} async-done(((bf16[32,128,128]{2,1,0:T(8,128)(2,1)}), bf16[32,128,128]{2,1,0:T(8,128)(2,1)S(1)}, u32[]{:S(2)}, u32[]{:S(2)}) %all-to-all-start) | async-done | bytes 1048608 | tf_op jit(solution)/shard_map/all_to_all | solution.py:121
  42.6 0.0 copy-start.2
  42.6 0.0 copy-done
  42.6 0.0 copy-done.1
  42.6 0.6 copy-done.2
  43.3 4.4 %shard_map.68 = f32[8,8,128]{2,1,0:T(8,128)S(1)} custom-call(s32[1,1,16]{2,1,0:T(1,128)S(1)} %copy-done.2, s32[1,1]{1,0:T(1,128)S(6)} %copy.7.count_ref, bf16[1024,128]{1,0:T(8,128)(2,1)S(1)} %copy-done, bf16[4096,128]{1,0:T(8,128)(2,1)S(1)} %bitcast.4, f32[32,128]{1,0:T(8,128)S(1)} %bitcast.9), custom_call_target="tpu_custom_call" | custom-call | tf_op jit(solution)/shard_map/pallas_call | solution.py:134
  47.7 14.7 %all_to_all.25.parts_ref = f32[8,8,128]{2,1,0:T(8,128)S(1)} all-to-all(f32[8,8,128]{2,1,0:T(8,128)S(1)} %shard_map.68), channel_id=1, replica_groups=mesh['y'=4,'z'=8,'x'=4,'c'=2] {'x','c'}, dimensions={0} | all-to-all | bytes 65536 | tf_op jit(solution)/shard_map/all_to_all | solution.py:121
  62.4 4.5 %shard_map.69 = (f32[32,32,128]{2,1,0:T(8,128)S(1)}, f32[8,128]{1,0:T(8,128)}) custom-call(s32[1,1,16]{2,1,0:T(1,128)S(1)} %copy-done.2, s32[1,1]{1,0:T(1,128)S(6)} %copy.7.count_ref, bf16[1024,128]{1,0:T(8,128)(2,1)S(1)} %copy-done, bf16[4096,128]{1,0:T(8,128)(2,1)S(1)} %bitcast.5, f32[8,8,128]{2,1,0:T(8,128)S(1)} %all_to_all.25.parts_ref), custom_call_target="tpu_custom_call" | custom-call | tf_op jit(solution)/shard_map/pallas_call | solution.py:150
  66.9 26.1 %all_to_all.26.parts_ref = f32[32,32,128]{2,1,0:T(8,128)S(1)} all-to-all(f32[32,32,128]{2,1,0:T(8,128)S(1)} %get-tuple-element.5), channel_id=1, replica_groups=mesh['y'=4,'z'=8,'x'=4,'c'=2] {'y','z'}, dimensions={0} | all-to-all | bytes 1048576 | tf_op jit(solution)/shard_map/all_to_all | solution.py:121
  93.0 3.9 %shard_map.70 = f32[8,8,128]{2,1,0:T(8,128)S(1)} custom-call(s32[1,1,16]{2,1,0:T(1,128)S(1)} %copy-done.2, s32[1,1]{1,0:T(1,128)S(6)} %copy.7.count_ref, bf16[1024,128]{1,0:T(8,128)(2,1)S(1)} %copy-done, bf16[4096,128]{1,0:T(8,128)(2,1)S(1)} %bitcast.6, f32[32,32,128]{2,1,0:T(8,128)S(1)} %all_to_all.26.parts_ref), custom_call_target="tpu_custom_call" | custom-call | tf_op jit(solution)/shard_map/pallas_call | solution.py:134
  96.9 13.2 %all_to_all.27.parts_ref = f32[8,8,128]{2,1,0:T(8,128)S(1)} all-to-all(f32[8,8,128]{2,1,0:T(8,128)S(1)} %shard_map.70), channel_id=1, replica_groups=mesh['y'=4,'z'=8,'x'=4,'c'=2] {'x','c'}, dimensions={0} | all-to-all | bytes 65536 | tf_op jit(solution)/shard_map/all_to_all | solution.py:121
  110.1 4.5 %shard_map.71 = (f32[32,32,128]{2,1,0:T(8,128)S(1)}, f32[8,128]{1,0:T(8,128)}) custom-call(s32[1,1,16]{2,1,0:T(1,128)S(1)} %copy-done.2, s32[1,1]{1,0:T(1,128)S(6)} %copy.7.count_ref, bf16[1024,128]{1,0:T(8,128)(2,1)S(1)} %copy-done, bf16[4096,128]{1,0:T(8,128)(2,1)S(1)} %bitcast.7, f32[8,8,128]{2,1,0:T(8,128)S(1)} %all_to_all.27.parts_ref), custom_call_target="tpu_custom_call" | custom-call | tf_op jit(solution)/shard_map/pallas_call | solution.py:150
  114.6 26.4 %all_to_all.28.parts_ref = f32[32,32,128]{2,1,0:T(8,128)S(1)} all-to-all(f32[32,32,128]{2,1,0:T(8,128)S(1)} %get-tuple-element.7), channel_id=1, replica_groups=mesh['y'=4,'z'=8,'x'=4,'c'=2] {'y','z'}, dimensions={0} | all-to-all | bytes 1048576 | tf_op jit(solution)/shard_map/all_to_all | solution.py:121
  141.1 1.3 shard_map.72
Async XLA Ops:
  2.6 40.0 %copy-start = (bf16[1024,128]{1,0:T(8,128)(2,1)S(1)}, bf16[1024,128]{1,0:T(8,128)(2,1)}, u32[]{:S(2)}) copy-start(bf16[1024,128]{1,0:T(8,128)(2,1)} %sources_ref.7) | copy-start | bytes 786436
  2.6 40.0 %copy-start.1 = (f32[4096]{0:T(1024)S(1)}, f32[4096]{0:T(1024)}, u32[]{:S(2)}) copy-start(f32[4096]{0:T(1024)} %param.7) | copy-start | bytes 49156
  2.6 40.0 %all-to-all-start = ((bf16[32,128,128]{2,1,0:T(8,128)(2,1)}), bf16[32,128,128]{2,1,0:T(8,128)(2,1)S(1)}, u32[]{:S(2)}, u32[]{:S(2)}) async-start(bf16[32,128,128]{2,1,0:T(8,128)(2,1)} %broadcast_in_dim.2), calls=%async_computation | async-start | bytes 2097152 | tf_op jit(solution)/shard_map/all_to_all | solution.py:121
  42.6 0.7 copy-start.2

commit v2 on v1

v2 whole, which is shorter than its diff:
```python
import functools
import math

import jax
import jax.numpy as jnp
from jax import lax
from jax.experimental import pallas as pl
from jax.experimental.pallas import tpu as pltpu
from jax.sharding import Mesh
from jax.sharding import PartitionSpec as P

BLOCK = 512
LANES = 128
EMB = 128
SB_DEV = 2
TB_DEV = 8
PAIRS_MAX = 16
ITERS = 2
NEG_START = -1e30
EPS_REG = 0.2
LOG2E = math.log2(math.e)
SCALE = 2.0 * LOG2E / EPS_REG
GROUPS = BLOCK // LANES

bf16 = jnp.bfloat16
f32 = jnp.float32


def squares(points):
    values = points.astype(f32)
    sq = values * values
    high = sq.astype(bf16)
    low = (sq - high.astype(f32)).astype(bf16)
    parts = jnp.concatenate([high, low], axis=1)
    ones = jnp.ones((8, 2 * EMB), bf16)
    sums = lax.dot_general(ones, parts, (((1,), (1,)), ((), ())), preferred_element_type=f32)
    count = points.shape[0] // LANES
    return jnp.concatenate([sums[0:1, r * LANES:(r + 1) * LANES] for r in range(count)], axis=0)


def bias_columns(bias):
    high = bias.astype(bf16).astype(f32)
    rest = bias - high
    middle = rest.astype(bf16).astype(f32)
    low = rest - middle
    count = bias.shape[0]
    stacked = jnp.concatenate([high, middle, low, jnp.zeros((LANES - 3 * count, LANES), f32)], axis=0)
    return stacked.T.astype(bf16)


def combined(parts):
    highest = jnp.max(parts, axis=0)
    total = jnp.sum(jnp.exp2(parts - highest[None]), axis=0)
    return highest + jnp.log(total) * LOG2E


def half_bias(lse):
    return (-0.5 * EPS_REG / LOG2E) * (math.log2(32768) + lse)


def clear(acc_max, acc_sum):
    acc_max[...] = jnp.full(acc_max.shape, NEG_START, f32)
    acc_sum[...] = jnp.zeros(acc_sum.shape, f32)


def sweep(pairs_ref, count, kept_ref, sum_ref, bias, acc_max, acc_sum, even, odd, kept_first, offset=0):
    kept_count = bias.shape[0]
    kept_bias = bias_columns(bias)
    lane = lax.broadcasted_iota(jnp.int32, (LANES, LANES), 1) & (kept_count - 1)
    ones = jnp.ones((BLOCK, LANES), bf16)
    total_pairs = count

    def where(number):
        pair = jnp.where(number < total_pairs, pairs_ref[jnp.minimum(number, PAIRS_MAX - 1)], 0)
        first, second = pair >> 3, pair & 7
        return (first, second) if kept_first else (jnp.where(number < total_pairs, second - offset, 0), first)

    def score(number, scores_ref):
        along, place = where(number)
        lhs = kept_ref[pl.ds(pl.multiple_of(along * BLOCK, BLOCK), BLOCK), :]
        bias = [jnp.where(lane == along * GROUPS + q, kept_bias, jnp.zeros_like(kept_bias)) for q in range(GROUPS)]
        lhs = jnp.concatenate([lhs, jnp.concatenate(bias, axis=0)], axis=1)
        rhs = sum_ref[pl.ds(pl.multiple_of(place * BLOCK, BLOCK), BLOCK), :]
        rhs = jnp.concatenate([rhs, ones], axis=1)
        scores = lax.dot_general(lhs, rhs, (((1,), (1,)), ((), ())), preferred_element_type=f32)
        scores_ref[...] = scores
        peak = scores_ref[0:8, :]
        for r in range(8, BLOCK, 8):
            peak = jnp.maximum(peak, scores_ref[r:r + 8, :])
        return jnp.where(number < total_pairs, jnp.max(peak, axis=0, keepdims=True), NEG_START)

    def fold(number, scores_ref, block_max):
        along, place = where(number)
        old_max = acc_max[pl.ds(place, 1), :]
        highest = jnp.maximum(old_max, block_max)
        shift = jnp.broadcast_to(highest, (8, BLOCK))
        partial = jnp.zeros((8, BLOCK), f32)
        for r in range(0, BLOCK, 8):
            partial = partial + jnp.exp2((scores_ref[r:r + 8, :] - shift) * SCALE)
        block_sum = jnp.sum(partial, axis=0, keepdims=True)
        block_sum = jnp.where(number < total_pairs, block_sum, 0.0)
        acc_sum[pl.ds(place, 1), :] = acc_sum[pl.ds(place, 1), :] * jnp.exp2((old_max - highest) * SCALE) + block_sum
        acc_max[pl.ds(place, 1), :] = highest

    def turn(k, even_max):
        odd_max = score(2 * k + 1, odd)
        fold(2 * k, even, even_max)
        even_max = score(2 * k + 2, even)
        fold(2 * k + 1, odd, odd_max)
        return even_max

    lax.fori_loop(0, (total_pairs + 1) >> 1, turn, score(0, even))


def finish(blocks, acc_max, acc_sum, out_ref):
    total = acc_sum[...]
    lse = jnp.where(total > 0, acc_max[...] * SCALE + jnp.log(total) * LOG2E, NEG_START)
    dense = jnp.concatenate(
        [lse[b:b + 1, q * LANES:(q + 1) * LANES] for b in range(blocks) for q in range(GROUPS)], axis=0
    )
    for k in range(out_ref.shape[0]):
        out_ref[k] = dense


def piece_rows(by, first, last, y_ref, pairs_ref, count_ref, sources_ref, piece_ref, potential_ref, *refs):
    if first:
        in_max = in_sum = None
    else:
        in_max, in_sum, *refs = refs
    if last:
        out_ref, acc_max, acc_sum, even, odd, chosen = refs
    else:
        acc_max, acc_sum, even, odd, chosen = refs
    if first:
        clear(acc_max, acc_sum)
    else:
        acc_max[...] = in_max[...]
        acc_sum[...] = in_sum[...]
    block0 = ((y_ref[0, 0] + 4 - by) & 3) * 2
    count = count_ref[0, 0]

    def pick(number, found):
        pair = pairs_ref[0, 0, number]
        chosen[found] = pair
        return found + jnp.where((pair & 6) == block0, 1, 0)

    found = lax.fori_loop(0, count, pick, 0)
    potential = potential_ref[pl.ds(pl.multiple_of(block0 * GROUPS, 8), 8), :]
    bias = 0.5 * (potential - squares(piece_ref[...]))
    sweep(chosen, found, piece_ref, sources_ref, bias, acc_max, acc_sum, even, odd, False, block0)
    if last:
        finish(SB_DEV, acc_max, acc_sum, out_ref)


def copied(pairs_ref, chosen):
    def one(number, carry):
        chosen[number] = pairs_ref[0, 0, number]
        return carry

    lax.fori_loop(0, PAIRS_MAX, one, 0)


def next_rows(pairs_ref, count_ref, sources_ref, targets_ref, parts_ref, out_ref, acc_max, acc_sum, even, odd, chosen):
    bias = half_bias(combined(parts_ref[...]))
    copied(pairs_ref, chosen)
    clear(acc_max, acc_sum)
    sweep(chosen, count_ref[0, 0], targets_ref, sources_ref, bias, acc_max, acc_sum, even, odd, False)
    finish(SB_DEV, acc_max, acc_sum, out_ref)


def first_columns(y_ref, pairs_ref, count_ref, sources_ref, own_ref, by1_ref, by2_ref, by3_ref, parts_ref, out_ref, targets_ref, *scratch):
    rows = own_ref.shape[0]
    for k, ref in enumerate((own_ref, by1_ref, by2_ref, by3_ref)):
        place = (y_ref[0, 0] + 4 - k) & 3
        targets_ref[pl.ds(pl.multiple_of(place * rows, rows), rows), :] = ref[...]
    half_columns(pairs_ref, count_ref, sources_ref, targets_ref, parts_ref, out_ref, *scratch)


def half_columns(pairs_ref, count_ref, sources_ref, targets_ref, parts_ref, out_ref, acc_max, acc_sum, even, odd, chosen):
    bias = half_bias(combined(parts_ref[...]))
    copied(pairs_ref, chosen)
    clear(acc_max, acc_sum)
    sweep(chosen, count_ref[0, 0], sources_ref, targets_ref, bias, acc_max, acc_sum, even, odd, True)
    finish(TB_DEV, acc_max, acc_sum, out_ref)
    return bias


def last_columns(pairs_ref, count_ref, sources_ref, targets_ref, parts_ref, out_ref, potential_ref, *scratch):
    bias = half_columns(pairs_ref, count_ref, sources_ref, targets_ref, parts_ref, out_ref, *scratch)
    potential_ref[...] = squares(sources_ref[...]) + 2.0 * bias


def last_potential(targets_ref, parts_ref, potential_ref):
    potential_ref[...] = squares(targets_ref[...]) + 2.0 * half_bias(combined(parts_ref[...]))


SMEM = pl.BlockSpec(memory_space=pltpu.SMEM)
VMEM = pl.BlockSpec(memory_space=pltpu.VMEM)
PARAMS = pltpu.CompilerParams(vmem_limit_bytes=24 * 1024 * 1024)
STATS = [pltpu.VMEM((8, BLOCK), f32)] * 2
WORK = [pltpu.VMEM((BLOCK, BLOCK), f32)] * 2 + [pltpu.SMEM((PAIRS_MAX,), jnp.int32)]


def spread(parts, axes):
    return lax.all_to_all(parts, axes, 0, 0, tiled=True)


def call(kernel, out_shape, smem, vmem, scratch):
    return pl.pallas_call(
        kernel,
        out_shape=out_shape,
        in_specs=[SMEM] * len(smem) + [VMEM] * len(vmem),
        out_specs=jax.tree.map(lambda _: VMEM, out_shape),
        scratch_shapes=scratch,
        compiler_params=PARAMS,
        cost_estimate=pl.CostEstimate(flops=1 << 30, bytes_accessed=1 << 22, transcendentals=1 << 20),
    )(*smem, *vmem)


def per_device(source_points, target_points, initial_potential, pair_list, pair_count):
    n_src = lax.axis_size(("y", "z"))
    n_tgt = lax.axis_size(("x", "c"))
    n_y, n_z = lax.axis_size("y"), lax.axis_size("z")
    own = target_points.shape[0]
    src_rows = source_points.shape[0] // LANES
    tgt_rows = own * n_src // LANES
    y = lax.axis_index("y").astype(jnp.int32).reshape(1, 1)

    piece = spread(jnp.broadcast_to(target_points[None], (n_z, own, EMB)), "z").reshape(n_z * own, EMB)
    shifted = [
        lax.ppermute(piece, "y", [(i, (i + k) % n_y) for i in range(n_y)]) for k in range(1, n_y)
    ]
    pieces = [piece] + shifted
    potential = initial_potential.reshape(tgt_rows, LANES)
    row_shape = jax.ShapeDtypeStruct((n_tgt, src_rows, LANES), f32)
    col_shape = jax.ShapeDtypeStruct((n_src, tgt_rows, LANES), f32)
    stat = jax.ShapeDtypeStruct((8, BLOCK), f32)
    stats = ()
    order = (0, 1, 3, 2)
    for k in order:
        first, last = k == order[0], k == order[-1]
        got = call(
            functools.partial(piece_rows, k, first, last),
            row_shape if last else [stat, stat],
            (y, pair_list, pair_count),
            (source_points, pieces[k], potential, *stats),
            STATS + WORK if last else WORK,
        )
        stats = got
    row_parts = spread(got, ("x", "c"))
    col_parts, targets = call(
        first_columns,
        [col_shape, jax.ShapeDtypeStruct((tgt_rows * LANES, EMB), bf16)],
        (y, pair_list, pair_count),
        (source_points, *pieces, row_parts),
        STATS + WORK,
    )
    for iteration in range(1, ITERS):
        col_parts = spread(col_parts, ("y", "z"))
        row_parts = call(
            next_rows, row_shape, (pair_list, pair_count), (source_points, targets, col_parts), STATS + WORK
        )
        row_parts = spread(row_parts, ("x", "c"))
        last = iteration == ITERS - 1
        out_shape = [col_shape, jax.ShapeDtypeStruct((src_rows, LANES), f32)]
        got = call(
            last_columns if last else half_columns,
            out_shape if last else col_shape,
            (pair_list, pair_count),
            (source_points, targets, row_parts),
            STATS + WORK,
        )
        col_parts = got[0] if last else got
    source_potential = got[1]
    col_parts = spread(col_parts, ("y", "z"))
    target_potential = call(
        last_potential, jax.ShapeDtypeStruct((tgt_rows, LANES), f32), (), (targets, col_parts), []
    )
    return source_potential.reshape(-1), target_potential.reshape(-1)


def solution(mesh):
    fine = Mesh(mesh.devices.reshape(4, 8, 4, 2), ("y", "z", "x", "c"))
    src, tgt = ("y", "z"), ("x", "c")
    placed = (P(src, None), P(tgt + src, None), P(tgt), P(src, tgt, None), P(src, tgt))
    return jax.shard_map(
        per_device, mesh=fine, in_specs=placed, out_specs=(P(src), P(tgt)), check_vma=False
    )
```

time: 142 us -> 123 us (0.87)
  waiting for transfers between devices: 27.9 us -> 1.9 us
  blocking collectives: 80.5 us -> 96.6 us
  starting transfers between devices: 11.5 us -> 5.31 us
  Pallas kernels: 18.5 us -> 16.4 us
    all_to_all x1 -> x0, waiting for transfers between devices: 27.9 us -> none  [spread(): return lax.all_to_all(parts, axes, 0, 0, tiled=True)]
    all_to_all x4 -> x5, blocking collectives: 80.5 us -> 96.6 us  [spread(): return lax.all_to_all(parts, axes, 0, 0, tiled=True)]
    all_to_all x1 -> x0, starting transfers between devices: 11.5 us -> none  [spread(): return lax.all_to_all(parts, axes, 0, 0, tiled=True)]
    ppermute x0 -> x3, starting transfers between devices: none -> 5.31 us  [per_device(): lax.ppermute(piece, 'y', [(i, (i + k) % n_y) for i in range(n_y)])]
    pallas_call x5 -> x8, Pallas kernels: 18.5 us -> 16.4 us  [call(): pl.pallas_call(kernel, out_shape=out_shape, in_specs=[SMEM] * len(smem) +...]
    ppermute x0 -> x3, waiting for transfers between devices: none -> 1.9 us  [per_device(): lax.ppermute(piece, 'y', [(i, (i + k) % n_y) for i in range(n_y)])]
  transfers between devices with their start and end apart: 1 -> 3, of which waited for: 1 -> 1; matrix products, arithmetic and copies ran while one was open for 0% -> 0% of each run, Pallas kernels for 0% -> 5%
where the time goes in v2:
time: 123 us
  blocking collectives  96.6 us (79%)
  Pallas kernels  16.4 us (13%)
  starting transfers between devices  5.31 us (4%)
  waiting for transfers between devices  1.9 us (2%)
  local copies, waits for them, and re-layouts  1.46 us (1%)
  between operations  1.35 us (1%)
    all_to_all x5, blocking collectives, spread(): return lax.all_to_all(parts, axes, 0, 0, tiled=True)  96.6 us
    pallas_call x8, Pallas kernels, call(): pl.pallas_call(kernel, out_shape=out_shape, in_specs=[SMEM] * len(smem) +...  16.4 us
    ppermute x3, starting transfers between devices, per_device(): lax.ppermute(piece, 'y', [(i, (i + k) % n_y) for i in range(n_y)])  5.31 us
  transfers between devices with their start and end apart: 3, of which 1 were waited for; matrix products, arithmetic and copies ran while one was open for 0% of the time, Pallas kernels for 5%

profile of v2, /device:TPU:32, one launch (start us, length us, event | category | flops | bytes accessed | tf_op | source)
XLA Modules:
  0.0 123.0 jit_solution(17251763187396054407)
XLA Ops:
  0.6 0.8 broadcast_in_dim.2
  1.4 0.0 copy-start
  1.4 0.0 copy-start.1
  1.4 18.9 %all_to_all.25 = bf16[8,128,128]{2,1,0:T(8,128)(2,1)S(1)} all-to-all(bf16[8,128,128]{2,1,0:T(8,128)(2,1)S(1)} %broadcast_in_dim.2), channel_id=1, replica_groups=mesh['y'=4,'z'=8,'x'=4,'c'=2] {'z'}, dimensions={0} | all-to-all | bytes 524288 | tf_op jit(solution)/shard_map/all_to_all | solution.py:205
  20.4 1.6 %collective-permute-start = (bf16[1024,128]{1,0:T(8,128)(2,1)S(1)}, bf16[1024,128]{1,0:T(8,128)(2,1)S(1)}, u32[]{:S(2)}, u32[]{:S(2)}) collective-permute-start(bf16[1024,128]{1,0:T(8,128)(2,1)S(1)} %bitcast.5), channel_id=1, source_target_pairs={{0,64},{64,128},{128,192},{192,0},{1,65},{65,129},{129,193},{193,1... | collective-permute-start | bytes 786440 | tf_op jit(solution)/shard_map/ppermute | solution.py:231
  21.9 1.7 %collective-permute-start.2 = (bf16[1024,128]{1,0:T(8,128)(2,1)S(1)}, bf16[1024,128]{1,0:T(8,128)(2,1)S(1)}, u32[]{:S(2)}, u32[]{:S(2)}) collective-permute-start(bf16[1024,128]{1,0:T(8,128)(2,1)S(1)} %bitcast.6), channel_id=1, source_target_pairs={{0,192},{64,0},{128,64},{192,128},{1,193},{65,1},{129,65},{193,129... | collective-permute-start | bytes 786440 | tf_op jit(solution)/shard_map/ppermute | solution.py:231
  24.3 2.1 %collective-permute-start.1 = (bf16[1024,128]{1,0:T(8,128)(2,1)S(1)}, bf16[1024,128]{1,0:T(8,128)(2,1)S(1)}, u32[]{:S(2)}, u32[]{:S(2)}) collective-permute-start(bf16[1024,128]{1,0:T(8,128)(2,1)S(1)} %bitcast.7), channel_id=1, source_target_pairs={{0,128},{64,192},{128,0},{192,64},{1,129},{65,193},{129,1},{193,65... | collective-permute-start | bytes 786440 | tf_op jit(solution)/shard_map/ppermute | solution.py:231
  26.3 0.0 copy-start.2
  26.3 0.0 copy-done
  26.3 0.0 copy-done.1
  26.3 0.6 copy-done.2
  27.0 1.9 %shard_map.68 = (f32[8,512]{1,0:T(8,128)S(1)}, f32[8,512]{1,0:T(8,128)S(1)}) custom-call(s32[1,1]{1,0:T(1,128)} %bitcast.y_ref, s32[1,1,16]{2,1,0:T(1,128)S(1)} %copy-done.2, s32[1,1]{1,0:T(1,128)S(6)} %copy.7.count_ref, bf16[1024,128]{1,0:T(8,128)(2,1)S(1)} %copy-done, bf16[1024,128]{1,0:T(8,128)(2,1)S(1)} %bitcast.8, f32[32,128]{1,0:T(8,128)S(1)} %bitcast.10), custom_call_target="tpu_custom_call" | custom-call | flops 1073741824 | bytes 4194304 | tf_op jit(solution)/shard_map/pallas_call | solution.py:209
  28.9 1.9 %collective-permute-done.piece_ref.by1_ref = bf16[1024,128]{1,0:T(8,128)(2,1)S(1)} collective-permute-done((bf16[1024,128]{1,0:T(8,128)(2,1)S(1)}, bf16[1024,128]{1,0:T(8,128)(2,1)S(1)}, u32[]{:S(2)}, u32[]{:S(2)}) %collective-permute-start) | collective-permute-done | bytes 262176 | tf_op jit(solution)/shard_map/ppermute | solution.py:231
  30.8 1.9 %shard_map.69 = (f32[8,512]{1,0:T(8,128)S(1)}, f32[8,512]{1,0:T(8,128)S(1)}) custom-call(s32[1,1]{1,0:T(1,128)} %bitcast.y_ref, s32[1,1,16]{2,1,0:T(1,128)S(1)} %copy-done.2, s32[1,1]{1,0:T(1,128)S(6)} %copy.7.count_ref, bf16[1024,128]{1,0:T(8,128)(2,1)S(1)} %copy-done, bf16[1024,128]{1,0:T(8,128)(2,1)S(1)} %collective-permute-done.piece_ref.by1_ref, ...), custom_call_target="tpu_custom_call" | custom-call | flops 1073741824 | bytes 4194304 | tf_op jit(solution)/shard_map/pallas_call | solution.py:209
  32.6 0.0 collective-permute-done.2.piece_ref.by3_ref
  32.6 1.9 %shard_map.70 = (f32[8,512]{1,0:T(8,128)S(1)}, f32[8,512]{1,0:T(8,128)S(1)}) custom-call(s32[1,1]{1,0:T(1,128)} %bitcast.y_ref, s32[1,1,16]{2,1,0:T(1,128)S(1)} %copy-done.2, s32[1,1]{1,0:T(1,128)S(6)} %copy.7.count_ref, bf16[1024,128]{1,0:T(8,128)(2,1)S(1)} %copy-done, bf16[1024,128]{1,0:T(8,128)(2,1)S(1)} %collective-permute-done.2.piece_ref.by3_ref, ...), custom_call_target="tpu_custom_call" | custom-call | flops 1073741824 | bytes 4194304 | tf_op jit(solution)/shard_map/pallas_call | solution.py:209
  34.5 0.0 collective-permute-done.1.piece_ref.by2_ref
  34.5 1.2 shard_map.71
  35.7 11.0 %all_to_all.26.parts_ref = f32[8,8,128]{2,1,0:T(8,128)S(1)} all-to-all(f32[8,8,128]{2,1,0:T(8,128)S(1)} %shard_map.71), channel_id=1, replica_groups=mesh['y'=4,'z'=8,'x'=4,'c'=2] {'x','c'}, dimensions={0} | all-to-all | bytes 65536 | tf_op jit(solution)/shard_map/all_to_all | solution.py:205
  46.8 2.5 %shard_map.72 = (f32[32,32,128]{2,1,0:T(8,128)S(1)}, bf16[4096,128]{1,0:T(8,128)(2,1)S(1)}) custom-call(s32[1,1]{1,0:T(1,128)} %bitcast.y_ref, s32[1,1,16]{2,1,0:T(1,128)S(1)} %copy-done.2, s32[1,1]{1,0:T(1,128)S(6)} %copy.7.count_ref, bf16[1024,128]{1,0:T(8,128)(2,1)S(1)} %copy-done, bf16[1024,128]{1,0:T(8,128)(2,1)S(1)} %bitcast.9, ...), custom_call_target="tpu_custom_call" | custom-call | flops 1073741824 | bytes 4194304 | tf_op jit(solution)/shard_map/pallas_call | solution.py:209
  49.3 28.1 %all_to_all.27.parts_ref = f32[32,32,128]{2,1,0:T(8,128)S(1)} all-to-all(f32[32,32,128]{2,1,0:T(8,128)S(1)} %get-tuple-element.19), channel_id=1, replica_groups=mesh['y'=4,'z'=8,'x'=4,'c'=2] {'y','z'}, dimensions={0} | all-to-all | bytes 1048576 | tf_op jit(solution)/shard_map/all_to_all | solution.py:205
  77.4 2.5 %shard_map.73 = f32[8,8,128]{2,1,0:T(8,128)S(1)} custom-call(s32[1,1,16]{2,1,0:T(1,128)S(1)} %copy-done.2, s32[1,1]{1,0:T(1,128)S(6)} %copy.7.count_ref, bf16[1024,128]{1,0:T(8,128)(2,1)S(1)} %copy-done, bf16[4096,128]{1,0:T(8,128)(2,1)S(1)} %get-tuple-element.18.targets_ref, f32[32,32,128]{2,1,0:T(8,128)S(1)} %all_to_all.27.parts_ref), custom_call_target="tpu_custom_call" | custom-call | flops 1073741824 | bytes 4194304 | tf_op jit(solution)/shard_map/pallas_call | solution.py:209
  80.0 10.2 %all_to_all.28.parts_ref = f32[8,8,128]{2,1,0:T(8,128)S(1)} all-to-all(f32[8,8,128]{2,1,0:T(8,128)S(1)} %shard_map.73), channel_id=1, replica_groups=mesh['y'=4,'z'=8,'x'=4,'c'=2] {'x','c'}, dimensions={0} | all-to-all | bytes 65536 | tf_op jit(solution)/shard_map/all_to_all | solution.py:205
  90.2 3.3 %shard_map.74 = (f32[32,32,128]{2,1,0:T(8,128)S(1)}, f32[8,128]{1,0:T(8,128)}) custom-call(s32[1,1,16]{2,1,0:T(1,128)S(1)} %copy-done.2, s32[1,1]{1,0:T(1,128)S(6)} %copy.7.count_ref, bf16[1024,128]{1,0:T(8,128)(2,1)S(1)} %copy-done, bf16[4096,128]{1,0:T(8,128)(2,1)S(1)} %get-tuple-element.18.targets_ref, f32[8,8,128]{2,1,0:T(8,128)S(1)} %all_to_all.28.parts_ref), custom_call_target="tpu_custom_call" | custom-call | flops 1073741824 | bytes 4194304 | tf_op jit(solution)/shard_map/pallas_call | solution.py:209
  93.5 28.3 %all_to_all.29.parts_ref = f32[32,32,128]{2,1,0:T(8,128)S(1)} all-to-all(f32[32,32,128]{2,1,0:T(8,128)S(1)} %get-tuple-element.21), channel_id=1, replica_groups=mesh['y'=4,'z'=8,'x'=4,'c'=2] {'y','z'}, dimensions={0} | all-to-all | bytes 1048576 | tf_op jit(solution)/shard_map/all_to_all | solution.py:205
  121.8 1.3 %shard_map.75 = f32[32,128]{1,0:T(8,128)} custom-call(bf16[4096,128]{1,0:T(8,128)(2,1)S(1)} %get-tuple-element.18.targets_ref, f32[32,32,128]{2,1,0:T(8,128)S(1)} %all_to_all.29.parts_ref), custom_call_target="tpu_custom_call" | custom-call | flops 1073741824 | bytes 4194304 | tf_op jit(solution)/shard_map/pallas_call | solution.py:209
Async XLA Ops:
  1.4 24.9 %copy-start = (bf16[1024,128]{1,0:T(8,128)(2,1)S(1)}, bf16[1024,128]{1,0:T(8,128)(2,1)}, u32[]{:S(2)}) copy-start(bf16[1024,128]{1,0:T(8,128)(2,1)} %sources_ref.13) | copy-start | bytes 786436
  1.4 24.9 %copy-start.1 = (f32[4096]{0:T(1024)S(1)}, f32[4096]{0:T(1024)}, u32[]{:S(2)}) copy-start(f32[4096]{0:T(1024)} %param.7) | copy-start | bytes 49156
  20.4 10.4 %collective-permute-start = (bf16[1024,128]{1,0:T(8,128)(2,1)S(1)}, bf16[1024,128]{1,0:T(8,128)(2,1)S(1)}, u32[]{:S(2)}, u32[]{:S(2)}) collective-permute-start(bf16[1024,128]{1,0:T(8,128)(2,1)S(1)} %bitcast.5), channel_id=1, source_target_pairs={{0,64},{64,128},{128,192},{192,0},{1,65},{65,129},{129,193},{193,1... | collective-permute-start | bytes 786440 | tf_op jit(solution)/shard_map/ppermute | solution.py:231
  21.9 10.7 %collective-permute-start.2 = (bf16[1024,128]{1,0:T(8,128)(2,1)S(1)}, bf16[1024,128]{1,0:T(8,128)(2,1)S(1)}, u32[]{:S(2)}, u32[]{:S(2)}) collective-permute-start(bf16[1024,128]{1,0:T(8,128)(2,1)S(1)} %bitcast.6), channel_id=1, source_target_pairs={{0,192},{64,0},{128,64},{192,128},{1,193},{65,1},{129,65},{193,129... | collective-permute-start | bytes 786440 | tf_op jit(solution)/shard_map/ppermute | solution.py:231
  24.3 10.3 %collective-permute-start.1 = (bf16[1024,128]{1,0:T(8,128)(2,1)S(1)}, bf16[1024,128]{1,0:T(8,128)(2,1)S(1)}, u32[]{:S(2)}, u32[]{:S(2)}) collective-permute-start(bf16[1024,128]{1,0:T(8,128)(2,1)S(1)} %bitcast.7), channel_id=1, source_target_pairs={{0,128},{64,192},{128,0},{192,64},{1,129},{65,193},{129,1},{193,65... | collective-permute-start | bytes 786440 | tf_op jit(solution)/shard_map/ppermute | solution.py:231
  26.3 0.7 copy-start.2

commit v3 on v2

v3 whole, which is shorter than its diff:
```python
import functools
import math

import jax
import jax.numpy as jnp
from jax import lax
from jax.experimental import pallas as pl
from jax.experimental.pallas import tpu as pltpu
from jax.sharding import Mesh
from jax.sharding import PartitionSpec as P

BLOCK = 512
LANES = 128
EMB = 128
SB_DEV = 2
TB_DEV = 8
PAIRS_MAX = 16
ITERS = 2
NEG_START = -1e30
EPS_REG = 0.2
LOG2E = math.log2(math.e)
SCALE = 2.0 * LOG2E / EPS_REG
GROUPS = BLOCK // LANES
HALF = BLOCK // 2
CHUNK = 32
CHUNKS = BLOCK // CHUNK
LAG = 12
PUSH_AT = 4

bf16 = jnp.bfloat16
f32 = jnp.float32


def squares(points):
    values = points.astype(f32)
    sq = values * values
    high = sq.astype(bf16)
    low = (sq - high.astype(f32)).astype(bf16)
    parts = jnp.concatenate([high, low], axis=1)
    ones = jnp.ones((16, 2 * EMB), bf16)
    groups = points.shape[0] // HALF
    slots = [(g % 2, g // 2 % 2) for g in range(groups)]

    def sums(products):
        for g, (mxu, stage) in enumerate(slots):
            pltpu.matmul_push_rhs(parts[g * HALF:(g + 1) * HALF], stage, mxu, transpose=True)
            pltpu.matmul_acc_lhs(products[g], ones, load_staged_rhs=stage)
        rows = []
        for g in range(groups):
            out = pltpu.matmul_pop(products[g])
            rows += [out[0:1, :LANES], out[0:1, LANES:]]
        return jnp.concatenate(rows, axis=0)

    return pl.run_scoped(sums, [pltpu.ACC(mxu)((16, HALF), f32) for mxu, _ in slots])


def bias_columns(bias):
    high = bias.astype(bf16).astype(f32)
    rest = bias - high
    middle = rest.astype(bf16).astype(f32)
    low = rest - middle
    count = bias.shape[0]
    stacked = jnp.concatenate([high, middle, low, jnp.zeros((LANES - 3 * count, LANES), f32)], axis=0)
    return stacked.T.astype(bf16)


def combined(parts):
    highest = jnp.max(parts, axis=0)
    total = jnp.sum(jnp.exp2(parts - highest[None]), axis=0)
    return highest + jnp.log(total) * LOG2E


def half_bias(lse):
    return (-0.5 * EPS_REG / LOG2E) * (math.log2(32768) + lse)


def clear(acc_max, acc_sum):
    acc_max[...] = jnp.full(acc_max.shape, NEG_START, f32)
    acc_sum[...] = jnp.zeros(acc_sum.shape, f32)


def sweep(*operands):
    products = [[pltpu.ACC(m)((CHUNK, HALF), f32) for _ in range(CHUNKS)] for m in range(2)]
    pl.run_scoped(functools.partial(sweep_with, *operands), products)


def sweep_with(pairs_ref, count, kept_ref, sum_ref, bias, acc_max, acc_sum, even, odd, kept_first, offset, mxus):
    kept_bias = bias_columns(bias)
    lane = lax.broadcasted_iota(jnp.int32, (CHUNK, LANES), 1) & (bias.shape[0] - 1)
    ones = jnp.ones((HALF, LANES), bf16)
    zeros = jnp.zeros((CHUNK, LANES), bf16)
    buffers = (even, odd)

    def where(number):
        real = number < count
        pair = jnp.where(real, pairs_ref[jnp.minimum(number, PAIRS_MAX - 1)], 0)
        first, second = pair >> 3, pair & 7
        return (first, second) if kept_first else (jnp.where(real, second - offset, 0), first)

    def push(number, parity):
        _, place = where(number)
        for m in range(2):
            rows = sum_ref[pl.ds(pl.multiple_of(place * BLOCK + m * HALF, HALF), HALF), :]
            pltpu.matmul_push_rhs(jnp.concatenate([rows, ones], axis=1), parity, m, transpose=True)

    def issue(along, parity, j):
        rows = kept_ref[pl.ds(pl.multiple_of(along * BLOCK + j * CHUNK, CHUNK), CHUNK), :]
        start = j * CHUNK % LANES
        mine = jnp.where(lane == along * GROUPS + j * CHUNK // LANES, kept_bias[start:start + CHUNK], zeros)
        lhs = jnp.concatenate([rows, mine], axis=1)
        for m in range(2):
            pltpu.matmul_acc_lhs(mxus[m][j], lhs, load_staged_rhs=parity if j == 0 else None)

    def take(parity, j, peak):
        for m in range(2):
            out = pltpu.matmul_pop(mxus[m][j])
            buffers[parity][j * CHUNK:(j + 1) * CHUNK, m * HALF:(m + 1) * HALF] = out
            for r in range(0, CHUNK, 8):
                peak[m] = jnp.maximum(peak[m], out[r:r + 8])

    def add(parity, j, shift, partial):
        for r in range(j * CHUNK, (j + 1) * CHUNK, 8):
            partial = partial + jnp.exp2((buffers[parity][r:r + 8, :] - shift) * SCALE)
        return partial

    def settle(number, peak):
        _, place = where(number)
        block_max = jnp.max(jnp.concatenate(peak, axis=1), axis=0, keepdims=True)
        old_max = acc_max[pl.ds(place, 1), :]
        highest = jnp.where(number < count, jnp.maximum(old_max, block_max), old_max)
        acc_max[pl.ds(place, 1), :] = highest
        acc_sum[pl.ds(place, 1), :] = acc_sum[pl.ds(place, 1), :] * jnp.exp2((old_max - highest) * SCALE)
        return jnp.broadcast_to(highest, (8, BLOCK))

    def fold(number, partial):
        _, place = where(number)
        block_sum = jnp.where((number >= 0) & (number < count), jnp.sum(partial, axis=0, keepdims=True), 0.0)
        place = jnp.where(number >= 0, place, 0)
        acc_sum[pl.ds(place, 1), :] = acc_sum[pl.ds(place, 1), :] + block_sum

    lowest = jnp.full((8, HALF), NEG_START, f32)
    nothing = jnp.zeros((8, BLOCK), f32)

    def body(i, parity, carry):
        peak0, peak1, shift, partial = carry
        peak = [peak0, peak1]
        along, _ = where(i + 1)
        for j in range(CHUNKS):
            issue(along, 1 - parity, j)
            if j == PUSH_AT:
                push(i + 2, parity)
            if j < LAG:
                take(parity, j + CHUNKS - LAG, peak)
                partial = add(1 - parity, j + CHUNKS - LAG, shift, partial)
                if j == LAG - 1:
                    fold(i - 1, partial)
                    shift = settle(i, peak)
                    peak = [lowest, lowest]
                    partial = nothing
            else:
                take(1 - parity, j - LAG, peak)
                partial = add(parity, j - LAG, shift, partial)
        return (*peak, shift, partial)

    push(0, 0)
    along, _ = where(0)
    peak = [lowest, lowest]
    for j in range(CHUNKS):
        issue(along, 0, j)
        if j == PUSH_AT:
            push(1, 1)
        if j >= LAG:
            take(0, j - LAG, peak)

    def turn(k, carry):
        return body(2 * k + 1, 1, body(2 * k, 0, carry))

    turns = (count + 1) >> 1
    carry = lax.fori_loop(0, turns, turn, (*peak, nothing, nothing))
    peak0, peak1, shift, partial = carry
    for j in range(LAG):
        take(0, j + CHUNKS - LAG, [peak0, peak1])
        partial = add(1, j + CHUNKS - LAG, shift, partial)
    fold(2 * turns - 1, partial)
    for m in range(2):
        pltpu.matmul_acc_lhs(mxus[m][0], jnp.zeros((CHUNK, 2 * LANES), bf16), load_staged_rhs=1)
        pltpu.matmul_pop(mxus[m][0])


def finish(blocks, acc_max, acc_sum, out_ref):
    total = acc_sum[...]
    lse = jnp.where(total > 0, acc_max[...] * SCALE + jnp.log(total) * LOG2E, NEG_START)
    dense = jnp.concatenate(
        [lse[b:b + 1, q * LANES:(q + 1) * LANES] for b in range(blocks) for q in range(GROUPS)], axis=0
    )
    for k in range(out_ref.shape[0]):
        out_ref[k] = dense


def piece_rows(by, first, last, y_ref, pairs_ref, count_ref, sources_ref, potential_ref, *refs):
    if last:
        low_ref, high_ref, *refs = refs
        *refs, piece_ref = refs
        piece_ref[0:BLOCK, :] = low_ref[...]
        piece_ref[BLOCK:2 * BLOCK, :] = high_ref[...]
    else:
        piece_ref, *refs = refs
    if not first:
        in_max, in_sum, *refs = refs
    squares_ref, *refs = refs
    if first:
        source_squares_ref, *refs = refs
        source_squares_ref[...] = squares(sources_ref[...])
    if last:
        out_ref, *refs = refs
    acc_max, acc_sum, even, odd, chosen = refs
    if first:
        clear(acc_max, acc_sum)
    else:
        acc_max[...] = in_max[...]
        acc_sum[...] = in_sum[...]
    block0 = ((y_ref[0, 0] + 4 - by) & 3) * 2
    count = count_ref[0, 0]

    def pick(number, found):
        pair = pairs_ref[0, 0, number]
        chosen[found] = pair
        return found + jnp.where((pair & 6) == block0, 1, 0)

    found = lax.fori_loop(0, count, pick, 0)
    potential = potential_ref[pl.ds(pl.multiple_of(block0 * GROUPS, 8), 8), :]
    squared = squares(piece_ref[...])
    squares_ref[...] = squared
    bias = 0.5 * (potential - squared)
    sweep(chosen, found, piece_ref, sources_ref, bias, acc_max, acc_sum, even, odd, False, block0)
    if last:
        finish(SB_DEV, acc_max, acc_sum, out_ref)


def copied(pairs_ref, chosen):
    def one(number, carry):
        chosen[number] = pairs_ref[0, 0, number]
        return carry

    lax.fori_loop(0, PAIRS_MAX, one, 0)


def next_rows(pairs_ref, count_ref, sources_ref, targets_ref, parts_ref, out_ref, acc_max, acc_sum, even, odd, chosen):
    bias = half_bias(combined(parts_ref[...]))
    copied(pairs_ref, chosen)
    clear(acc_max, acc_sum)
    sweep(chosen, count_ref[0, 0], targets_ref, sources_ref, bias, acc_max, acc_sum, even, odd, False, 0)
    finish(SB_DEV, acc_max, acc_sum, out_ref)


def first_columns(y_ref, pairs_ref, count_ref, sources_ref, own_ref, by1_ref, low2_ref, high2_ref, by3_ref, parts_ref, out_ref, targets_ref, *scratch):
    def place(by):
        return pl.multiple_of(((y_ref[0, 0] + 4 - by) & 3) * 2 * BLOCK, 2 * BLOCK)

    for by, ref in ((0, own_ref), (1, by1_ref), (3, by3_ref)):
        targets_ref[pl.ds(place(by), 2 * BLOCK), :] = ref[...]
    targets_ref[pl.ds(place(2), BLOCK), :] = low2_ref[...]
    targets_ref[pl.ds(place(2) + BLOCK, BLOCK), :] = high2_ref[...]
    half_columns(pairs_ref, count_ref, sources_ref, targets_ref, parts_ref, out_ref, *scratch)


def half_columns(pairs_ref, count_ref, sources_ref, targets_ref, parts_ref, out_ref, acc_max, acc_sum, even, odd, chosen):
    bias = half_bias(combined(parts_ref[...]))
    copied(pairs_ref, chosen)
    clear(acc_max, acc_sum)
    sweep(chosen, count_ref[0, 0], sources_ref, targets_ref, bias, acc_max, acc_sum, even, odd, True, 0)
    finish(TB_DEV, acc_max, acc_sum, out_ref)


def last_columns(pairs_ref, count_ref, sources_ref, targets_ref, squares_ref, parts_ref, out_ref, potential_ref, *scratch):
    potential_ref[...] = squares_ref[...] + 2.0 * half_bias(combined(parts_ref[...]))
    half_columns(pairs_ref, count_ref, sources_ref, targets_ref, parts_ref, out_ref, *scratch)


def last_potential(y_ref, own_ref, by1_ref, by2_ref, by3_ref, parts_ref, potential_ref):
    potential_ref[...] = 2.0 * half_bias(combined(parts_ref[...]))
    for by, ref in enumerate((own_ref, by1_ref, by2_ref, by3_ref)):
        rows = pl.ds(pl.multiple_of(((y_ref[0, 0] + 4 - by) & 3) * 8, 8), 8)
        potential_ref[rows, :] = potential_ref[rows, :] + ref[...]


SMEM = pl.BlockSpec(memory_space=pltpu.SMEM)
VMEM = pl.BlockSpec(memory_space=pltpu.VMEM)
PARAMS = pltpu.CompilerParams(vmem_limit_bytes=24 * 1024 * 1024)
STATS = [pltpu.VMEM((8, BLOCK), f32)] * 2


def work():
    return [pltpu.VMEM((BLOCK, BLOCK), f32)] * 2 + [pltpu.SMEM((PAIRS_MAX,), jnp.int32)]


def spread(parts, axes):
    return lax.all_to_all(parts, axes, 0, 0, tiled=True)


def call(kernel, out_shape, smem, vmem, scratch):
    return pl.pallas_call(
        kernel,
        out_shape=out_shape,
        in_specs=[SMEM] * len(smem) + [VMEM] * len(vmem),
        out_specs=jax.tree.map(lambda _: VMEM, out_shape),
        scratch_shapes=scratch,
        compiler_params=PARAMS,
        cost_estimate=pl.CostEstimate(flops=1 << 30, bytes_accessed=1 << 22, transcendentals=1 << 20),
    )(*smem, *vmem)


def per_device(source_points, target_points, initial_potential, pair_list, pair_count):
    n_src = lax.axis_size(("y", "z"))
    n_tgt = lax.axis_size(("x", "c"))
    n_y, n_z = lax.axis_size("y"), lax.axis_size("z")
    own = target_points.shape[0]
    src_rows = source_points.shape[0] // LANES
    tgt_rows = own * n_src // LANES
    y = lax.axis_index("y").astype(jnp.int32).reshape(1, 1)

    piece = spread(jnp.broadcast_to(target_points[None], (n_z, own, EMB)), "z").reshape(n_z * own, EMB)

    def along_y(array, by):
        return lax.ppermute(array, "y", [(i, (i + by) % n_y) for i in range(n_y)])

    by1, by3 = along_y(piece, 1), along_y(piece, n_y - 1)
    low2, high2 = along_y(by1[:BLOCK], 1), along_y(by3[BLOCK:], n_y - 1)
    potential = initial_potential.reshape(tgt_rows, LANES)
    row_shape = jax.ShapeDtypeStruct((n_tgt, src_rows, LANES), f32)
    col_shape = jax.ShapeDtypeStruct((n_src, tgt_rows, LANES), f32)
    stat = jax.ShapeDtypeStruct((8, BLOCK), f32)
    square_shape = jax.ShapeDtypeStruct((8, LANES), f32)
    whole_piece = pltpu.VMEM((2 * BLOCK, EMB), bf16)
    target_squares = {}
    lists = (y, pair_list, pair_count)
    target_squares[0], source_squares, *stats = call(
        functools.partial(piece_rows, 0, True, False),
        [square_shape, square_shape, stat, stat],
        lists,
        (source_points, potential, piece),
        work(),
    )
    for by, array in ((1, by1), (3, by3)):
        target_squares[by], *stats = call(
            functools.partial(piece_rows, by, False, False),
            [square_shape, stat, stat],
            lists,
            (source_points, potential, array, *stats),
            work(),
        )
    target_squares[2], row_parts = call(
        functools.partial(piece_rows, 2, False, True),
        [square_shape, row_shape],
        lists,
        (source_points, potential, low2, high2, *stats),
        STATS + work() + [whole_piece],
    )
    row_parts = spread(row_parts, ("x", "c"))
    col_parts, targets = call(
        first_columns,
        [col_shape, jax.ShapeDtypeStruct((tgt_rows * LANES, EMB), bf16)],
        lists,
        (source_points, piece, by1, low2, high2, by3, row_parts),
        STATS + work(),
    )
    for iteration in range(1, ITERS):
        col_parts = spread(col_parts, ("y", "z"))
        row_parts = call(
            next_rows, row_shape, (pair_list, pair_count), (source_points, targets, col_parts), STATS + work()
        )
        row_parts = spread(row_parts, ("x", "c"))
        if iteration < ITERS - 1:
            col_parts = call(
                half_columns, col_shape, (pair_list, pair_count), (source_points, targets, row_parts), STATS + work()
            )
        else:
            col_parts, source_potential = call(
                last_columns,
                [col_shape, square_shape],
                (pair_list, pair_count),
                (source_points, targets, source_squares, row_parts),
                STATS + work(),
            )
    col_parts = spread(col_parts, ("y", "z"))
    target_potential = call(
        last_potential,
        jax.ShapeDtypeStruct((tgt_rows, LANES), f32),
        (y,),
        (*(target_squares[by] for by in range(4)), col_parts),
        [],
    )
    return source_potential.reshape(-1), target_potential.reshape(-1)


def solution(mesh):
    fine = Mesh(mesh.devices.reshape(4, 8, 4, 2), ("y", "z", "x", "c"))
    src, tgt = ("y", "z"), ("x", "c")
    placed = (P(src, None), P(tgt + src, None), P(tgt), P(src, tgt, None), P(src, tgt))
    return jax.shard_map(
        per_device, mesh=fine, in_specs=placed, out_specs=(P(src), P(tgt)), check_vma=False
    )
```

time: 123 us -> 115 us (0.935)
  blocking collectives: 96.6 us -> 85 us
  waiting for transfers between devices: 1.9 us -> 3.99 us
  starting transfers between devices: 5.31 us -> 6.87 us
    all_to_all x5, blocking collectives: 96.6 us -> 85 us  [spread(): return lax.all_to_all(parts, axes, 0, 0, tiled=True)]
    ppermute x3 -> x4, waiting for transfers between devices: 1.9 us -> 3.99 us  [along_y(): return lax.ppermute(array, 'y', [(i, (i + by) % n_y) for i in range(n_y)])]
    ppermute x3 -> x4, starting transfers between devices: 5.31 us -> 6.87 us  [along_y(): return lax.ppermute(array, 'y', [(i, (i + by) % n_y) for i in range(n_y)])]
    pallas_call x8, Pallas kernels: 16.4 us -> 15.2 us  [call(): pl.pallas_call(kernel, out_shape=out_shape, in_specs=[SMEM] * len(smem) +...]
  transfers between devices with their start and end apart: 3 -> 4, of which waited for: 1 -> 2; matrix products, arithmetic and copies ran while one was open for 0% -> 0% of each run, Pallas kernels for 5% -> 4%
where the time goes in v3:
time: 115 us; the launch traced here: 114 us
  blocking collectives  85 us (74%)
  Pallas kernels  15.2 us (13%)
  starting transfers between devices  6.87 us (6%)
  waiting for transfers between devices  3.99 us (3%)
  local copies, waits for them, and re-layouts  1.46 us (1%)
  between operations  1.39 us (1%)
    all_to_all x5, blocking collectives, spread(): return lax.all_to_all(parts, axes, 0, 0, tiled=True)  85 us
    pallas_call x8, Pallas kernels, call(): pl.pallas_call(kernel, out_shape=out_shape, in_specs=[SMEM] * len(smem) +...  15.2 us
    ppermute x4, starting transfers between devices, along_y(): return lax.ppermute(array, 'y', [(i, (i + by) % n_y) for i in range(n_y)])  6.87 us
    ppermute x4, waiting for transfers between devices, along_y(): return lax.ppermute(array, 'y', [(i, (i + by) % n_y) for i in range(n_y)])  3.99 us
  transfers between devices with their start and end apart: 4, of which 2 were waited for; matrix products, arithmetic and copies ran while one was open for 0% of the time, Pallas kernels for 4%

profile of v3, /device:TPU:32, one launch (start us, length us, event | category | flops | bytes accessed | tf_op | source)
XLA Modules:
  0.0 113.9 jit_solution(17883564427090582876)
XLA Ops:
  0.6 0.8 broadcast_in_dim.2
  1.4 0.0 copy-start
  1.4 0.0 copy-start.1
  1.4 18.9 %all_to_all.25 = bf16[8,128,128]{2,1,0:T(8,128)(2,1)S(1)} all-to-all(bf16[8,128,128]{2,1,0:T(8,128)(2,1)S(1)} %broadcast_in_dim.2), channel_id=1, replica_groups=mesh['y'=4,'z'=8,'x'=4,'c'=2] {'z'}, dimensions={0} | all-to-all | bytes 524288 | tf_op jit(solution)/shard_map/all_to_all | solution.py:298
  20.4 3.0 %collective-permute-start.2 = (bf16[1024,128]{1,0:T(8,128)(2,1)S(1)}, bf16[1024,128]{1,0:T(8,128)(2,1)S(1)}, u32[]{:S(2)}, u32[]{:S(2)}) collective-permute-start(bf16[1024,128]{1,0:T(8,128)(2,1)S(1)} %bitcast.5), channel_id=1, source_target_pairs={{0,192},{64,0},{128,64},{192,128},{1,193},{65,1},{129,65},{193,129... | collective-permute-start | bytes 786440 | tf_op jit(solution)/shard_map/ppermute | solution.py:325
  23.4 0.0 collective-permute-start
  24.0 0.0 copy-start.2
  24.1 0.0 copy-done
  24.1 0.0 copy-done.1
  24.1 0.6 copy-done.2
  24.7 1.9 %shard_map.68 = (f32[8,128]{1,0:T(8,128)S(1)}, f32[8,128]{1,0:T(8,128)S(1)}, f32[8,512]{1,0:T(8,128)S(1)}, f32[8,512]{1,0:T(8,128)S(1)}) custom-call(s32[1,1]{1,0:T(1,128)} %bitcast.y_ref, s32[1,1,16]{2,1,0:T(1,128)S(1)} %copy-done.2, s32[1,1]{1,0:T(1,128)S(6)} %copy.7.count_ref, bf16[1024,128]{1,0:T(8,128)(2,1)S(1)} %copy-done, f32[32,128]{1,0:T(8,128)S(1)} %bitcast.9, ...), custom_call_target="tpu_custom_call" | custom-call | flops 1073741824 | bytes 4194304 | tf_op jit(solution)/shard_map/pallas_call | solution.py:302
  26.6 0.7 collective-permute-done.2.refs_0_.by3_ref
  27.3 3.8 %collective-permute-start.3 = (bf16[512,128]{1,0:T(8,128)(2,1)S(1)}, bf16[512,128]{1,0:T(8,128)(2,1)S(1)}, u32[]{:S(2)}, u32[]{:S(2)}) collective-permute-start(bf16[512,128]{1,0:T(8,128)(2,1)S(1)} %slice.9), channel_id=1, source_target_pairs={{0,192},{64,0},{128,64},{192,128},{1,193},{65,1},{129,65},{193,129... | collective-permute-start | bytes 393224 | tf_op jit(solution)/shard_map/ppermute | solution.py:325
  31.1 0.0 collective-permute-done.refs_0_.by1_ref
  31.1 0.1 collective-permute-start.1
  31.2 1.2 %shard_map.69 = (f32[8,128]{1,0:T(8,128)S(1)}, f32[8,512]{1,0:T(8,128)S(1)}, f32[8,512]{1,0:T(8,128)S(1)}) custom-call(s32[1,1]{1,0:T(1,128)} %bitcast.y_ref, s32[1,1,16]{2,1,0:T(1,128)S(1)} %copy-done.2, s32[1,1]{1,0:T(1,128)S(6)} %copy.7.count_ref, bf16[1024,128]{1,0:T(8,128)(2,1)S(1)} %copy-done, f32[32,128]{1,0:T(8,128)S(1)} %bitcast.10, ...), custom_call_target="tpu_custom_call" | custom-call | flops 1073741824 | bytes 4194304 | tf_op jit(solution)/shard_map/pallas_call | solution.py:302
  32.4 1.7 %shard_map.70 = (f32[8,128]{1,0:T(8,128)S(1)}, f32[8,512]{1,0:T(8,128)S(1)}, f32[8,512]{1,0:T(8,128)S(1)}) custom-call(s32[1,1]{1,0:T(1,128)} %bitcast.y_ref, s32[1,1,16]{2,1,0:T(1,128)S(1)} %copy-done.2, s32[1,1]{1,0:T(1,128)S(6)} %copy.7.count_ref, bf16[1024,128]{1,0:T(8,128)(2,1)S(1)} %copy-done, f32[32,128]{1,0:T(8,128)S(1)} %bitcast.11, ...), custom_call_target="tpu_custom_call" | custom-call | flops 1073741824 | bytes 4194304 | tf_op jit(solution)/shard_map/pallas_call | solution.py:302
  34.1 0.0 collective-permute-done.3.refs_1_.high2_ref
  34.1 3.3 %collective-permute-done.1.refs_0_.low2_ref = bf16[512,128]{1,0:T(8,128)(2,1)S(1)} collective-permute-done((bf16[512,128]{1,0:T(8,128)(2,1)S(1)}, bf16[512,128]{1,0:T(8,128)(2,1)S(1)}, u32[]{:S(2)}, u32[]{:S(2)}) %collective-permute-start.1) | collective-permute-done | bytes 131104 | tf_op jit(solution)/shard_map/ppermute | solution.py:325
  37.4 1.7 %shard_map.71 = (f32[8,128]{1,0:T(8,128)S(1)}, f32[8,8,128]{2,1,0:T(8,128)S(1)}) custom-call(s32[1,1]{1,0:T(1,128)} %bitcast.y_ref, s32[1,1,16]{2,1,0:T(1,128)S(1)} %copy-done.2, s32[1,1]{1,0:T(1,128)S(6)} %copy.7.count_ref, bf16[1024,128]{1,0:T(8,128)(2,1)S(1)} %copy-done, f32[32,128]{1,0:T(8,128)S(1)} %bitcast.12, ...), custom_call_target="tpu_custom_call" | custom-call | flops 1073741824 | bytes 4194304 | tf_op jit(solution)/shard_map/pallas_call | solution.py:302
  39.1 9.8 %all_to_all.26.parts_ref = f32[8,8,128]{2,1,0:T(8,128)S(1)} all-to-all(f32[8,8,128]{2,1,0:T(8,128)S(1)} %get-tuple-element.24), channel_id=1, replica_groups=mesh['y'=4,'z'=8,'x'=4,'c'=2] {'x','c'}, dimensions={0} | all-to-all | bytes 65536 | tf_op jit(solution)/shard_map/all_to_all | solution.py:298
  48.9 2.5 %shard_map.72 = (f32[32,32,128]{2,1,0:T(8,128)S(1)}, bf16[4096,128]{1,0:T(8,128)(2,1)S(1)}) custom-call(s32[1,1]{1,0:T(1,128)} %bitcast.y_ref, s32[1,1,16]{2,1,0:T(1,128)S(1)} %copy-done.2, s32[1,1]{1,0:T(1,128)S(6)} %copy.7.count_ref, bf16[1024,128]{1,0:T(8,128)(2,1)S(1)} %copy-done, bf16[1024,128]{1,0:T(8,128)(2,1)S(1)} %bitcast.8, ...), custom_call_target="tpu_custom_call" | custom-call | flops 1073741824 | bytes 4194304 | tf_op jit(solution)/shard_map/pallas_call | solution.py:302
  51.4 24.2 %all_to_all.27.parts_ref = f32[32,32,128]{2,1,0:T(8,128)S(1)} all-to-all(f32[32,32,128]{2,1,0:T(8,128)S(1)} %get-tuple-element.27), channel_id=1, replica_groups=mesh['y'=4,'z'=8,'x'=4,'c'=2] {'y','z'}, dimensions={0} | all-to-all | bytes 1048576 | tf_op jit(solution)/shard_map/all_to_all | solution.py:298
  75.6 2.6 %shard_map.73 = f32[8,8,128]{2,1,0:T(8,128)S(1)} custom-call(s32[1,1,16]{2,1,0:T(1,128)S(1)} %copy-done.2, s32[1,1]{1,0:T(1,128)S(6)} %copy.7.count_ref, bf16[1024,128]{1,0:T(8,128)(2,1)S(1)} %copy-done, bf16[4096,128]{1,0:T(8,128)(2,1)S(1)} %get-tuple-element.25.targets_ref, f32[32,32,128]{2,1,0:T(8,128)S(1)} %all_to_all.27.parts_ref), custom_call_target="tpu_custom_call" | custom-call | flops 1073741824 | bytes 4194304 | tf_op jit(solution)/shard_map/pallas_call | solution.py:302
  78.2 8.7 %all_to_all.28.parts_ref = f32[8,8,128]{2,1,0:T(8,128)S(1)} all-to-all(f32[8,8,128]{2,1,0:T(8,128)S(1)} %shard_map.73), channel_id=1, replica_groups=mesh['y'=4,'z'=8,'x'=4,'c'=2] {'x','c'}, dimensions={0} | all-to-all | bytes 65536 | tf_op jit(solution)/shard_map/all_to_all | solution.py:298
  86.9 2.9 %shard_map.74 = (f32[32,32,128]{2,1,0:T(8,128)S(1)}, f32[8,128]{1,0:T(8,128)}) custom-call(s32[1,1,16]{2,1,0:T(1,128)S(1)} %copy-done.2, s32[1,1]{1,0:T(1,128)S(6)} %copy.7.count_ref, bf16[1024,128]{1,0:T(8,128)(2,1)S(1)} %copy-done, bf16[4096,128]{1,0:T(8,128)(2,1)S(1)} %get-tuple-element.25.targets_ref, f32[8,128]{1,0:T(8,128)S(1)} %get-tuple-element.26.squares_ref, ...), custom_call_target="tpu_custom_call" | custom-call | flops 1073741824 | bytes 4194304 | tf_op jit(solution)/shard_map/pallas_call | solution.py:302
  89.7 23.4 %all_to_all.29.parts_ref = f32[32,32,128]{2,1,0:T(8,128)S(1)} all-to-all(f32[32,32,128]{2,1,0:T(8,128)S(1)} %get-tuple-element.33), channel_id=1, replica_groups=mesh['y'=4,'z'=8,'x'=4,'c'=2] {'y','z'}, dimensions={0} | all-to-all | bytes 1048576 | tf_op jit(solution)/shard_map/all_to_all | solution.py:298
  113.1 0.7 shard_map.75
  (2 shorter events, 0.0 us)
Async XLA Ops:
  1.4 22.6 %copy-start = (bf16[1024,128]{1,0:T(8,128)(2,1)S(1)}, bf16[1024,128]{1,0:T(8,128)(2,1)}, u32[]{:S(2)}) copy-start(bf16[1024,128]{1,0:T(8,128)(2,1)} %sources_ref.13) | copy-start | bytes 786436
  1.4 22.6 %copy-start.1 = (f32[4096]{0:T(1024)S(1)}, f32[4096]{0:T(1024)}, u32[]{:S(2)}) copy-start(f32[4096]{0:T(1024)} %param.7) | copy-start | bytes 49156
  20.4 6.9 %collective-permute-start.2 = (bf16[1024,128]{1,0:T(8,128)(2,1)S(1)}, bf16[1024,128]{1,0:T(8,128)(2,1)S(1)}, u32[]{:S(2)}, u32[]{:S(2)}) collective-permute-start(bf16[1024,128]{1,0:T(8,128)(2,1)S(1)} %bitcast.5), channel_id=1, source_target_pairs={{0,192},{64,0},{128,64},{192,128},{1,193},{65,1},{129,65},{193,129... | collective-permute-start | bytes 786440 | tf_op jit(solution)/shard_map/ppermute | solution.py:325
  23.4 7.7 %collective-permute-start = (bf16[1024,128]{1,0:T(8,128)(2,1)S(1)}, bf16[1024,128]{1,0:T(8,128)(2,1)S(1)}, u32[]{:S(2)}, u32[]{:S(2)}) collective-permute-start(bf16[1024,128]{1,0:T(8,128)(2,1)S(1)} %bitcast.6), channel_id=1, source_target_pairs={{0,64},{64,128},{128,192},{192,0},{1,65},{65,129},{129,193},{193,1... | collective-permute-start | bytes 786440 | tf_op jit(solution)/shard_map/ppermute | solution.py:325
  24.0 0.7 copy-start.2
  27.3 6.8 %collective-permute-start.3 = (bf16[512,128]{1,0:T(8,128)(2,1)S(1)}, bf16[512,128]{1,0:T(8,128)(2,1)S(1)}, u32[]{:S(2)}, u32[]{:S(2)}) collective-permute-start(bf16[512,128]{1,0:T(8,128)(2,1)S(1)} %slice.9), channel_id=1, source_target_pairs={{0,192},{64,0},{128,64},{192,128},{1,193},{65,1},{129,65},{193,129... | collective-permute-start | bytes 393224 | tf_op jit(solution)/shard_map/ppermute | solution.py:325
  31.1 6.3 %collective-permute-start.1 = (bf16[512,128]{1,0:T(8,128)(2,1)S(1)}, bf16[512,128]{1,0:T(8,128)(2,1)S(1)}, u32[]{:S(2)}, u32[]{:S(2)}) collective-permute-start(bf16[512,128]{1,0:T(8,128)(2,1)S(1)} %slice.8), channel_id=1, source_target_pairs={{0,64},{64,128},{128,192},{192,0},{1,65},{65,129},{129,193},{193,1... | collective-permute-start | bytes 393224 | tf_op jit(solution)/shard_map/ppermute | solution.py:325

commit v4 on v3

v4 whole, which is shorter than its diff:
```python
import functools
import math

import jax
import jax.numpy as jnp
from jax import lax
from jax.experimental import pallas as pl
from jax.experimental.pallas import tpu as pltpu
from jax.sharding import Mesh
from jax.sharding import PartitionSpec as P

BLOCK = 512
LANES = 128
EMB = 128
SRC_BLOCKS = 8
TGT_BLOCKS = 2
PAIRS_MAX = 16
ITERS = 2
NEG_START = -1e30
EPS_REG = 0.2
LOG2E = math.log2(math.e)
SCALE = 2.0 * LOG2E / EPS_REG
GROUPS = BLOCK // LANES
HALF = BLOCK // 2
CHUNK = 32
CHUNKS = BLOCK // CHUNK
LAG = 12
PUSH_AT = 4

bf16 = jnp.bfloat16
f32 = jnp.float32


def squares(points):
    values = points.astype(f32)
    sq = values * values
    high = sq.astype(bf16)
    low = (sq - high.astype(f32)).astype(bf16)
    parts = jnp.concatenate([high, low], axis=1)
    ones = jnp.ones((16, 2 * EMB), bf16)
    groups = points.shape[0] // HALF
    slots = [(g % 2, g // 2 % 2) for g in range(groups)]

    def sums(products):
        for g, (mxu, stage) in enumerate(slots):
            pltpu.matmul_push_rhs(parts[g * HALF:(g + 1) * HALF], stage, mxu, transpose=True)
            pltpu.matmul_acc_lhs(products[g], ones, load_staged_rhs=stage)
        rows = []
        for g in range(groups):
            out = pltpu.matmul_pop(products[g])
            rows += [out[0:1, :LANES], out[0:1, LANES:]]
        return jnp.concatenate(rows, axis=0)

    return pl.run_scoped(sums, [pltpu.ACC(mxu)((16, HALF), f32) for mxu, _ in slots])


def bias_columns(bias):
    high = bias.astype(bf16).astype(f32)
    rest = bias - high
    middle = rest.astype(bf16).astype(f32)
    low = rest - middle
    count = bias.shape[0]
    stacked = jnp.concatenate([high, middle, low, jnp.zeros((LANES - 3 * count, LANES), f32)], axis=0)
    return stacked.T.astype(bf16)


def combined(parts):
    highest = jnp.max(parts, axis=0)
    total = jnp.sum(jnp.exp2(parts - highest[None]), axis=0)
    return highest + jnp.log(total) * LOG2E


def half_bias(lse):
    return (-0.5 * EPS_REG / LOG2E) * (math.log2(32768) + lse)


def clear(acc_max, acc_sum):
    acc_max[...] = jnp.full(acc_max.shape, NEG_START, f32)
    acc_sum[...] = jnp.zeros(acc_sum.shape, f32)


def sweep(*operands):
    products = [[pltpu.ACC(m)((CHUNK, HALF), f32) for _ in range(CHUNKS)] for m in range(2)]
    pl.run_scoped(functools.partial(sweep_with, *operands), products)


def sweep_with(pairs_ref, count, kept_ref, sum_ref, bias, acc_max, acc_sum, even, odd, kept_first, mxus):
    kept_bias = bias_columns(bias)
    lane = lax.broadcasted_iota(jnp.int32, (CHUNK, LANES), 1) & (bias.shape[0] - 1)
    ones = jnp.ones((HALF, LANES), bf16)
    zeros = jnp.zeros((CHUNK, LANES), bf16)
    buffers = (even, odd)

    def where(number):
        real = number < count
        pair = jnp.where(real, pairs_ref[jnp.minimum(number, PAIRS_MAX - 1)], 0)
        first, second = pair >> 1, pair & 1
        return (first, second) if kept_first else (second, first)

    def push(number, parity):
        _, place = where(number)
        for m in range(2):
            rows = sum_ref[pl.ds(pl.multiple_of(place * BLOCK + m * HALF, HALF), HALF), :]
            pltpu.matmul_push_rhs(jnp.concatenate([rows, ones], axis=1), parity, m, transpose=True)

    def issue(along, parity, j):
        rows = kept_ref[pl.ds(pl.multiple_of(along * BLOCK + j * CHUNK, CHUNK), CHUNK), :]
        start = j * CHUNK % LANES
        mine = jnp.where(lane == along * GROUPS + j * CHUNK // LANES, kept_bias[start:start + CHUNK], zeros)
        lhs = jnp.concatenate([rows, mine], axis=1)
        for m in range(2):
            pltpu.matmul_acc_lhs(mxus[m][j], lhs, load_staged_rhs=parity if j == 0 else None)

    def take(parity, j, peak):
        for m in range(2):
            out = pltpu.matmul_pop(mxus[m][j])
            buffers[parity][j * CHUNK:(j + 1) * CHUNK, m * HALF:(m + 1) * HALF] = out
            for r in range(0, CHUNK, 8):
                peak[m] = jnp.maximum(peak[m], out[r:r + 8])

    def add(parity, j, shift, partial):
        for r in range(j * CHUNK, (j + 1) * CHUNK, 8):
            partial = partial + jnp.exp2((buffers[parity][r:r + 8, :] - shift) * SCALE)
        return partial

    def settle(number, peak):
        _, place = where(number)
        block_max = jnp.max(jnp.concatenate(peak, axis=1), axis=0, keepdims=True)
        old_max = acc_max[pl.ds(place, 1), :]
        highest = jnp.where(number < count, jnp.maximum(old_max, block_max), old_max)
        acc_max[pl.ds(place, 1), :] = highest
        acc_sum[pl.ds(place, 1), :] = acc_sum[pl.ds(place, 1), :] * jnp.exp2((old_max - highest) * SCALE)
        return jnp.broadcast_to(highest, (8, BLOCK))

    def fold(number, partial):
        _, place = where(number)
        block_sum = jnp.where((number >= 0) & (number < count), jnp.sum(partial, axis=0, keepdims=True), 0.0)
        place = jnp.where(number >= 0, place, 0)
        acc_sum[pl.ds(place, 1), :] = acc_sum[pl.ds(place, 1), :] + block_sum

    lowest = jnp.full((8, HALF), NEG_START, f32)
    nothing = jnp.zeros((8, BLOCK), f32)

    def body(i, parity, carry):
        peak0, peak1, shift, partial = carry
        peak = [peak0, peak1]
        along, _ = where(i + 1)
        for j in range(CHUNKS):
            issue(along, 1 - parity, j)
            if j == PUSH_AT:
                push(i + 2, parity)
            if j < LAG:
                take(parity, j + CHUNKS - LAG, peak)
                partial = add(1 - parity, j + CHUNKS - LAG, shift, partial)
                if j == LAG - 1:
                    fold(i - 1, partial)
                    shift = settle(i, peak)
                    peak = [lowest, lowest]
                    partial = nothing
            else:
                take(1 - parity, j - LAG, peak)
                partial = add(parity, j - LAG, shift, partial)
        return (*peak, shift, partial)

    push(0, 0)
    along, _ = where(0)
    peak = [lowest, lowest]
    for j in range(CHUNKS):
        issue(along, 0, j)
        if j == PUSH_AT:
            push(1, 1)
        if j >= LAG:
            take(0, j - LAG, peak)

    def turn(k, carry):
        return body(2 * k + 1, 1, body(2 * k, 0, carry))

    turns = (count + 1) >> 1
    carry = lax.fori_loop(0, turns, turn, (*peak, nothing, nothing))
    peak0, peak1, shift, partial = carry
    for j in range(LAG):
        take(0, j + CHUNKS - LAG, [peak0, peak1])
        partial = add(1, j + CHUNKS - LAG, shift, partial)
    fold(2 * turns - 1, partial)
    for m in range(2):
        pltpu.matmul_acc_lhs(mxus[m][0], jnp.zeros((CHUNK, 2 * LANES), bf16), load_staged_rhs=1)
        pltpu.matmul_pop(mxus[m][0])


def finish(blocks, acc_max, acc_sum, out_ref, offset):
    total = acc_sum[...]
    lse = jnp.where(total > 0, acc_max[...] * SCALE + jnp.log(total) * LOG2E, NEG_START)
    dense = jnp.concatenate(
        [lse[b:b + 1, q * LANES:(q + 1) * LANES] for b in range(blocks) for q in range(GROUPS)], axis=0
    )
    if offset is not None:
        dense = dense + offset
    for k in range(out_ref.shape[0]):
        out_ref[k] = dense


def bits(list_row, y_from, y):
    pair = list_row.astype(jnp.int32)
    number = y_from * 4 + ((pair >> 3) << 1) + (pair & 1)
    mine = (pair >= 0) & (((pair >> 1) & 3) == y)
    return jnp.where(mine, jnp.left_shift(jnp.ones_like(number), jnp.where(mine, number, 0)), 0).astype(f32)


def first_rows(y_ref, own_ref, by1_ref, by2_ref, by3_ref, targets_ref, potential_ref, out_ref, sources_ref, source_squares_ref, target_squares_ref, pairs_ref, *scratch):
    y = y_ref[0, 0]
    rows = targets_ref.shape[0]
    kept = jnp.zeros((1, LANES), f32)
    for by, ref in enumerate((own_ref, by1_ref, by2_ref, by3_ref)):
        y_from = (y + 4 - by) & 3
        kept = kept + bits(ref[rows:rows + 16, :].astype(f32)[0:1, :], y_from, y)
        sources_ref[pl.ds(pl.multiple_of(y_from * rows, rows), rows), :] = ref[0:rows, :]
    kept = jnp.sum(kept).astype(jnp.int32)

    def pick(number, found):
        pairs_ref[found] = number
        return found + ((kept >> number) & 1)

    found = lax.fori_loop(0, PAIRS_MAX, pick, 0)
    pairs_ref[PAIRS_MAX] = found
    source_squares_ref[...] = squares(own_ref[0:rows, :])
    squared = squares(targets_ref[...])
    target_squares_ref[...] = squared
    potential = potential_ref[pl.ds(pl.multiple_of(y * 8, 8), 8), :]
    bias = 0.5 * (potential - squared)
    half_step(pairs_ref, targets_ref, sources_ref, bias, False, out_ref, *scratch)


def half_step(pairs_ref, kept_ref, sum_ref, bias, kept_first, out_ref, acc_max, acc_sum, even, odd, offset=None):
    clear(acc_max, acc_sum)
    sweep(pairs_ref, pairs_ref[PAIRS_MAX], kept_ref, sum_ref, bias, acc_max, acc_sum, even, odd, kept_first)
    finish(sum_ref.shape[0] // BLOCK, acc_max, acc_sum, out_ref, offset)


def next_rows(pairs_ref, sources_ref, targets_ref, parts_ref, out_ref, *scratch):
    bias = half_bias(combined(parts_ref[...]))
    half_step(pairs_ref, targets_ref, sources_ref, bias, False, out_ref, *scratch)


def next_columns(pairs_ref, sources_ref, targets_ref, parts_ref, out_ref, *scratch):
    bias = half_bias(combined(parts_ref[...]))
    half_step(pairs_ref, sources_ref, targets_ref, bias, True, out_ref, *scratch)


def last_columns(pairs_ref, y_ref, sources_ref, targets_ref, source_squares_ref, target_squares_ref, parts_ref, out_ref, potential_ref, all_bias, *scratch):
    bias = half_bias(combined(parts_ref[...]))
    all_bias[...] = bias
    own = all_bias[pl.ds(pl.multiple_of(y_ref[0, 0] * 8, 8), 8), :]
    potential_ref[...] = source_squares_ref[...] + 2.0 * own
    offset = target_squares_ref[...] * (-LOG2E / EPS_REG)
    half_step(pairs_ref, sources_ref, targets_ref, bias, True, out_ref, *scratch, offset)


def last_potential(parts_ref, potential_ref):
    count = parts_ref.shape[0] // 4
    for y in range(4):
        lse = combined(parts_ref[y * count:(y + 1) * count])
        potential_ref[y * 8:(y + 1) * 8, :] = 2.0 * half_bias(lse)


SMEM = pl.BlockSpec(memory_space=pltpu.SMEM)
VMEM = pl.BlockSpec(memory_space=pltpu.VMEM)
PARAMS = pltpu.CompilerParams(vmem_limit_bytes=24 * 1024 * 1024)
WORK = [pltpu.VMEM((8, BLOCK), f32)] * 2 + [pltpu.VMEM((BLOCK, BLOCK), f32)] * 2


def spread(parts, axes):
    return lax.all_to_all(parts, axes, 0, 0, tiled=True)


def call(kernel, out_shape, smem, vmem, scratch, smem_outs=0):
    out_specs = jax.tree.map(lambda _: VMEM, out_shape)
    if smem_outs:
        out_specs = out_specs[:-smem_outs] + [SMEM] * smem_outs
    return pl.pallas_call(
        kernel,
        out_shape=out_shape,
        in_specs=[SMEM] * len(smem) + [VMEM] * len(vmem),
        out_specs=out_specs,
        scratch_shapes=scratch,
        compiler_params=PARAMS,
        cost_estimate=pl.CostEstimate(flops=1 << 30, bytes_accessed=1 << 22, transcendentals=1 << 20),
    )(*smem, *vmem)


def per_device(source_points, target_points, initial_potential, pair_list, pair_count):
    n_y, n_z = lax.axis_size("y"), lax.axis_size("z")
    n_rows = lax.axis_size(("x", "c", "y"))
    own = target_points.shape[0]
    src_rows = source_points.shape[0] // LANES
    tgt_rows = n_z * own // LANES
    y = lax.axis_index("y").astype(jnp.int32).reshape(1, 1)

    listed = jnp.pad(pair_list.reshape(1, PAIRS_MAX).astype(bf16), ((0, 15), (0, LANES - PAIRS_MAX)), constant_values=-1)
    sources = jnp.concatenate([source_points, listed], axis=0)
    by = [
        lax.ppermute(sources, "y", [(i, (i + k) % n_y) for i in range(n_y)]) for k in range(1, n_y)
    ]
    targets = spread(jnp.broadcast_to(target_points[None], (n_z, own, EMB)), "z").reshape(n_z * own, EMB)
    potential = initial_potential.reshape(n_y * tgt_rows, LANES)

    def shape(*dims):
        return jax.ShapeDtypeStruct(dims, f32)

    row_shape = shape(n_rows, n_y * src_rows, LANES)
    row_parts, sources, source_squares, target_squares, pairs = call(
        first_rows,
        [
            row_shape,
            jax.ShapeDtypeStruct((n_y * src_rows * LANES, EMB), bf16),
            shape(src_rows, LANES),
            shape(tgt_rows, LANES),
            jax.ShapeDtypeStruct((2 * PAIRS_MAX,), jnp.int32),
        ],
        (y,),
        (sources, *by, targets, potential),
        WORK,
        1,
    )
    for iteration in range(ITERS):
        if iteration > 0:
            row_parts = call(next_rows, row_shape, (pairs,), (sources, targets, col_parts), WORK)
        row_parts = spread(row_parts, ("x", "c", "y"))
        if iteration < ITERS - 1:
            col_parts = call(next_columns, shape(n_z, tgt_rows, LANES), (pairs,), (sources, targets, row_parts), WORK)
            col_parts = spread(col_parts, "z")
        else:
            col_parts, source_potential = call(
                last_columns,
                [shape(n_y * n_z, tgt_rows, LANES), shape(src_rows, LANES)],
                (pairs, y),
                (sources, targets, source_squares, target_squares, row_parts),
                [pltpu.VMEM((n_y * src_rows, LANES), f32)] + WORK,
            )
            col_parts = spread(col_parts, ("y", "z"))
    target_potential = call(last_potential, shape(n_y * tgt_rows, LANES), (), (col_parts,), [])
    return source_potential.reshape(-1), target_potential.reshape(-1)


def solution(mesh):
    fine = Mesh(mesh.devices.reshape(4, 8, 4, 2), ("y", "z", "x", "c"))
    src, tgt = ("y", "z"), ("x", "c")
    placed = (P(src, None), P(tgt + src, None), P(tgt), P(src, tgt, None), P(src, tgt))
    return jax.shard_map(
        per_device, mesh=fine, in_specs=placed, out_specs=(P(src), P(tgt)), check_vma=False
    )
```

time: 115 us -> 103 us (0.90)
  blocking collectives: 85 us -> 58.7 us
  waiting for transfers between devices: 3.99 us -> 12.9 us
  starting transfers between devices: 6.87 us -> 13.4 us
    all_to_all x5 -> x4, blocking collectives: 85 us -> 58.7 us  [spread(): return lax.all_to_all(parts, axes, 0, 0, tiled=True)]
    ppermute x4 -> x3, waiting for transfers between devices: 3.99 us -> 12.9 us  [per_device(): lax.ppermute(sources, 'y', [(i, (i + k) % n_y) for i in range(n_y)])]
    all_to_all x0 -> x1, starting transfers between devices: none -> 8.7 us  [spread(): return lax.all_to_all(parts, axes, 0, 0, tiled=True)]
    ppermute x4 -> x3, starting transfers between devices: 6.87 us -> 4.69 us  [per_device(): lax.ppermute(sources, 'y', [(i, (i + k) % n_y) for i in range(n_y)])]
    pallas_call x8 -> x5, Pallas kernels: 15.2 us -> 15 us  [call(): pl.pallas_call(kernel, out_shape=out_shape, in_specs=[SMEM] * len(smem) +...]
  transfers between devices with their start and end apart: 4 -> 4, of which waited for: 2 -> 2; matrix products, arithmetic and copies ran while one was open for 0% -> 0% of each run, Pallas kernels for 4% -> 0%
where the time goes in v4:
time: 103 us; the launch traced here: 102 us
  blocking collectives  58.7 us (57%)
  Pallas kernels  15 us (15%)
  starting transfers between devices  13.4 us (13%)
  waiting for transfers between devices  12.9 us (13%)
  local copies, waits for them, and re-layouts  1.5 us (1%)
    all_to_all x4, blocking collectives, spread(): return lax.all_to_all(parts, axes, 0, 0, tiled=True)  58.7 us
    pallas_call x5, Pallas kernels, call(): pl.pallas_call(kernel, out_shape=out_shape, in_specs=[SMEM] * len(smem) +...  15 us
    ppermute x3, waiting for transfers between devices, per_device(): lax.ppermute(sources, 'y', [(i, (i + k) % n_y) for i in range(n_y)])  12.9 us
    all_to_all x1, starting transfers between devices, spread(): return lax.all_to_all(parts, axes, 0, 0, tiled=True)  8.7 us
    ppermute x3, starting transfers between devices, per_device(): lax.ppermute(sources, 'y', [(i, (i + k) % n_y) for i in range(n_y)])  4.69 us
  transfers between devices with their start and end apart: 4, of which 2 were waited for; matrix products, arithmetic and copies ran while one was open for 0% of the time, Pallas kernels for 0%

profile of v4, /device:TPU:32, one launch (start us, length us, event | category | flops | bytes accessed | tf_op | source)
XLA Modules:
  0.0 102.2 jit_solution(2879888788724075752)
XLA Ops:
  0.6 1.5 %broadcast_in_dim.2 = bf16[8,128,128]{2,1,0:T(8,128)(2,1)} broadcast(bf16[128,128]{1,0:T(8,128)(2,1)} %param.6), dimensions={1,2} | broadcast | bytes 294912 | tf_op jit(solution)/shard_map/broadcast_in_dim | solution.py:303
  2.1 0.0 copy-start.2
  2.1 0.0 copy-start.1
  2.1 8.7 %all-to-all-start = ((bf16[8,128,128]{2,1,0:T(8,128)(2,1)}), bf16[8,128,128]{2,1,0:T(8,128)(2,1)S(1)}, u32[]{:S(2)}, u32[]{:S(2)}) async-start(bf16[8,128,128]{2,1,0:T(8,128)(2,1)} %broadcast_in_dim.2), calls=%async_computation | async-start | bytes 524288 | tf_op jit(solution)/shard_map/all_to_all | solution.py:272
  10.8 0.0 copy-done.2
  10.8 0.0 copy-done.1
  10.8 0.0 copy-start
  10.9 3.1 %collective-permute-start.2 = (bf16[1040,128]{1,0:T(8,128)(2,1)S(1)}, bf16[1040,128]{1,0:T(8,128)(2,1)S(1)}, u32[]{:S(2)}, u32[]{:S(2)}) collective-permute-start(bf16[1040,128]{1,0:T(8,128)(2,1)S(1)} %fusion.1.own_ref), channel_id=1, source_target_pairs={{0,192},{64,0},{128,64},{192,128},{1,193},{65,1},{129,65},{193,129... | collective-permute-start | bytes 798728 | tf_op jit(solution)/shard_map/ppermute | solution.py:301
  14.0 0.6 collective-permute-start.1
  14.6 1.0 collective-permute-start
  15.6 9.2 %collective-permute-done.2.by3_ref = bf16[1040,128]{1,0:T(8,128)(2,1)S(1)} collective-permute-done((bf16[1040,128]{1,0:T(8,128)(2,1)S(1)}, bf16[1040,128]{1,0:T(8,128)(2,1)S(1)}, u32[]{:S(2)}, u32[]{:S(2)}) %collective-permute-start.2) | collective-permute-done | bytes 266272 | tf_op jit(solution)/shard_map/ppermute | solution.py:301
  24.8 0.0 collective-permute-done.1.by2_ref
  24.8 3.7 %collective-permute-done.by1_ref = bf16[1040,128]{1,0:T(8,128)(2,1)S(1)} collective-permute-done((bf16[1040,128]{1,0:T(8,128)(2,1)S(1)}, bf16[1040,128]{1,0:T(8,128)(2,1)S(1)}, u32[]{:S(2)}, u32[]{:S(2)}) %collective-permute-start) | collective-permute-done | bytes 266272 | tf_op jit(solution)/shard_map/ppermute | solution.py:301
  28.5 0.0 all-to-all-done
  28.5 0.0 copy-done
  28.5 3.8 %shard_map.59 = (f32[32,32,128]{2,1,0:T(8,128)S(1)}, bf16[4096,128]{1,0:T(8,128)(2,1)S(1)}, f32[8,128]{1,0:T(8,128)S(1)}, f32[8,128]{1,0:T(8,128)S(1)}, s32[32]{0:T(128)S(1)}) custom-call(s32[1,1]{1,0:T(1,128)} %bitcast.y_ref, bf16[1040,128]{1,0:T(8,128)(2,1)S(1)} %fusion.1.own_ref, bf16[1040,128]{1,0:T(8,128)(2,1)S(1)} %collective-permute-done.by1_ref, ...), custom_call_target="tpu_custom_call" | custom-call | flops 1073741824 | bytes 4194304 | tf_op jit(solution)/shard_map/pallas_call | solution.py:279
  32.3 16.4 %all_to_all.25.parts_ref = f32[32,32,128]{2,1,0:T(8,128)S(1)} all-to-all(f32[32,32,128]{2,1,0:T(8,128)S(1)} %get-tuple-element.13), channel_id=1, replica_groups=mesh['y'=4,'z'=8,'x'=4,'c'=2] {'x','c','y'}, dimensions={0} | all-to-all | bytes 1048576 | tf_op jit(solution)/shard_map/all_to_all | solution.py:272
  48.7 3.4 %shard_map.60 = f32[8,8,128]{2,1,0:T(8,128)S(1)} custom-call(s32[32]{0:T(128)S(1)} %get-tuple-element.9.pairs_ref, bf16[4096,128]{1,0:T(8,128)(2,1)S(1)} %get-tuple-element.10.sources_ref, bf16[1024,128]{1,0:T(8,128)(2,1)S(1)} %bitcast.8, f32[32,32,128]{2,1,0:T(8,128)S(1)} %all_to_all.25.parts_ref), custom_call_target="tpu_custom_call" | custom-call | flops 1073741824 | bytes 4194304 | tf_op jit(solution)/shard_map/pallas_call | solution.py:279
  52.1 12.1 %all_to_all.26.parts_ref = f32[8,8,128]{2,1,0:T(8,128)S(1)} all-to-all(f32[8,8,128]{2,1,0:T(8,128)S(1)} %shard_map.60), channel_id=1, replica_groups=mesh['y'=4,'z'=8,'x'=4,'c'=2] {'z'}, dimensions={0} | all-to-all | bytes 65536 | tf_op jit(solution)/shard_map/all_to_all | solution.py:272
  64.2 3.3 %shard_map.61 = f32[32,32,128]{2,1,0:T(8,128)S(1)} custom-call(s32[32]{0:T(128)S(1)} %get-tuple-element.9.pairs_ref, bf16[4096,128]{1,0:T(8,128)(2,1)S(1)} %get-tuple-element.10.sources_ref, bf16[1024,128]{1,0:T(8,128)(2,1)S(1)} %bitcast.9, f32[8,8,128]{2,1,0:T(8,128)S(1)} %all_to_all.26.parts_ref), custom_call_target="tpu_custom_call" | custom-call | flops 1073741824 | bytes 4194304 | tf_op jit(solution)/shard_map/pallas_call | solution.py:279
  67.5 15.8 %all_to_all.27.parts_ref = f32[32,32,128]{2,1,0:T(8,128)S(1)} all-to-all(f32[32,32,128]{2,1,0:T(8,128)S(1)} %shard_map.61), channel_id=1, replica_groups=mesh['y'=4,'z'=8,'x'=4,'c'=2] {'x','c','y'}, dimensions={0} | all-to-all | bytes 1048576 | tf_op jit(solution)/shard_map/all_to_all | solution.py:272
  83.4 3.8 %shard_map.62 = (f32[32,8,128]{2,1,0:T(8,128)S(1)}, f32[8,128]{1,0:T(8,128)}) custom-call(s32[32]{0:T(128)S(1)} %get-tuple-element.9.pairs_ref, s32[1,1]{1,0:T(1,128)} %bitcast.y_ref, bf16[4096,128]{1,0:T(8,128)(2,1)S(1)} %get-tuple-element.10.sources_ref, bf16[1024,128]{1,0:T(8,128)(2,1)S(1)} %bitcast.10, ...), custom_call_target="tpu_custom_call" | custom-call | flops 1073741824 | bytes 4194304 | tf_op jit(solution)/shard_map/pallas_call | solution.py:279
  87.2 14.3 %all_to_all.28.parts_ref = f32[32,8,128]{2,1,0:T(8,128)S(1)} all-to-all(f32[32,8,128]{2,1,0:T(8,128)S(1)} %get-tuple-element.15), channel_id=1, replica_groups=mesh['y'=4,'z'=8,'x'=4,'c'=2] {'y','z'}, dimensions={0} | all-to-all | bytes 262144 | tf_op jit(solution)/shard_map/all_to_all | solution.py:272
  101.5 0.6 shard_map.63
  (2 shorter events, 0.0 us)
Async XLA Ops:
  2.1 8.7 %copy-start.2 = (s32[1,1,16]{2,1,0:T(1,128)S(1)}, s32[1,1,16]{2,1,0:T(1,128)}, u32[]{:S(2)}) copy-start(s32[1,1,16]{2,1,0:T(1,128)} %param.8) | copy-start | bytes 196
  2.1 8.7 %copy-start.1 = (bf16[1024,128]{1,0:T(8,128)(2,1)S(1)}, bf16[1024,128]{1,0:T(8,128)(2,1)}, u32[]{:S(2)}) copy-start(bf16[1024,128]{1,0:T(8,128)(2,1)} %param.5) | copy-start | bytes 786436
  2.1 26.4 %all-to-all-start = ((bf16[8,128,128]{2,1,0:T(8,128)(2,1)}), bf16[8,128,128]{2,1,0:T(8,128)(2,1)S(1)}, u32[]{:S(2)}, u32[]{:S(2)}) async-start(bf16[8,128,128]{2,1,0:T(8,128)(2,1)} %broadcast_in_dim.2), calls=%async_computation | async-start | bytes 524288 | tf_op jit(solution)/shard_map/all_to_all | solution.py:272
  10.8 17.6 %copy-start = (f32[4096]{0:T(1024)S(1)}, f32[4096]{0:T(1024)}, u32[]{:S(2)}) copy-start(f32[4096]{0:T(1024)} %param.7) | copy-start | bytes 49156
  10.9 13.9 %collective-permute-start.2 = (bf16[1040,128]{1,0:T(8,128)(2,1)S(1)}, bf16[1040,128]{1,0:T(8,128)(2,1)S(1)}, u32[]{:S(2)}, u32[]{:S(2)}) collective-permute-start(bf16[1040,128]{1,0:T(8,128)(2,1)S(1)} %fusion.1.own_ref), channel_id=1, source_target_pairs={{0,192},{64,0},{128,64},{192,128},{1,193},{65,1},{129,65},{193,129... | collective-permute-start | bytes 798728 | tf_op jit(solution)/shard_map/ppermute | solution.py:301
  14.0 10.8 %collective-permute-start.1 = (bf16[1040,128]{1,0:T(8,128)(2,1)S(1)}, bf16[1040,128]{1,0:T(8,128)(2,1)S(1)}, u32[]{:S(2)}, u32[]{:S(2)}) collective-permute-start(bf16[1040,128]{1,0:T(8,128)(2,1)S(1)} %fusion.1.own_ref), channel_id=1, source_target_pairs={{0,128},{64,192},{128,0},{192,64},{1,129},{65,193},{129,1},{193,65... | collective-permute-start | bytes 798728 | tf_op jit(solution)/shard_map/ppermute | solution.py:301
  14.6 13.9 %collective-permute-start = (bf16[1040,128]{1,0:T(8,128)(2,1)S(1)}, bf16[1040,128]{1,0:T(8,128)(2,1)S(1)}, u32[]{:S(2)}, u32[]{:S(2)}) collective-permute-start(bf16[1040,128]{1,0:T(8,128)(2,1)S(1)} %fusion.1.own_ref), channel_id=1, source_target_pairs={{0,64},{64,128},{128,192},{192,0},{1,65},{65,129},{129,193},{193,1... | collective-permute-start | bytes 798728 | tf_op jit(solution)/shard_map/ppermute | solution.py:301

commit v5 on v4

--- a/solution.py
+++ b/solution.py
@@ -12,8 +12,6 @@
 BLOCK = 512
 LANES = 128
 EMB = 128
-SRC_BLOCKS = 8
-TGT_BLOCKS = 2
 PAIRS_MAX = 16
 ITERS = 2
 NEG_START = -1e30
@@ -94,7 +92,7 @@
     def where(number):
         real = number < count
         pair = jnp.where(real, pairs_ref[jnp.minimum(number, PAIRS_MAX - 1)], 0)
-        first, second = pair >> 1, pair & 1
+        first, second = pair >> 2, pair & 3
         return (first, second) if kept_first else (second, first)
 
     def push(number, parity):
@@ -187,33 +185,28 @@
         pltpu.matmul_pop(mxus[m][0])
 
 
-def finish(blocks, acc_max, acc_sum, out_ref, offset):
+def finished(acc_max, acc_sum):
     total = acc_sum[...]
     lse = jnp.where(total > 0, acc_max[...] * SCALE + jnp.log(total) * LOG2E, NEG_START)
-    dense = jnp.concatenate(
-        [lse[b:b + 1, q * LANES:(q + 1) * LANES] for b in range(blocks) for q in range(GROUPS)], axis=0
-    )
-    if offset is not None:
-        dense = dense + offset
-    for k in range(out_ref.shape[0]):
-        out_ref[k] = dense
-
-
-def bits(list_row, y_from, y):
+    return jnp.concatenate([lse[b:b + 1, q * LANES:(q + 1) * LANES] for b in range(4) for q in range(GROUPS)], axis=0)
+
+
+def bits(list_row, y_from, c_from, y, c):
     pair = list_row.astype(jnp.int32)
-    number = y_from * 4 + ((pair >> 3) << 1) + (pair & 1)
-    mine = (pair >= 0) & (((pair >> 1) & 3) == y)
-    return jnp.where(mine, jnp.left_shift(jnp.ones_like(number), jnp.where(mine, number, 0)), 0).astype(f32)
-
-
-def first_rows(y_ref, own_ref, by1_ref, by2_ref, by3_ref, targets_ref, potential_ref, out_ref, sources_ref, source_squares_ref, target_squares_ref, pairs_ref, *scratch):
-    y = y_ref[0, 0]
-    rows = targets_ref.shape[0]
+    number = y_from * 4 + c_from * 2 + (pair & 1)
+    mine = (pair >> 3 == c) & (((pair >> 1) & 3) == y)
+    return jnp.where(mine, jnp.left_shift(jnp.ones_like(pair), number), 0).astype(f32)
+
+
+def first_rows(place_ref, own_ref, by1_ref, by2_ref, by3_ref, targets_ref, shared_ref, out_ref, sources_ref, source_squares_ref, target_squares_ref, pairs_ref, *scratch):
+    y, c = place_ref[0], place_ref[1]
     kept = jnp.zeros((1, LANES), f32)
     for by, ref in enumerate((own_ref, by1_ref, by2_ref, by3_ref)):
         y_from = (y + 4 - by) & 3
-        kept = kept + bits(ref[rows:rows + 16, :].astype(f32)[0:1, :], y_from, y)
-        sources_ref[pl.ds(pl.multiple_of(y_from * rows, rows), rows), :] = ref[0:rows, :]
+        lists = ref[BLOCK:BLOCK + 16, :].astype(f32)
+        for c_from in range(2):
+            kept = kept + bits(lists[c_from:c_from + 1, :], y_from, c_from, y, c)
+        sources_ref[pl.ds(pl.multiple_of(y_from * BLOCK, BLOCK), BLOCK), :] = ref[0:BLOCK, :]
     kept = jnp.sum(kept).astype(jnp.int32)
 
     def pick(number, found):
@@ -222,37 +215,56 @@
 
     found = lax.fori_loop(0, PAIRS_MAX, pick, 0)
     pairs_ref[PAIRS_MAX] = found
-    source_squares_ref[...] = squares(own_ref[0:rows, :])
+    source_squares_ref[...] = squares(own_ref[0:BLOCK, :])
     squared = squares(targets_ref[...])
     target_squares_ref[...] = squared
-    potential = potential_ref[pl.ds(pl.multiple_of(y * 8, 8), 8), :]
+    rows = pl.ds(pl.multiple_of(y * 8, 8), 8)
+    potential = jnp.concatenate([shared_ref[0, rows, :], shared_ref[1, rows, :]], axis=0)
     bias = 0.5 * (potential - squared)
-    half_step(pairs_ref, targets_ref, sources_ref, bias, False, out_ref, *scratch)
-
-
-def half_step(pairs_ref, kept_ref, sum_ref, bias, kept_first, out_ref, acc_max, acc_sum, even, odd, offset=None):
+    half_step(pairs_ref, targets_ref, sources_ref, bias, False, *scratch)
+    spread_out(out_ref, scratch)
+
+
+def half_step(pairs_ref, kept_ref, sum_ref, bias, kept_first, acc_max, acc_sum, even, odd):
     clear(acc_max, acc_sum)
     sweep(pairs_ref, pairs_ref[PAIRS_MAX], kept_ref, sum_ref, bias, acc_max, acc_sum, even, odd, kept_first)
-    finish(sum_ref.shape[0] // BLOCK, acc_max, acc_sum, out_ref, offset)
+
+
+def spread_out(out_ref, scratch):
+    dense = finished(scratch[0], scratch[1])
+    for k in range(out_ref.shape[0]):
+        out_ref[k] = dense
 
 
 def next_rows(pairs_ref, sources_ref, targets_ref, parts_ref, out_ref, *scratch):
     bias = half_bias(combined(parts_ref[...]))
-    half_step(pairs_ref, targets_ref, sources_ref, bias, False, out_ref, *scratch)
+    half_step(pairs_ref, targets_ref, sources_ref, bias, False, *scratch)
+    spread_out(out_ref, scratch)
 
 
 def next_columns(pairs_ref, sources_ref, targets_ref, parts_ref, out_ref, *scratch):
     bias = half_bias(combined(parts_ref[...]))
-    half_step(pairs_ref, sources_ref, targets_ref, bias, True, out_ref, *scratch)
-
-
-def last_columns(pairs_ref, y_ref, sources_ref, targets_ref, source_squares_ref, target_squares_ref, parts_ref, out_ref, potential_ref, all_bias, *scratch):
+    half_step(pairs_ref, sources_ref, targets_ref, bias, True, *scratch)
+    spread_out(out_ref, scratch)
+
+
+def last_columns(pairs_ref, place_ref, sources_ref, targets_ref, source_squares_ref, target_squares_ref, parts_ref, out_ref, all_bias, *scratch):
     bias = half_bias(combined(parts_ref[...]))
     all_bias[...] = bias
-    own = all_bias[pl.ds(pl.multiple_of(y_ref[0, 0] * 8, 8), 8), :]
-    potential_ref[...] = source_squares_ref[...] + 2.0 * own
-    offset = target_squares_ref[...] * (-LOG2E / EPS_REG)
-    half_step(pairs_ref, sources_ref, targets_ref, bias, True, out_ref, *scratch, offset)
+    half_step(pairs_ref, sources_ref, targets_ref, bias, True, *scratch)
+    out_ref[0:16, :] = finished(scratch[0], scratch[1]) - target_squares_ref[...] * (LOG2E / EPS_REG)
+    own = all_bias[pl.ds(place_ref[0] * GROUPS, GROUPS), :]
+    out_ref[16:16 + GROUPS, :] = source_squares_ref[...] + 2.0 * own
+    out_ref[16 + GROUPS:24, :] = jnp.zeros((8 - GROUPS, LANES), f32)
+
+
+def both_cores(place_ref, parts_ref, out_ref, potential_ref):
+    rows = pl.ds(pl.multiple_of(place_ref[1] * 8, 8), 8)
+    lse = combined(jnp.stack([parts_ref[0, rows, :], parts_ref[1, rows, :]]))
+    for k in range(out_ref.shape[0]):
+        out_ref[k] = lse
+    for b in range(2):
+        potential_ref[b * GROUPS:(b + 1) * GROUPS, :] = parts_ref[b, 16:16 + GROUPS, :]
 
 
 def last_potential(parts_ref, potential_ref):
@@ -289,54 +301,61 @@
 
 def per_device(source_points, target_points, initial_potential, pair_list, pair_count):
     n_y, n_z = lax.axis_size("y"), lax.axis_size("z")
-    n_rows = lax.axis_size(("x", "c", "y"))
     own = target_points.shape[0]
-    src_rows = source_points.shape[0] // LANES
     tgt_rows = n_z * own // LANES
-    y = lax.axis_index("y").astype(jnp.int32).reshape(1, 1)
-
-    listed = jnp.pad(pair_list.reshape(1, PAIRS_MAX).astype(bf16), ((0, 15), (0, LANES - PAIRS_MAX)), constant_values=-1)
-    sources = jnp.concatenate([source_points, listed], axis=0)
+    y, c = lax.axis_index("y"), lax.axis_index("c")
+    place = jnp.stack([y, c]).astype(jnp.int32)
+
+    def shape(*dims):
+        return jax.ShapeDtypeStruct(dims, f32)
+
+    listed = jnp.pad(pair_list.reshape(1, PAIRS_MAX).astype(f32), ((0, 7), (0, LANES - PAIRS_MAX)), constant_values=-1)
+    shared = jnp.concatenate([initial_potential.reshape(n_y * tgt_rows, LANES), listed], axis=0)
+    shared = lax.all_gather(shared, "c")
+    lists = jnp.pad(shared[:, n_y * tgt_rows, :].astype(bf16), ((0, 14), (0, 0)), constant_values=-1)
+    sources = jnp.concatenate([lax.dynamic_slice_in_dim(source_points, c * BLOCK, BLOCK, 0), lists], axis=0)
     by = [
         lax.ppermute(sources, "y", [(i, (i + k) % n_y) for i in range(n_y)]) for k in range(1, n_y)
     ]
     targets = spread(jnp.broadcast_to(target_points[None], (n_z, own, EMB)), "z").reshape(n_z * own, EMB)
-    potential = initial_potential.reshape(n_y * tgt_rows, LANES)
-
-    def shape(*dims):
-        return jax.ShapeDtypeStruct(dims, f32)
-
-    row_shape = shape(n_rows, n_y * src_rows, LANES)
+    targets = lax.all_gather(targets, "c", axis=0, tiled=True)
+    row_shape = shape(16, 16, LANES)
     row_parts, sources, source_squares, target_squares, pairs = call(
         first_rows,
         [
             row_shape,
-            jax.ShapeDtypeStruct((n_y * src_rows * LANES, EMB), bf16),
-            shape(src_rows, LANES),
-            shape(tgt_rows, LANES),
+            jax.ShapeDtypeStruct((n_y * BLOCK, EMB), bf16),
+            shape(GROUPS, LANES),
+            shape(2 * tgt_rows, LANES),
             jax.ShapeDtypeStruct((2 * PAIRS_MAX,), jnp.int32),
         ],
-        (y,),
-        (sources, *by, targets, potential),
+        (place,),
+        (sources, *by, targets, shared),
         WORK,
         1,
     )
     for iteration in range(ITERS):
         if iteration > 0:
             row_parts = call(next_rows, row_shape, (pairs,), (sources, targets, col_parts), WORK)
-        row_parts = spread(row_parts, ("x", "c", "y"))
+        row_parts = spread(row_parts, ("y", "x"))
         if iteration < ITERS - 1:
-            col_parts = call(next_columns, shape(n_z, tgt_rows, LANES), (pairs,), (sources, targets, row_parts), WORK)
-            col_parts = spread(col_parts, "z")
-        else:
-            col_parts, source_potential = call(
-                last_columns,
-                [shape(n_y * n_z, tgt_rows, LANES), shape(src_rows, LANES)],
-                (pairs, y),
-                (sources, targets, source_squares, target_squares, row_parts),
-                [pltpu.VMEM((n_y * src_rows, LANES), f32)] + WORK,
-            )
-            col_parts = spread(col_parts, ("y", "z"))
+            col_parts = call(next_columns, row_shape, (pairs,), (sources, targets, row_parts), WORK)
+            col_parts = spread(col_parts, ("z", "c"))
+    parts = call(
+        last_columns,
+        shape(24, LANES),
+        (pairs, place),
+        (sources, targets, source_squares, target_squares, row_parts),
+        [pltpu.VMEM((16, LANES), f32)] + WORK,
+    )
+    col_parts, source_potential = call(
+        both_cores,
+        [shape(n_y * n_z, tgt_rows, LANES), shape(2 * GROUPS, LANES)],
+        (place,),
+        (lax.all_gather(parts, "c"),),
+        [],
+    )
+    col_parts = spread(col_parts, ("y", "z"))
     target_potential = call(last_potential, shape(n_y * tgt_rows, LANES), (), (col_parts,), [])
     return source_potential.reshape(-1), target_potential.reshape(-1)
 

time: 103 us -> 98 us (0.951)
  waiting for transfers between devices: 12.9 us -> 5.93 us
  blocking collectives: 58.7 us -> 63.1 us
  Pallas kernels: 15 us -> 12.5 us
    ppermute x3, waiting for transfers between devices: 12.9 us -> 2.84 us  [per_device(): lax.ppermute(sources, 'y', [(i, (i + k) % n_y) for i in range(n_y)])]
    all_gather x0 -> x3, blocking collectives: none -> 5.83 us  [the longest x1 2.17 us: per_device(): targets = lax.all_gather(targets, 'c', axis=0, tiled=True)]
    all_to_all x1, waiting for transfers between devices: 0.01 us -> 3.09 us  [spread(): return lax.all_to_all(parts, axes, 0, 0, tiled=True)]
    pallas_call x5 -> x6, Pallas kernels: 15 us -> 12.5 us  [call(): pl.pallas_call(kernel, out_shape=out_shape, in_specs=[SMEM] * len(smem) +...]
    all_to_all x4, blocking collectives: 58.7 us -> 57.3 us  [spread(): return lax.all_to_all(parts, axes, 0, 0, tiled=True)]
  transfers between devices with their start and end apart: 4 -> 4, of which waited for: 2 -> 3; matrix products, arithmetic and copies ran while one was open for 0% -> 0% of each run, Pallas kernels for 0% -> 0%
where the time goes in v5:
time: 98 us; the launch traced here: 97.9 us
  blocking collectives  63.1 us (64%)
  starting transfers between devices  13.4 us (14%)
  Pallas kernels  12.5 us (13%)
  waiting for transfers between devices  5.93 us (6%)
  local copies, waits for them, and re-layouts  2.23 us (2%)
    all_to_all x4, blocking collectives, spread(): return lax.all_to_all(parts, axes, 0, 0, tiled=True)  57.3 us
    pallas_call x6, Pallas kernels, call(): pl.pallas_call(kernel, out_shape=out_shape, in_specs=[SMEM] * len(smem) +...  12.5 us
    all_to_all x1, starting transfers between devices, spread(): return lax.all_to_all(parts, axes, 0, 0, tiled=True)  8.7 us
    ppermute x3, starting transfers between devices, per_device(): lax.ppermute(sources, 'y', [(i, (i + k) % n_y) for i in range(n_y)])  4.69 us
    all_to_all x1, waiting for transfers between devices, spread(): return lax.all_to_all(parts, axes, 0, 0, tiled=True)  3.09 us
    ppermute x3, waiting for transfers between devices, per_device(): lax.ppermute(sources, 'y', [(i, (i + k) % n_y) for i in range(n_y)])  2.84 us
    all_gather x1, blocking collectives, per_device(): targets = lax.all_gather(targets, 'c', axis=0, tiled=True)  2.17 us
  transfers between devices with their start and end apart: 4, of which 3 were waited for; matrix products, arithmetic and copies ran while one was open for 0% of the time, Pallas kernels for 0%

profile of v5, /device:TPU:32, one launch (start us, length us, event | category | flops | bytes accessed | tf_op | source)
XLA Modules:
  0.0 97.9 jit_solution(3022571068290490956)
XLA Ops:
  0.6 0.0 copy-start
  0.6 1.5 %broadcast_in_dim.2 = bf16[8,128,128]{2,1,0:T(8,128)(2,1)} broadcast(bf16[128,128]{1,0:T(8,128)(2,1)} %param.6), dimensions={1,2} | broadcast | bytes 294912 | tf_op jit(solution)/shard_map/broadcast_in_dim | solution.py:320
  2.2 0.0 copy-start.1
  2.2 8.7 %all-to-all-start = ((bf16[8,128,128]{2,1,0:T(8,128)(2,1)}), bf16[8,128,128]{2,1,0:T(8,128)(2,1)S(1)}, u32[]{:S(2)}, u32[]{:S(2)}) async-start(bf16[8,128,128]{2,1,0:T(8,128)(2,1)} %broadcast_in_dim.2), calls=%async_computation | async-start | bytes 524288 | tf_op jit(solution)/shard_map/all_to_all | solution.py:284
  10.9 0.0 copy-start.2
  10.9 0.7 copy-done.2
  11.5 0.0 copy-done.1
  11.6 1.8 %all-gather = f32[80,128]{1,0:T(8,128)S(1)} all-gather(f32[40,128]{1,0:T(8,128)S(1)} %select_maximum_fusion), channel_id=2, replica_groups=mesh['y'=4,'z'=8,'x'=4,'c'=2] {'c'}, dimensions={0}, use_global_device_ids=true | all-gather | bytes 61440 | tf_op jit(solution)/shard_map/all_gather | solution.py:314
  13.4 0.0 copy-done
  13.4 3.1 %collective-permute-start.2 = (bf16[528,128]{1,0:T(8,128)(2,1)S(1)}, bf16[528,128]{1,0:T(8,128)(2,1)S(1)}, u32[]{:S(2)}, u32[]{:S(2)}) collective-permute-start(bf16[528,128]{1,0:T(8,128)(2,1)S(1)} %fusion.1.own_ref), channel_id=1, source_target_pairs={{0,192},{64,0},{128,64},{192,128},{1,193},{65,1},{129,65},{193,129... | collective-permute-start | bytes 405512 | tf_op jit(solution)/shard_map/ppermute | solution.py:318
  16.5 0.6 collective-permute-start.1
  17.2 1.0 collective-permute-start
  18.1 0.1 pad_add_fusion.place_ref
  18.2 3.1 %all-to-all-done = bf16[8,128,128]{2,1,0:T(8,128)(2,1)S(1)} async-done(((bf16[8,128,128]{2,1,0:T(8,128)(2,1)}), bf16[8,128,128]{2,1,0:T(8,128)(2,1)S(1)}, u32[]{:S(2)}, u32[]{:S(2)}) %all-to-all-start) | async-done | bytes 262176 | tf_op jit(solution)/shard_map/all_to_all | solution.py:284
  21.3 2.2 %all_gather.17.targets_ref = bf16[2048,128]{1,0:T(8,128)(2,1)S(1)} all-gather(bf16[1024,128]{1,0:T(8,128)(2,1)S(1)} %bitcast.16), channel_id=1, replica_groups=mesh['y'=4,'z'=8,'x'=4,'c'=2] {'c'}, dimensions={0}, use_global_device_ids=true | all-gather | bytes 786432 | tf_op jit(solution)/shard_map/all_gather | solution.py:321
  23.5 0.0 collective-permute-done.2.by3_ref
  23.5 1.1 %collective-permute-done.1.by2_ref = bf16[528,128]{1,0:T(8,128)(2,1)S(1)} collective-permute-done((bf16[528,128]{1,0:T(8,128)(2,1)S(1)}, bf16[528,128]{1,0:T(8,128)(2,1)S(1)}, u32[]{:S(2)}, u32[]{:S(2)}) %collective-permute-start.1) | collective-permute-done | bytes 135200 | tf_op jit(solution)/shard_map/ppermute | solution.py:318
  24.5 1.8 %collective-permute-done.by1_ref = bf16[528,128]{1,0:T(8,128)(2,1)S(1)} collective-permute-done((bf16[528,128]{1,0:T(8,128)(2,1)S(1)}, bf16[528,128]{1,0:T(8,128)(2,1)S(1)}, u32[]{:S(2)}, u32[]{:S(2)}) %collective-permute-start) | collective-permute-done | bytes 135200 | tf_op jit(solution)/shard_map/ppermute | solution.py:318
  26.3 3.5 %shard_map.59 = (f32[16,16,128]{2,1,0:T(8,128)S(1)}, bf16[2048,128]{1,0:T(8,128)(2,1)S(1)}, f32[4,128]{1,0:T(4,128)S(1)}, f32[16,128]{1,0:T(8,128)S(1)}, s32[32]{0:T(128)S(1)}) custom-call(s32[2]{0:T(128)S(1)} %pad_add_fusion.place_ref, bf16[528,128]{1,0:T(8,128)(2,1)S(1)} %fusion.1.own_ref, bf16[528,128]{1,0:T(8,128)(2,1)S(1)} %collective-permute-done.by1_ref, ...), custom_call_target="tpu_custom_call" | custom-call | flops 1073741824 | bytes 4194304 | tf_op jit(solution)/shard_map/pallas_call | solution.py:291
  29.8 12.9 %all_to_all.25.parts_ref = f32[16,16,128]{2,1,0:T(8,128)S(1)} all-to-all(f32[16,16,128]{2,1,0:T(8,128)S(1)} %get-tuple-element.13), channel_id=1, replica_groups=mesh['y'=4,'z'=8,'x'=4,'c'=2] {'y','x'}, dimensions={0} | all-to-all | bytes 262144 | tf_op jit(solution)/shard_map/all_to_all | solution.py:284
  42.7 2.4 %shard_map.60 = f32[16,16,128]{2,1,0:T(8,128)S(1)} custom-call(s32[32]{0:T(128)S(1)} %get-tuple-element.9.pairs_ref, bf16[2048,128]{1,0:T(8,128)(2,1)S(1)} %get-tuple-element.10.sources_ref, bf16[2048,128]{1,0:T(8,128)(2,1)S(1)} %all_gather.17.targets_ref, f32[16,16,128]{2,1,0:T(8,128)S(1)} %all_to_all.25.parts_ref), custom_call_target="tpu_custom_call" | custom-call | flops 1073741824 | bytes 4194304 | tf_op jit(solution)/shard_map/pallas_call | solution.py:291
  45.1 14.7 %all_to_all.26.parts_ref = f32[16,16,128]{2,1,0:T(8,128)S(1)} all-to-all(f32[16,16,128]{2,1,0:T(8,128)S(1)} %shard_map.60), channel_id=1, replica_groups=mesh['y'=4,'z'=8,'x'=4,'c'=2] {'z','c'}, dimensions={0} | all-to-all | bytes 262144 | tf_op jit(solution)/shard_map/all_to_all | solution.py:284
  59.8 2.4 %shard_map.61 = f32[16,16,128]{2,1,0:T(8,128)S(1)} custom-call(s32[32]{0:T(128)S(1)} %get-tuple-element.9.pairs_ref, bf16[2048,128]{1,0:T(8,128)(2,1)S(1)} %get-tuple-element.10.sources_ref, bf16[2048,128]{1,0:T(8,128)(2,1)S(1)} %all_gather.17.targets_ref, f32[16,16,128]{2,1,0:T(8,128)S(1)} %all_to_all.26.parts_ref), custom_call_target="tpu_custom_call" | custom-call | flops 1073741824 | bytes 4194304 | tf_op jit(solution)/shard_map/pallas_call | solution.py:291
  62.2 12.5 %all_to_all.27.parts_ref = f32[16,16,128]{2,1,0:T(8,128)S(1)} all-to-all(f32[16,16,128]{2,1,0:T(8,128)S(1)} %shard_map.61), channel_id=1, replica_groups=mesh['y'=4,'z'=8,'x'=4,'c'=2] {'y','x'}, dimensions={0} | all-to-all | bytes 262144 | tf_op jit(solution)/shard_map/all_to_all | solution.py:284
  74.7 2.4 %shard_map.62 = f32[24,128]{1,0:T(8,128)S(1)} custom-call(s32[32]{0:T(128)S(1)} %get-tuple-element.9.pairs_ref, s32[2]{0:T(128)S(1)} %pad_add_fusion.place_ref, bf16[2048,128]{1,0:T(8,128)(2,1)S(1)} %get-tuple-element.10.sources_ref, bf16[2048,128]{1,0:T(8,128)(2,1)S(1)} %all_gather.17.targets_ref, f32[4,128]{1,0:T(4,128)S(1)} %get-tuple-element.11.source_squares_ref, ...), custom_call_target="tpu_custom_call" | custom-call | flops 1073741824 | bytes 4194304 | tf_op jit(solution)/shard_map/pallas_call | solution.py:291
  77.1 1.8 %all-gather.1 = f32[48,128]{1,0:T(8,128)S(1)} all-gather(f32[24,128]{1,0:T(8,128)S(1)} %shard_map.62), channel_id=3, replica_groups=mesh['y'=4,'z'=8,'x'=4,'c'=2] {'c'}, dimensions={0}, use_global_device_ids=true | all-gather | bytes 36864 | tf_op jit(solution)/shard_map/all_gather | solution.py:355
  78.9 1.1 %shard_map.63 = (f32[32,8,128]{2,1,0:T(8,128)S(1)}, f32[8,128]{1,0:T(8,128)}) custom-call(s32[2]{0:T(128)S(1)} %pad_add_fusion.place_ref, f32[2,24,128]{2,1,0:T(8,128)S(1)} %bitcast.15), custom_call_target="tpu_custom_call" | custom-call | flops 1073741824 | bytes 4194304 | tf_op jit(solution)/shard_map/pallas_call | solution.py:291
  80.0 17.2 %all_to_all.28.parts_ref = f32[32,8,128]{2,1,0:T(8,128)S(1)} all-to-all(f32[32,8,128]{2,1,0:T(8,128)S(1)} %get-tuple-element.15), channel_id=1, replica_groups=mesh['y'=4,'z'=8,'x'=4,'c'=2] {'y','z'}, dimensions={0} | all-to-all | bytes 262144 | tf_op jit(solution)/shard_map/all_to_all | solution.py:284
  97.3 0.6 shard_map.64
  (6 shorter events, 0.0 us)
Async XLA Ops:
  0.6 12.8 %copy-start = (bf16[1024,128]{1,0:T(8,128)(2,1)S(1)}, bf16[1024,128]{1,0:T(8,128)(2,1)}, u32[]{:S(2)}) copy-start(bf16[1024,128]{1,0:T(8,128)(2,1)} %param.5) | copy-start | bytes 786436
  2.2 9.4 %copy-start.1 = (f32[4096]{0:T(1024)S(1)}, f32[4096]{0:T(1024)}, u32[]{:S(2)}) copy-start(f32[4096]{0:T(1024)} %param.7) | copy-start | bytes 49156
  2.2 19.1 %all-to-all-start = ((bf16[8,128,128]{2,1,0:T(8,128)(2,1)}), bf16[8,128,128]{2,1,0:T(8,128)(2,1)S(1)}, u32[]{:S(2)}, u32[]{:S(2)}) async-start(bf16[8,128,128]{2,1,0:T(8,128)(2,1)} %broadcast_in_dim.2), calls=%async_computation | async-start | bytes 524288 | tf_op jit(solution)/shard_map/all_to_all | solution.py:284
  10.9 0.7 copy-start.2
  13.4 10.0 %collective-permute-start.2 = (bf16[528,128]{1,0:T(8,128)(2,1)S(1)}, bf16[528,128]{1,0:T(8,128)(2,1)S(1)}, u32[]{:S(2)}, u32[]{:S(2)}) collective-permute-start(bf16[528,128]{1,0:T(8,128)(2,1)S(1)} %fusion.1.own_ref), channel_id=1, source_target_pairs={{0,192},{64,0},{128,64},{192,128},{1,193},{65,1},{129,65},{193,129... | collective-permute-start | bytes 405512 | tf_op jit(solution)/shard_map/ppermute | solution.py:318
  16.5 8.0 %collective-permute-start.1 = (bf16[528,128]{1,0:T(8,128)(2,1)S(1)}, bf16[528,128]{1,0:T(8,128)(2,1)S(1)}, u32[]{:S(2)}, u32[]{:S(2)}) collective-permute-start(bf16[528,128]{1,0:T(8,128)(2,1)S(1)} %fusion.1.own_ref), channel_id=1, source_target_pairs={{0,128},{64,192},{128,0},{192,64},{1,129},{65,193},{129,1},{193,65... | collective-permute-start | bytes 405512 | tf_op jit(solution)/shard_map/ppermute | solution.py:318
  17.2 9.1 %collective-permute-start = (bf16[528,128]{1,0:T(8,128)(2,1)S(1)}, bf16[528,128]{1,0:T(8,128)(2,1)S(1)}, u32[]{:S(2)}, u32[]{:S(2)}) collective-permute-start(bf16[528,128]{1,0:T(8,128)(2,1)S(1)} %fusion.1.own_ref), channel_id=1, source_target_pairs={{0,64},{64,128},{128,192},{192,0},{1,65},{65,129},{129,193},{193,1... | collective-permute-start | bytes 405512 | tf_op jit(solution)/shard_map/ppermute | solution.py:318

commit v6 on v5

--- a/solution.py
+++ b/solution.py
@@ -198,36 +198,36 @@
     return jnp.where(mine, jnp.left_shift(jnp.ones_like(pair), number), 0).astype(f32)
 
 
-def first_rows(place_ref, own_ref, by1_ref, by2_ref, by3_ref, targets_ref, shared_ref, out_ref, sources_ref, source_squares_ref, target_squares_ref, pairs_ref, *scratch):
-    y, c = place_ref[0], place_ref[1]
+def first_rows(own_ref, by1_ref, by2_ref, by3_ref, shared_ref, potential_ref, out_ref, sources_ref, targets_ref, source_squares_ref, target_squares_ref, kept_ref, *scratch):
+    y, c = lax.axis_index("y"), lax.axis_index("c")
     kept = jnp.zeros((1, LANES), f32)
+    points = 2 * BLOCK
+    for c_from in range(2):
+        lists = shared_ref[c_from, points:points + 16, :].astype(f32)
+        for by in range(4):
+            kept = kept + bits(lists[by:by + 1, :], (y + 4 - by) & 3, c_from, y, c)
+        targets_ref[c_from * points:(c_from + 1) * points, :] = shared_ref[c_from, 0:points, :]
+    kept_ref[...] = jnp.broadcast_to(kept, kept_ref.shape)
     for by, ref in enumerate((own_ref, by1_ref, by2_ref, by3_ref)):
-        y_from = (y + 4 - by) & 3
-        lists = ref[BLOCK:BLOCK + 16, :].astype(f32)
-        for c_from in range(2):
-            kept = kept + bits(lists[c_from:c_from + 1, :], y_from, c_from, y, c)
-        sources_ref[pl.ds(pl.multiple_of(y_from * BLOCK, BLOCK), BLOCK), :] = ref[0:BLOCK, :]
-    kept = jnp.sum(kept).astype(jnp.int32)
-
-    def pick(number, found):
-        pairs_ref[found] = number
-        return found + ((kept >> number) & 1)
-
-    found = lax.fori_loop(0, PAIRS_MAX, pick, 0)
-    pairs_ref[PAIRS_MAX] = found
+        sources_ref[pl.ds(pl.multiple_of(((y + 4 - by) & 3) * BLOCK, BLOCK), BLOCK), :] = ref[0:BLOCK, :]
     source_squares_ref[...] = squares(own_ref[0:BLOCK, :])
     squared = squares(targets_ref[...])
     target_squares_ref[...] = squared
     rows = pl.ds(pl.multiple_of(y * 8, 8), 8)
-    potential = jnp.concatenate([shared_ref[0, rows, :], shared_ref[1, rows, :]], axis=0)
+    potential = jnp.concatenate([potential_ref[0, rows, :], potential_ref[1, rows, :]], axis=0)
     bias = 0.5 * (potential - squared)
-    half_step(pairs_ref, targets_ref, sources_ref, bias, False, *scratch)
+    half_step(kept_ref, targets_ref, sources_ref, bias, False, *scratch)
     spread_out(out_ref, scratch)
 
 
-def half_step(pairs_ref, kept_ref, sum_ref, bias, kept_first, acc_max, acc_sum, even, odd):
+def half_step(kept_pairs_ref, kept_ref, sum_ref, bias, kept_first, acc_max, acc_sum, even, odd, chosen):
     clear(acc_max, acc_sum)
-    sweep(pairs_ref, pairs_ref[PAIRS_MAX], kept_ref, sum_ref, bias, acc_max, acc_sum, even, odd, kept_first)
+    kept = jnp.sum(kept_pairs_ref[0:1, :]).astype(jnp.int32)
+    found = jnp.int32(0)
+    for number in range(PAIRS_MAX):
+        chosen[found] = number
+        found = found + ((kept >> number) & 1)
+    sweep(chosen, found, kept_ref, sum_ref, bias, acc_max, acc_sum, even, odd, kept_first)
 
 
 def spread_out(out_ref, scratch):
@@ -236,127 +236,120 @@
         out_ref[k] = dense
 
 
-def next_rows(pairs_ref, sources_ref, targets_ref, parts_ref, out_ref, *scratch):
+def next_rows(kept_ref, sources_ref, targets_ref, parts_ref, out_ref, *scratch):
     bias = half_bias(combined(parts_ref[...]))
-    half_step(pairs_ref, targets_ref, sources_ref, bias, False, *scratch)
+    half_step(kept_ref, targets_ref, sources_ref, bias, False, *scratch)
     spread_out(out_ref, scratch)
 
 
-def next_columns(pairs_ref, sources_ref, targets_ref, parts_ref, out_ref, *scratch):
+def next_columns(kept_ref, sources_ref, targets_ref, parts_ref, out_ref, *scratch):
     bias = half_bias(combined(parts_ref[...]))
-    half_step(pairs_ref, sources_ref, targets_ref, bias, True, *scratch)
+    half_step(kept_ref, sources_ref, targets_ref, bias, True, *scratch)
     spread_out(out_ref, scratch)
 
 
-def last_columns(pairs_ref, place_ref, sources_ref, targets_ref, source_squares_ref, target_squares_ref, parts_ref, out_ref, all_bias, *scratch):
+def last_columns(kept_ref, sources_ref, targets_ref, source_squares_ref, target_squares_ref, parts_ref, out_ref, all_bias, *scratch):
     bias = half_bias(combined(parts_ref[...]))
     all_bias[...] = bias
-    half_step(pairs_ref, sources_ref, targets_ref, bias, True, *scratch)
-    out_ref[0:16, :] = finished(scratch[0], scratch[1]) - target_squares_ref[...] * (LOG2E / EPS_REG)
-    own = all_bias[pl.ds(place_ref[0] * GROUPS, GROUPS), :]
+    own = all_bias[pl.ds(lax.axis_index("y") * GROUPS, GROUPS), :]
     out_ref[16:16 + GROUPS, :] = source_squares_ref[...] + 2.0 * own
     out_ref[16 + GROUPS:24, :] = jnp.zeros((8 - GROUPS, LANES), f32)
-
-
-def both_cores(place_ref, parts_ref, out_ref, potential_ref):
-    rows = pl.ds(pl.multiple_of(place_ref[1] * 8, 8), 8)
+    half_step(kept_ref, sources_ref, targets_ref, bias, True, *scratch)
+    out_ref[0:16, :] = finished(scratch[0], scratch[1]) - target_squares_ref[...] * (LOG2E / EPS_REG)
+
+
+def both_cores(parts_ref, out_ref):
+    rows = pl.ds(pl.multiple_of(lax.axis_index("c") * 8, 8), 8)
     lse = combined(jnp.stack([parts_ref[0, rows, :], parts_ref[1, rows, :]]))
     for k in range(out_ref.shape[0]):
         out_ref[k] = lse
+
+
+def last_potentials(parts_ref, cores_ref, source_ref, target_ref):
     for b in range(2):
-        potential_ref[b * GROUPS:(b + 1) * GROUPS, :] = parts_ref[b, 16:16 + GROUPS, :]
-
-
-def last_potential(parts_ref, potential_ref):
+        source_ref[b * GROUPS:(b + 1) * GROUPS, :] = cores_ref[b, 16:16 + GROUPS, :]
     count = parts_ref.shape[0] // 4
     for y in range(4):
         lse = combined(parts_ref[y * count:(y + 1) * count])
-        potential_ref[y * 8:(y + 1) * 8, :] = 2.0 * half_bias(lse)
-
-
-SMEM = pl.BlockSpec(memory_space=pltpu.SMEM)
+        target_ref[y * 8:(y + 1) * 8, :] = 2.0 * half_bias(lse)
+
+
 VMEM = pl.BlockSpec(memory_space=pltpu.VMEM)
 PARAMS = pltpu.CompilerParams(vmem_limit_bytes=24 * 1024 * 1024)
-WORK = [pltpu.VMEM((8, BLOCK), f32)] * 2 + [pltpu.VMEM((BLOCK, BLOCK), f32)] * 2
+WORK = [pltpu.VMEM((8, BLOCK), f32)] * 2 + [pltpu.VMEM((BLOCK, BLOCK), f32)] * 2 + [pltpu.SMEM((PAIRS_MAX,), jnp.int32)]
 
 
 def spread(parts, axes):
     return lax.all_to_all(parts, axes, 0, 0, tiled=True)
 
 
-def call(kernel, out_shape, smem, vmem, scratch, smem_outs=0):
-    out_specs = jax.tree.map(lambda _: VMEM, out_shape)
-    if smem_outs:
-        out_specs = out_specs[:-smem_outs] + [SMEM] * smem_outs
+def call(kernel, out_shape, operands, scratch):
     return pl.pallas_call(
         kernel,
         out_shape=out_shape,
-        in_specs=[SMEM] * len(smem) + [VMEM] * len(vmem),
-        out_specs=out_specs,
+        in_specs=[VMEM] * len(operands),
+        out_specs=jax.tree.map(lambda _: VMEM, out_shape),
         scratch_shapes=scratch,
         compiler_params=PARAMS,
         cost_estimate=pl.CostEstimate(flops=1 << 30, bytes_accessed=1 << 22, transcendentals=1 << 20),
-    )(*smem, *vmem)
+    )(*operands)
 
 
 def per_device(source_points, target_points, initial_potential, pair_list, pair_count):
     n_y, n_z = lax.axis_size("y"), lax.axis_size("z")
     own = target_points.shape[0]
     tgt_rows = n_z * own // LANES
-    y, c = lax.axis_index("y"), lax.axis_index("c")
-    place = jnp.stack([y, c]).astype(jnp.int32)
+    c = lax.axis_index("c")
 
     def shape(*dims):
         return jax.ShapeDtypeStruct(dims, f32)
 
-    listed = jnp.pad(pair_list.reshape(1, PAIRS_MAX).astype(f32), ((0, 7), (0, LANES - PAIRS_MAX)), constant_values=-1)
-    shared = jnp.concatenate([initial_potential.reshape(n_y * tgt_rows, LANES), listed], axis=0)
-    shared = lax.all_gather(shared, "c")
-    lists = jnp.pad(shared[:, n_y * tgt_rows, :].astype(bf16), ((0, 14), (0, 0)), constant_values=-1)
-    sources = jnp.concatenate([lax.dynamic_slice_in_dim(source_points, c * BLOCK, BLOCK, 0), lists], axis=0)
+    def points(*dims):
+        return jax.ShapeDtypeStruct(dims, bf16)
+
+    listed = jnp.pad(pair_list.reshape(1, PAIRS_MAX).astype(bf16), ((0, 15), (0, LANES - PAIRS_MAX)), constant_values=-1)
+    sources = jnp.concatenate([lax.dynamic_slice_in_dim(source_points, c * BLOCK, BLOCK, 0), listed], axis=0)
     by = [
         lax.ppermute(sources, "y", [(i, (i + k) % n_y) for i in range(n_y)]) for k in range(1, n_y)
     ]
     targets = spread(jnp.broadcast_to(target_points[None], (n_z, own, EMB)), "z").reshape(n_z * own, EMB)
-    targets = lax.all_gather(targets, "c", axis=0, tiled=True)
+    lists = [part[BLOCK:BLOCK + 1] for part in (sources, *by)]
+    targets = jnp.concatenate([targets, *lists, listed[4:]], axis=0)
+    targets = lax.all_gather(targets, "c")
+    potential = lax.all_gather(initial_potential.reshape(n_y * tgt_rows, LANES), "c")
     row_shape = shape(16, 16, LANES)
-    row_parts, sources, source_squares, target_squares, pairs = call(
+    row_parts, sources, targets, source_squares, target_squares, kept = call(
         first_rows,
         [
             row_shape,
-            jax.ShapeDtypeStruct((n_y * BLOCK, EMB), bf16),
+            points(n_y * BLOCK, EMB),
+            points(2 * n_z * own, EMB),
             shape(GROUPS, LANES),
             shape(2 * tgt_rows, LANES),
-            jax.ShapeDtypeStruct((2 * PAIRS_MAX,), jnp.int32),
+            shape(8, LANES),
         ],
-        (place,),
-        (sources, *by, targets, shared),
+        (sources, *by, targets, potential),
         WORK,
-        1,
     )
     for iteration in range(ITERS):
         if iteration > 0:
-            row_parts = call(next_rows, row_shape, (pairs,), (sources, targets, col_parts), WORK)
+            row_parts = call(next_rows, row_shape, (kept, sources, targets, col_parts), WORK)
         row_parts = spread(row_parts, ("y", "x"))
         if iteration < ITERS - 1:
-            col_parts = call(next_columns, row_shape, (pairs,), (sources, targets, row_parts), WORK)
+            col_parts = call(next_columns, row_shape, (kept, sources, targets, row_parts), WORK)
             col_parts = spread(col_parts, ("z", "c"))
     parts = call(
         last_columns,
         shape(24, LANES),
-        (pairs, place),
-        (sources, targets, source_squares, target_squares, row_parts),
+        (kept, sources, targets, source_squares, target_squares, row_parts),
         [pltpu.VMEM((16, LANES), f32)] + WORK,
     )
-    col_parts, source_potential = call(
-        both_cores,
-        [shape(n_y * n_z, tgt_rows, LANES), shape(2 * GROUPS, LANES)],
-        (place,),
-        (lax.all_gather(parts, "c"),),
-        [],
+    parts = lax.all_gather(parts, "c")
+    col_parts = call(both_cores, shape(n_y * n_z, tgt_rows, LANES), (parts,), [])
+    col_parts = spread(col_parts, ("y", "z"))
+    source_potential, target_potential = call(
+        last_potentials, [shape(2 * GROUPS, LANES), shape(n_y * tgt_rows, LANES)], (col_parts, parts), []
     )
-    col_parts = spread(col_parts, ("y", "z"))
-    target_potential = call(last_potential, shape(n_y * tgt_rows, LANES), (), (col_parts,), [])
     return source_potential.reshape(-1), target_potential.reshape(-1)
 
 

time: 98 us -> 93 us (0.949)
  blocking collectives: 63.1 us -> 59.8 us
  Pallas kernels: 12.5 us -> 10.8 us
    all_to_all x4, blocking collectives: 57.3 us -> 53.9 us  [spread(): return lax.all_to_all(parts, axes, 0, 0, tiled=True)]
    all_to_all x1, waiting for transfers between devices: 3.09 us -> 0.01 us  [spread(): return lax.all_to_all(parts, axes, 0, 0, tiled=True)]
    ppermute x3, waiting for transfers between devices: 2.84 us -> 5.45 us  [per_device(): lax.ppermute(sources, 'y', [(i, (i + k) % n_y) for i in range(n_y)])]
    pallas_call x6, Pallas kernels: 12.5 us -> 10.8 us  [call(): pl.pallas_call(kernel, out_shape=out_shape, in_specs=[VMEM] * len(operand...]
where the time goes in v6:
time: 93 us; the launch traced here: 92 us
  blocking collectives  59.8 us (64%)
  starting transfers between devices  13.4 us (14%)
  Pallas kernels  10.8 us (12%)
  waiting for transfers between devices  5.45 us (6%)
  local copies, waits for them, and re-layouts  1.85 us (2%)
    all_to_all x4, blocking collectives, spread(): return lax.all_to_all(parts, axes, 0, 0, tiled=True)  53.9 us
    pallas_call x6, Pallas kernels, call(): pl.pallas_call(kernel, out_shape=out_shape, in_specs=[VMEM] * len(operand...  10.8 us
    all_to_all x1, starting transfers between devices, spread(): return lax.all_to_all(parts, axes, 0, 0, tiled=True)  8.7 us
    ppermute x3, waiting for transfers between devices, per_device(): lax.ppermute(sources, 'y', [(i, (i + k) % n_y) for i in range(n_y)])  5.45 us
    ppermute x3, starting transfers between devices, per_device(): lax.ppermute(sources, 'y', [(i, (i + k) % n_y) for i in range(n_y)])  4.69 us
    all_gather x1, blocking collectives, per_device(): targets = lax.all_gather(targets, 'c')  2.19 us
  transfers between devices with their start and end apart: 4, of which 3 were waited for; matrix products, arithmetic and copies ran while one was open for 0% of the time, Pallas kernels for 0%

profile of v6, /device:TPU:32, one launch (start us, length us, event | category | flops | bytes accessed | tf_op | source)
XLA Modules:
  0.0 92.0 jit_solution(5163928921042433672)
XLA Ops:
  0.6 0.0 copy-start
  0.6 1.5 %broadcast_in_dim.2 = bf16[8,128,128]{2,1,0:T(8,128)(2,1)} broadcast(bf16[128,128]{1,0:T(8,128)(2,1)} %param.6), dimensions={1,2} | broadcast | bytes 294912 | tf_op jit(solution)/shard_map/broadcast_in_dim | solution.py:315
  2.2 0.0 copy-start.2
  2.2 8.7 %all-to-all-start = ((bf16[8,128,128]{2,1,0:T(8,128)(2,1)}), bf16[8,128,128]{2,1,0:T(8,128)(2,1)S(1)}, u32[]{:S(2)}, u32[]{:S(2)}) async-start(bf16[8,128,128]{2,1,0:T(8,128)(2,1)} %broadcast_in_dim.2), calls=%async_computation | async-start | bytes 524288 | tf_op jit(solution)/shard_map/all_to_all | solution.py:283
  10.9 0.0 copy-done.2
  10.9 0.0 copy-done
  10.9 0.0 copy-start.1
  11.0 3.1 %collective-permute-start.2 = (bf16[528,128]{1,0:T(8,128)(2,1)S(1)}, bf16[528,128]{1,0:T(8,128)(2,1)S(1)}, u32[]{:S(2)}, u32[]{:S(2)}) collective-permute-start(bf16[528,128]{1,0:T(8,128)(2,1)S(1)} %pad_maximum_fusion.own_ref), channel_id=1, source_target_pairs={{0,192},{64,0},{128,64},{192,128},{1,193},{65,1},{129,65},{193,129... | collective-permute-start | bytes 405512 | tf_op jit(solution)/shard_map/ppermute | solution.py:313
  14.1 0.6 collective-permute-start.1
  14.7 1.0 %collective-permute-start = (bf16[528,128]{1,0:T(8,128)(2,1)S(1)}, bf16[528,128]{1,0:T(8,128)(2,1)S(1)}, u32[]{:S(2)}, u32[]{:S(2)}) collective-permute-start(bf16[528,128]{1,0:T(8,128)(2,1)S(1)} %pad_maximum_fusion.own_ref), channel_id=1, source_target_pairs={{0,64},{64,128},{128,192},{192,0},{1,65},{65,129},{129,193},{193,1... | collective-permute-start | bytes 405512 | tf_op jit(solution)/shard_map/ppermute | solution.py:313
  15.7 0.0 copy-done.1
  15.7 1.8 %all_gather.17.potential_ref = f32[2,32,128]{2,1,0:T(8,128)S(1)} all-gather(f32[1,32,128]{2,1,0:T(8,128)S(1)} %bitcast.12), channel_id=1, replica_groups=mesh['y'=4,'z'=8,'x'=4,'c'=2] {'c'}, dimensions={0}, use_global_device_ids=true | all-gather | bytes 49152 | tf_op jit(solution)/shard_map/all_gather | solution.py:319
  17.5 1.8 %collective-permute-done.2.by3_ref = bf16[528,128]{1,0:T(8,128)(2,1)S(1)} collective-permute-done((bf16[528,128]{1,0:T(8,128)(2,1)S(1)}, bf16[528,128]{1,0:T(8,128)(2,1)S(1)}, u32[]{:S(2)}, u32[]{:S(2)}) %collective-permute-start.2) | collective-permute-done | bytes 135200 | tf_op jit(solution)/shard_map/ppermute | solution.py:313
  19.3 2.3 %collective-permute-done.1.by2_ref = bf16[528,128]{1,0:T(8,128)(2,1)S(1)} collective-permute-done((bf16[528,128]{1,0:T(8,128)(2,1)S(1)}, bf16[528,128]{1,0:T(8,128)(2,1)S(1)}, u32[]{:S(2)}, u32[]{:S(2)}) %collective-permute-start.1) | collective-permute-done | bytes 135200 | tf_op jit(solution)/shard_map/ppermute | solution.py:313
  21.6 1.4 %collective-permute-done.by1_ref = bf16[528,128]{1,0:T(8,128)(2,1)S(1)} collective-permute-done((bf16[528,128]{1,0:T(8,128)(2,1)S(1)}, bf16[528,128]{1,0:T(8,128)(2,1)S(1)}, u32[]{:S(2)}, u32[]{:S(2)}) %collective-permute-start) | collective-permute-done | bytes 135200 | tf_op jit(solution)/shard_map/ppermute | solution.py:313
  23.0 0.0 all-to-all-done
  23.0 0.3 concatenate.7
  23.2 2.2 %all-gather = bf16[2080,128]{1,0:T(8,128)(2,1)S(1)} all-gather(bf16[1040,128]{1,0:T(8,128)(2,1)S(1)} %concatenate.7), channel_id=2, replica_groups=mesh['y'=4,'z'=8,'x'=4,'c'=2] {'c'}, dimensions={0}, use_global_device_ids=true | all-gather | bytes 798720 | tf_op jit(solution)/shard_map/all_gather | solution.py:318
  25.4 2.8 %shard_map.59 = (f32[16,16,128]{2,1,0:T(8,128)S(1)}, bf16[2048,128]{1,0:T(8,128)(2,1)S(1)}, bf16[2048,128]{1,0:T(8,128)(2,1)S(1)}, f32[4,128]{1,0:T(4,128)S(1)},...) custom-call(bf16[528,128]{1,0:T(8,128)(2,1)S(1)} %pad_maximum_fusion.own_ref, ...), custom_call_target="tpu_custom_call" | custom-call | flops 1073741824 | bytes 4194304 | tf_op jit(solution)/shard_map/pallas_call | solution.py:287
  28.2 12.9 %all_to_all.25.parts_ref = f32[16,16,128]{2,1,0:T(8,128)S(1)} all-to-all(f32[16,16,128]{2,1,0:T(8,128)S(1)} %get-tuple-element.15), channel_id=1, replica_groups=mesh['y'=4,'z'=8,'x'=4,'c'=2] {'y','x'}, dimensions={0} | all-to-all | bytes 262144 | tf_op jit(solution)/shard_map/all_to_all | solution.py:283
  41.1 2.4 %shard_map.60 = f32[16,16,128]{2,1,0:T(8,128)S(1)} custom-call(f32[8,128]{1,0:T(8,128)S(1)} %get-tuple-element.10.kept_ref, bf16[2048,128]{1,0:T(8,128)(2,1)S(1)} %get-tuple-element.11.sources_ref, bf16[2048,128]{1,0:T(8,128)(2,1)S(1)} %get-tuple-element.12.targets_ref, f32[16,16,128]{2,1,0:T(8,128)S(1)} %all_to_all.25.parts_ref), custom_call_target="tpu_custom_call" | custom-call | flops 1073741824 | bytes 4194304 | tf_op jit(solution)/shard_map/pallas_call | solution.py:287
  43.5 13.8 %all_to_all.26.parts_ref = f32[16,16,128]{2,1,0:T(8,128)S(1)} all-to-all(f32[16,16,128]{2,1,0:T(8,128)S(1)} %shard_map.60), channel_id=1, replica_groups=mesh['y'=4,'z'=8,'x'=4,'c'=2] {'z','c'}, dimensions={0} | all-to-all | bytes 262144 | tf_op jit(solution)/shard_map/all_to_all | solution.py:283
  57.3 2.4 %shard_map.61 = f32[16,16,128]{2,1,0:T(8,128)S(1)} custom-call(f32[8,128]{1,0:T(8,128)S(1)} %get-tuple-element.10.kept_ref, bf16[2048,128]{1,0:T(8,128)(2,1)S(1)} %get-tuple-element.11.sources_ref, bf16[2048,128]{1,0:T(8,128)(2,1)S(1)} %get-tuple-element.12.targets_ref, f32[16,16,128]{2,1,0:T(8,128)S(1)} %all_to_all.26.parts_ref), custom_call_target="tpu_custom_call" | custom-call | flops 1073741824 | bytes 4194304 | tf_op jit(solution)/shard_map/pallas_call | solution.py:287
  59.7 11.8 %all_to_all.27.parts_ref = f32[16,16,128]{2,1,0:T(8,128)S(1)} all-to-all(f32[16,16,128]{2,1,0:T(8,128)S(1)} %shard_map.61), channel_id=1, replica_groups=mesh['y'=4,'z'=8,'x'=4,'c'=2] {'y','x'}, dimensions={0} | all-to-all | bytes 262144 | tf_op jit(solution)/shard_map/all_to_all | solution.py:283
  71.5 2.5 %shard_map.62 = f32[24,128]{1,0:T(8,128)S(1)} custom-call(f32[8,128]{1,0:T(8,128)S(1)} %get-tuple-element.10.kept_ref, bf16[2048,128]{1,0:T(8,128)(2,1)S(1)} %get-tuple-element.11.sources_ref, bf16[2048,128]{1,0:T(8,128)(2,1)S(1)} %get-tuple-element.12.targets_ref, f32[4,128]{1,0:T(4,128)S(1)} %get-tuple-element.13.source_squares_ref, ...), custom_call_target="tpu_custom_call" | custom-call | flops 1073741824 | bytes 4194304 | tf_op jit(solution)/shard_map/pallas_call | solution.py:287
  74.0 1.8 %all-gather.1 = f32[48,128]{1,0:T(8,128)S(1)} all-gather(f32[24,128]{1,0:T(8,128)S(1)} %shard_map.62), channel_id=3, replica_groups=mesh['y'=4,'z'=8,'x'=4,'c'=2] {'c'}, dimensions={0}, use_global_device_ids=true | all-gather | bytes 36864 | tf_op jit(solution)/shard_map/all_gather | solution.py:347
  75.9 15.5 %all_to_all.28.parts_ref = f32[32,8,128]{2,1,0:T(8,128)S(1)} all-to-all(f32[32,8,128]{2,1,0:T(8,128)S(1)} %shard_map.63), channel_id=1, replica_groups=mesh['y'=4,'z'=8,'x'=4,'c'=2] {'y','z'}, dimensions={0} | all-to-all | bytes 262144 | tf_op jit(solution)/shard_map/all_to_all | solution.py:283
  91.3 0.7 shard_map.64
  (10 shorter events, 0.1 us)
Async XLA Ops:
  0.6 10.3 %copy-start = (bf16[1024,128]{1,0:T(8,128)(2,1)S(1)}, bf16[1024,128]{1,0:T(8,128)(2,1)}, u32[]{:S(2)}) copy-start(bf16[1024,128]{1,0:T(8,128)(2,1)} %param.5) | copy-start | bytes 786436
  2.2 8.7 %copy-start.2 = (s32[1,1,16]{2,1,0:T(1,128)S(1)}, s32[1,1,16]{2,1,0:T(1,128)}, u32[]{:S(2)}) copy-start(s32[1,1,16]{2,1,0:T(1,128)} %param.8) | copy-start | bytes 196
  2.2 20.8 %all-to-all-start = ((bf16[8,128,128]{2,1,0:T(8,128)(2,1)}), bf16[8,128,128]{2,1,0:T(8,128)(2,1)S(1)}, u32[]{:S(2)}, u32[]{:S(2)}) async-start(bf16[8,128,128]{2,1,0:T(8,128)(2,1)} %broadcast_in_dim.2), calls=%async_computation | async-start | bytes 524288 | tf_op jit(solution)/shard_map/all_to_all | solution.py:283
  10.9 4.7 %copy-start.1 = (f32[4096]{0:T(1024)S(1)}, f32[4096]{0:T(1024)}, u32[]{:S(2)}) copy-start(f32[4096]{0:T(1024)} %param.7) | copy-start | bytes 49156
  11.0 8.3 %collective-permute-start.2 = (bf16[528,128]{1,0:T(8,128)(2,1)S(1)}, bf16[528,128]{1,0:T(8,128)(2,1)S(1)}, u32[]{:S(2)}, u32[]{:S(2)}) collective-permute-start(bf16[528,128]{1,0:T(8,128)(2,1)S(1)} %pad_maximum_fusion.own_ref), channel_id=1, source_target_pairs={{0,192},{64,0},{128,64},{192,128},{1,193},{65,1},{129,65},{193,129... | collective-permute-start | bytes 405512 | tf_op jit(solution)/shard_map/ppermute | solution.py:313
  14.1 7.5 %collective-permute-start.1 = (bf16[528,128]{1,0:T(8,128)(2,1)S(1)}, bf16[528,128]{1,0:T(8,128)(2,1)S(1)}, u32[]{:S(2)}, u32[]{:S(2)}) collective-permute-start(bf16[528,128]{1,0:T(8,128)(2,1)S(1)} %pad_maximum_fusion.own_ref), channel_id=1, source_target_pairs={{0,128},{64,192},{128,0},{192,64},{1,129},{65,193},{129,1},{193,65... | collective-permute-start | bytes 405512 | tf_op jit(solution)/shard_map/ppermute | solution.py:313
  14.7 8.3 %collective-permute-start = (bf16[528,128]{1,0:T(8,128)(2,1)S(1)}, bf16[528,128]{1,0:T(8,128)(2,1)S(1)}, u32[]{:S(2)}, u32[]{:S(2)}) collective-permute-start(bf16[528,128]{1,0:T(8,128)(2,1)S(1)} %pad_maximum_fusion.own_ref), channel_id=1, source_target_pairs={{0,64},{64,128},{128,192},{192,0},{1,65},{65,129},{129,193},{193,1... | collective-permute-start | bytes 405512 | tf_op jit(solution)/shard_map/ppermute | solution.py:313

commit v7 on v6

--- a/solution.py
+++ b/solution.py
@@ -13,10 +13,12 @@
 LANES = 128
 EMB = 128
 PAIRS_MAX = 16
-ITERS = 2
 NEG_START = -1e30
 EPS_REG = 0.2
 LOG2E = math.log2(math.e)
+LOG2_N = math.log2(32768)
+SMALLEST = 2.0 ** -85
+WIDEST = 85.0
 SCALE = 2.0 * LOG2E / EPS_REG
 GROUPS = BLOCK // LANES
 HALF = BLOCK // 2
@@ -29,27 +31,31 @@
 f32 = jnp.float32
 
 
-def squares(points):
-    values = points.astype(f32)
-    sq = values * values
-    high = sq.astype(bf16)
-    low = (sq - high.astype(f32)).astype(bf16)
-    parts = jnp.concatenate([high, low], axis=1)
+def lane_sums(terms):
     ones = jnp.ones((16, 2 * EMB), bf16)
-    groups = points.shape[0] // HALF
-    slots = [(g % 2, g // 2 % 2) for g in range(groups)]
+    groups = terms[0].shape[0] // HALF
 
     def sums(products):
-        for g, (mxu, stage) in enumerate(slots):
-            pltpu.matmul_push_rhs(parts[g * HALF:(g + 1) * HALF], stage, mxu, transpose=True)
-            pltpu.matmul_acc_lhs(products[g], ones, load_staged_rhs=stage)
+        for k in range(0, len(terms), 2):
+            parts = jnp.concatenate(terms[k:k + 2], axis=1)
+            for g in range(groups):
+                stage = g // 2 % 2
+                pltpu.matmul_push_rhs(parts[g * HALF:(g + 1) * HALF], stage, g % 2, transpose=True)
+                pltpu.matmul_acc_lhs(products[g], ones, load_staged_rhs=stage)
         rows = []
         for g in range(groups):
             out = pltpu.matmul_pop(products[g])
             rows += [out[0:1, :LANES], out[0:1, LANES:]]
         return jnp.concatenate(rows, axis=0)
 
-    return pl.run_scoped(sums, [pltpu.ACC(mxu)((16, HALF), f32) for mxu, _ in slots])
+    return pl.run_scoped(sums, [pltpu.ACC(g % 2)((16, HALF), f32) for g in range(groups)])
+
+
+def squares(points):
+    values = points.astype(f32)
+    sq = values * values
+    high = sq.astype(bf16)
+    return lane_sums([high, (sq - high.astype(f32)).astype(bf16)])
 
 
 def bias_columns(bias):
@@ -69,7 +75,7 @@
 
 
 def half_bias(lse):
-    return (-0.5 * EPS_REG / LOG2E) * (math.log2(32768) + lse)
+    return (-0.5 * EPS_REG / LOG2E) * (LOG2_N + lse)
 
 
 def clear(acc_max, acc_sum):
@@ -82,7 +88,7 @@
     pl.run_scoped(functools.partial(sweep_with, *operands), products)
 
 
-def sweep_with(pairs_ref, count, kept_ref, sum_ref, bias, acc_max, acc_sum, even, odd, kept_first, mxus):
+def sweep_with(pairs_ref, count, kept_ref, sum_ref, bias, acc_max, acc_sum, even, odd, kept_first, saved, mxus):
     kept_bias = bias_columns(bias)
     lane = lax.broadcasted_iota(jnp.int32, (CHUNK, LANES), 1) & (bias.shape[0] - 1)
     ones = jnp.ones((HALF, LANES), bf16)
@@ -116,9 +122,12 @@
             for r in range(0, CHUNK, 8):
                 peak[m] = jnp.maximum(peak[m], out[r:r + 8])
 
-    def add(parity, j, shift, partial):
+    def add(number, parity, j, shift, partial):
         for r in range(j * CHUNK, (j + 1) * CHUNK, 8):
-            partial = partial + jnp.exp2((buffers[parity][r:r + 8, :] - shift) * SCALE)
+            terms = jnp.exp2((buffers[parity][r:r + 8, :] - shift) * SCALE)
+            partial = partial + terms
+            if saved is not None:
+                saved[0][jnp.maximum(number, 0), r:r + 8, :] = terms
         return partial
 
     def settle(number, peak):
@@ -127,6 +136,8 @@
         old_max = acc_max[pl.ds(place, 1), :]
         highest = jnp.where(number < count, jnp.maximum(old_max, block_max), old_max)
         acc_max[pl.ds(place, 1), :] = highest
+        if saved is not None:
+            saved[1][pl.ds(number, 1), :] = highest
         acc_sum[pl.ds(place, 1), :] = acc_sum[pl.ds(place, 1), :] * jnp.exp2((old_max - highest) * SCALE)
         return jnp.broadcast_to(highest, (8, BLOCK))
 
@@ -149,7 +160,7 @@
                 push(i + 2, parity)
             if j < LAG:
                 take(parity, j + CHUNKS - LAG, peak)
-                partial = add(1 - parity, j + CHUNKS - LAG, shift, partial)
+                partial = add(i - 1, 1 - parity, j + CHUNKS - LAG, shift, partial)
                 if j == LAG - 1:
                     fold(i - 1, partial)
                     shift = settle(i, peak)
@@ -157,7 +168,7 @@
                     partial = nothing
             else:
                 take(1 - parity, j - LAG, peak)
-                partial = add(parity, j - LAG, shift, partial)
+                partial = add(i, parity, j - LAG, shift, partial)
         return (*peak, shift, partial)
 
     push(0, 0)
@@ -178,7 +189,7 @@
     peak0, peak1, shift, partial = carry
     for j in range(LAG):
         take(0, j + CHUNKS - LAG, [peak0, peak1])
-        partial = add(1, j + CHUNKS - LAG, shift, partial)
+        partial = add(2 * turns - 1, 1, j + CHUNKS - LAG, shift, partial)
     fold(2 * turns - 1, partial)
     for m in range(2):
         pltpu.matmul_acc_lhs(mxus[m][0], jnp.zeros((CHUNK, 2 * LANES), bf16), load_staged_rhs=1)
@@ -198,15 +209,13 @@
     return jnp.where(mine, jnp.left_shift(jnp.ones_like(pair), number), 0).astype(f32)
 
 
-def first_rows(own_ref, by1_ref, by2_ref, by3_ref, shared_ref, potential_ref, out_ref, sources_ref, targets_ref, source_squares_ref, target_squares_ref, kept_ref, *scratch):
+def first_rows(own_ref, by1_ref, by2_ref, by3_ref, targets_ref, shared_ref, out_ref, sources_ref, source_squares_ref, target_squares_ref, kept_ref, *scratch):
     y, c = lax.axis_index("y"), lax.axis_index("c")
     kept = jnp.zeros((1, LANES), f32)
-    points = 2 * BLOCK
     for c_from in range(2):
-        lists = shared_ref[c_from, points:points + 16, :].astype(f32)
+        lists = shared_ref[c_from, 32:40, :]
         for by in range(4):
             kept = kept + bits(lists[by:by + 1, :], (y + 4 - by) & 3, c_from, y, c)
-        targets_ref[c_from * points:(c_from + 1) * points, :] = shared_ref[c_from, 0:points, :]
     kept_ref[...] = jnp.broadcast_to(kept, kept_ref.shape)
     for by, ref in enumerate((own_ref, by1_ref, by2_ref, by3_ref)):
         sources_ref[pl.ds(pl.multiple_of(((y + 4 - by) & 3) * BLOCK, BLOCK), BLOCK), :] = ref[0:BLOCK, :]
@@ -214,20 +223,25 @@
     squared = squares(targets_ref[...])
     target_squares_ref[...] = squared
     rows = pl.ds(pl.multiple_of(y * 8, 8), 8)
-    potential = jnp.concatenate([potential_ref[0, rows, :], potential_ref[1, rows, :]], axis=0)
+    potential = jnp.concatenate([shared_ref[0, rows, :], shared_ref[1, rows, :]], axis=0)
     bias = 0.5 * (potential - squared)
     half_step(kept_ref, targets_ref, sources_ref, bias, False, *scratch)
     spread_out(out_ref, scratch)
 
 
-def half_step(kept_pairs_ref, kept_ref, sum_ref, bias, kept_first, acc_max, acc_sum, even, odd, chosen):
-    clear(acc_max, acc_sum)
+def kept_pairs(kept_pairs_ref, chosen):
     kept = jnp.sum(kept_pairs_ref[0:1, :]).astype(jnp.int32)
     found = jnp.int32(0)
     for number in range(PAIRS_MAX):
         chosen[found] = number
         found = found + ((kept >> number) & 1)
-    sweep(chosen, found, kept_ref, sum_ref, bias, acc_max, acc_sum, even, odd, kept_first)
+    return kept, found
+
+
+def half_step(kept_pairs_ref, kept_ref, sum_ref, bias, kept_first, acc_max, acc_sum, even, odd, chosen, saved=None):
+    clear(acc_max, acc_sum)
+    _, found = kept_pairs(kept_pairs_ref, chosen)
+    sweep(chosen, found, kept_ref, sum_ref, bias, acc_max, acc_sum, even, odd, kept_first, saved)
 
 
 def spread_out(out_ref, scratch):
@@ -236,26 +250,108 @@
         out_ref[k] = dense
 
 
-def next_rows(kept_ref, sources_ref, targets_ref, parts_ref, out_ref, *scratch):
+def next_columns(kept_ref, sources_ref, targets_ref, parts_ref, out_ref, bias_ref, terms_ref, maxima_ref, *scratch):
     bias = half_bias(combined(parts_ref[...]))
-    half_step(kept_ref, targets_ref, sources_ref, bias, False, *scratch)
+    bias_ref[...] = bias
+    half_step(kept_ref, sources_ref, targets_ref, bias, True, *scratch, (terms_ref, maxima_ref))
     spread_out(out_ref, scratch)
 
 
-def next_columns(kept_ref, sources_ref, targets_ref, parts_ref, out_ref, *scratch):
-    bias = half_bias(combined(parts_ref[...]))
-    half_step(kept_ref, sources_ref, targets_ref, bias, True, *scratch)
-    spread_out(out_ref, scratch)
-
-
-def last_columns(kept_ref, sources_ref, targets_ref, source_squares_ref, target_squares_ref, parts_ref, out_ref, all_bias, *scratch):
+def in_kept_blocks(kept):
+    block = lax.broadcasted_iota(jnp.int32, (16, LANES), 0) >> 2
+    inside = jnp.zeros((16, LANES), jnp.int32)
+    for b in range(4):
+        inside = jnp.where(block == b, (kept >> (4 * b)) & 15, inside)
+    return inside > 0
+
+
+def any_of(condition):
+    return jnp.max(jnp.where(condition, 1.0, 0.0)) > 0.5
+
+
+def next_rows(kept_ref, sources_ref, targets_ref, old_bias_ref, terms_ref, maxima_ref, parts_ref, out_ref, acc_max, acc_sum, even, odd, chosen, rows_ref, lse_ref):
+    lse = combined(parts_ref[...])
+    kept, found = kept_pairs(kept_ref, chosen)
+    for b in range(4):
+        lse_ref[b:b + 1, :] = jnp.concatenate([lse[4 * b + q:4 * b + q + 1, :] for q in range(GROUPS)], axis=1)
+    rows_ref[...] = jnp.zeros(rows_ref.shape, f32)
+
+    def one(n, carry):
+        pair = chosen[n]
+        first, second = pair >> 2, pair & 3
+        weight = jnp.exp2(maxima_ref[pl.ds(n, 1), :] * SCALE - lse_ref[pl.ds(second, 1), :])
+        weight = jnp.broadcast_to(weight, (8, BLOCK))
+        for r in range(0, BLOCK, 8):
+            scaled = terms_ref[n, r:r + 8, :] * weight
+            total = (scaled[:, 0:LANES] + scaled[:, LANES:2 * LANES]) + (scaled[:, 2 * LANES:3 * LANES] + scaled[:, 3 * LANES:])
+            place = pl.ds(pl.multiple_of(first * BLOCK + r, 8), 8)
+            rows_ref[place, :] = rows_ref[place, :] + total
+        return carry
+
+    lax.fori_loop(0, found, one, 0)
+    total = rows_ref[...]
+    high = total.astype(bf16)
+    rest = total - high.astype(f32)
+    middle = rest.astype(bf16)
+    low = (rest - middle.astype(f32)).astype(bf16)
+    sums = lane_sums([high, middle, low, jnp.zeros_like(low)])
+    inside = in_kept_blocks(kept)
+    bad = any_of(inside & (sums < SMALLEST))
+    safe = jnp.where(inside, sums, 1.0)
+    dense = jnp.where(inside, jnp.log(safe) * LOG2E - SCALE * old_bias_ref[...] - LOG2_N, NEG_START)
+
+    @pl.when(jnp.logical_not(bad))
+    def _():
+        for k in range(out_ref.shape[0]):
+            out_ref[k] = dense
+
+    @pl.when(bad)
+    def _():
+        half_step(kept_ref, targets_ref, sources_ref, half_bias(lse), False, acc_max, acc_sum, even, odd, chosen)
+        spread_out(out_ref, (acc_max, acc_sum))
+
+
+def last_columns(kept_ref, sources_ref, targets_ref, source_squares_ref, target_squares_ref, old_bias_ref, terms_ref, maxima_ref, parts_ref, out_ref, all_bias, acc_max, acc_sum, even, odd, chosen, ratio_ref):
     bias = half_bias(combined(parts_ref[...]))
     all_bias[...] = bias
     own = all_bias[pl.ds(lax.axis_index("y") * GROUPS, GROUPS), :]
     out_ref[16:16 + GROUPS, :] = source_squares_ref[...] + 2.0 * own
     out_ref[16 + GROUPS:24, :] = jnp.zeros((8 - GROUPS, LANES), f32)
-    half_step(kept_ref, sources_ref, targets_ref, bias, True, *scratch)
-    out_ref[0:16, :] = finished(scratch[0], scratch[1]) - target_squares_ref[...] * (LOG2E / EPS_REG)
+    offset = target_squares_ref[...] * (LOG2E / EPS_REG)
+    kept, found = kept_pairs(kept_ref, chosen)
+    inside = in_kept_blocks(kept)
+    moved = SCALE * (bias - old_bias_ref[...])
+    largest = jnp.max(jnp.where(inside, moved, NEG_START))
+    bad = any_of(inside & (moved < largest - WIDEST))
+    ratio = jnp.exp2(jnp.where(inside, moved - largest, 0.0))
+
+    @pl.when(jnp.logical_not(bad))
+    def _():
+        for k in range(16):
+            ratio_ref[k * LANES:(k + 1) * LANES, :] = jnp.broadcast_to(ratio[k:k + 1, :], (LANES, LANES)).T
+        clear(acc_max, acc_sum)
+
+        def one(n, carry):
+            pair = chosen[n]
+            first, second = pair >> 2, pair & 3
+            partial = [jnp.zeros((8, BLOCK), f32), jnp.zeros((8, BLOCK), f32)]
+            for r in range(0, BLOCK, 8):
+                factor = ratio_ref[pl.ds(pl.multiple_of(first * BLOCK + r, 8), 8), :]
+                partial[r // 8 % 2] = partial[r // 8 % 2] + terms_ref[n, r:r + 8, :] * jnp.concatenate([factor] * GROUPS, axis=1)
+            block_sum = jnp.sum(partial[0] + partial[1], axis=0, keepdims=True)
+            highest = maxima_ref[pl.ds(n, 1), :]
+            old = jnp.exp2((acc_max[pl.ds(second, 1), :] - highest) * SCALE)
+            acc_sum[pl.ds(second, 1), :] = acc_sum[pl.ds(second, 1), :] * old + block_sum
+            acc_max[pl.ds(second, 1), :] = highest
+            return carry
+
+        lax.fori_loop(0, found, one, 0)
+        out_ref[0:16, :] = finished(acc_max, acc_sum) + largest - offset
+
+    @pl.when(bad)
+    def _():
+        half_step(kept_ref, sources_ref, targets_ref, bias, True, acc_max, acc_sum, even, odd, chosen)
+        out_ref[0:16, :] = finished(acc_max, acc_sum) - offset
 
 
 def both_cores(parts_ref, out_ref):
@@ -275,7 +371,7 @@
 
 
 VMEM = pl.BlockSpec(memory_space=pltpu.VMEM)
-PARAMS = pltpu.CompilerParams(vmem_limit_bytes=24 * 1024 * 1024)
+PARAMS = pltpu.CompilerParams(vmem_limit_bytes=8 * 1024 * 1024)
 WORK = [pltpu.VMEM((8, BLOCK), f32)] * 2 + [pltpu.VMEM((BLOCK, BLOCK), f32)] * 2 + [pltpu.SMEM((PAIRS_MAX,), jnp.int32)]
 
 
@@ -313,36 +409,43 @@
         lax.ppermute(sources, "y", [(i, (i + k) % n_y) for i in range(n_y)]) for k in range(1, n_y)
     ]
     targets = spread(jnp.broadcast_to(target_points[None], (n_z, own, EMB)), "z").reshape(n_z * own, EMB)
-    lists = [part[BLOCK:BLOCK + 1] for part in (sources, *by)]
-    targets = jnp.concatenate([targets, *lists, listed[4:]], axis=0)
-    targets = lax.all_gather(targets, "c")
-    potential = lax.all_gather(initial_potential.reshape(n_y * tgt_rows, LANES), "c")
+    lists = [part[BLOCK:BLOCK + 1].astype(f32) for part in (sources, *by)]
+    potential = initial_potential.reshape(n_y * tgt_rows, LANES)
+    shared = lax.all_gather(jnp.concatenate([potential, *lists, jnp.zeros((4, LANES), f32)], axis=0), "c")
+    targets = lax.all_gather(targets, "c", axis=0, tiled=True)
     row_shape = shape(16, 16, LANES)
-    row_parts, sources, targets, source_squares, target_squares, kept = call(
+    row_parts, sources, source_squares, target_squares, kept = call(
         first_rows,
         [
             row_shape,
             points(n_y * BLOCK, EMB),
-            points(2 * n_z * own, EMB),
             shape(GROUPS, LANES),
             shape(2 * tgt_rows, LANES),
             shape(8, LANES),
         ],
-        (sources, *by, targets, potential),
+        (sources, *by, targets, shared),
         WORK,
     )
-    for iteration in range(ITERS):
-        if iteration > 0:
-            row_parts = call(next_rows, row_shape, (kept, sources, targets, col_parts), WORK)
-        row_parts = spread(row_parts, ("y", "x"))
-        if iteration < ITERS - 1:
-            col_parts = call(next_columns, row_shape, (kept, sources, targets, row_parts), WORK)
-            col_parts = spread(col_parts, ("z", "c"))
+    row_parts = spread(row_parts, ("y", "x"))
+    col_parts, bias, terms, maxima = call(
+        next_columns,
+        [row_shape, shape(16, LANES), shape(PAIRS_MAX, BLOCK, BLOCK), shape(PAIRS_MAX, BLOCK)],
+        (kept, sources, targets, row_parts),
+        WORK,
+    )
+    col_parts = spread(col_parts, ("z", "c"))
+    row_parts = call(
+        next_rows,
+        row_shape,
+        (kept, sources, targets, bias, terms, maxima, col_parts),
+        WORK + [pltpu.VMEM((16 * LANES, LANES), f32), pltpu.VMEM((8, BLOCK), f32)],
+    )
+    row_parts = spread(row_parts, ("y", "x"))
     parts = call(
         last_columns,
         shape(24, LANES),
-        (kept, sources, targets, source_squares, target_squares, row_parts),
-        [pltpu.VMEM((16, LANES), f32)] + WORK,
+        (kept, sources, targets, source_squares, target_squares, bias, terms, maxima, row_parts),
+        [pltpu.VMEM((16, LANES), f32)] + WORK + [pltpu.VMEM((16 * LANES, LANES), f32)],
     )
     parts = lax.all_gather(parts, "c")
     col_parts = call(both_cores, shape(n_y * n_z, tgt_rows, LANES), (parts,), [])

time: 93 us -> 91.8 us (0.987)
  Pallas kernels: 10.8 us -> 7.84 us
  waiting for transfers between devices: 5.45 us -> 6.94 us
    all_to_all x1, waiting for transfers between devices: 0.01 us -> 6.93 us  [spread(): return lax.all_to_all(parts, axes, 0, 0, tiled=True)]
    ppermute x3, waiting for transfers between devices: 5.45 us -> 0.01 us  [per_device(): lax.ppermute(sources, 'y', [(i, (i + k) % n_y) for i in range(n_y)])]
    pallas_call x6, Pallas kernels: 10.8 us -> 7.84 us  [call(): pl.pallas_call(kernel, out_shape=out_shape, in_specs=[VMEM] * len(operand...]
  transfers between devices with their start and end apart: 4 -> 4, of which waited for: 3 -> 1; matrix products, arithmetic and copies ran while one was open for 0% -> 2% of each run, Pallas kernels for 0% -> 0%
where the time goes in v7:
time: 91.8 us; the launch traced here: 91.3 us
  blocking collectives  59.3 us (65%)
  starting transfers between devices  13.3 us (14%)
  Pallas kernels  7.84 us (9%)
  waiting for transfers between devices  6.94 us (8%)
  local copies, waits for them, and re-layouts  2.5 us (3%)
    all_to_all x4, blocking collectives, spread(): return lax.all_to_all(parts, axes, 0, 0, tiled=True)  53.5 us
    all_to_all x1, starting transfers between devices, spread(): return lax.all_to_all(parts, axes, 0, 0, tiled=True)  8.57 us
    pallas_call x6, Pallas kernels, call(): pl.pallas_call(kernel, out_shape=out_shape, in_specs=[VMEM] * len(operand...  7.84 us
    all_to_all x1, waiting for transfers between devices, spread(): return lax.all_to_all(parts, axes, 0, 0, tiled=True)  6.93 us
    ppermute x3, starting transfers between devices, per_device(): lax.ppermute(sources, 'y', [(i, (i + k) % n_y) for i in range(n_y)])  4.69 us
    all_gather x1, blocking collectives, per_device(): targets = lax.all_gather(targets, 'c', axis=0, tiled=True)  2.17 us
  transfers between devices with their start and end apart: 4, of which 1 were waited for; matrix products, arithmetic and copies ran while one was open for 2% of the time, Pallas kernels for 0%

profile of v7, /device:TPU:32, one launch (start us, length us, event | category | flops | bytes accessed | tf_op | source)
XLA Modules:
  0.0 91.3 jit_solution(476472410275742811)
XLA Ops:
  0.6 0.0 copy-start
  0.6 0.7 convert_bitcast_fusion
  1.4 0.2 copy-done
  1.6 3.1 %collective-permute-start.2 = (bf16[528,128]{1,0:T(8,128)(2,1)S(1)}, bf16[528,128]{1,0:T(8,128)(2,1)S(1)}, u32[]{:S(2)}, u32[]{:S(2)}) collective-permute-start(bf16[528,128]{1,0:T(8,128)(2,1)S(1)} %pad_maximum_fusion.own_ref), channel_id=1, source_target_pairs={{0,192},{64,0},{128,64},{192,128},{1,193},{65,1},{129,65},{193,129... | collective-permute-start | bytes 405512 | tf_op jit(solution)/shard_map/ppermute | solution.py:409
  4.7 0.6 collective-permute-start.1
  5.4 1.0 %collective-permute-start = (bf16[528,128]{1,0:T(8,128)(2,1)S(1)}, bf16[528,128]{1,0:T(8,128)(2,1)S(1)}, u32[]{:S(2)}, u32[]{:S(2)}) collective-permute-start(bf16[528,128]{1,0:T(8,128)(2,1)S(1)} %pad_maximum_fusion.own_ref), channel_id=1, source_target_pairs={{0,64},{64,128},{128,192},{192,0},{1,65},{65,129},{129,193},{193,1... | collective-permute-start | bytes 405512 | tf_op jit(solution)/shard_map/ppermute | solution.py:409
  6.3 1.5 %broadcast_in_dim.4 = bf16[8,128,128]{2,1,0:T(8,128)(2,1)} broadcast(bf16[128,128]{1,0:T(8,128)(2,1)} %param.6), dimensions={1,2} | broadcast | bytes 294912 | tf_op jit(solution)/shard_map/broadcast_in_dim | solution.py:411
  7.8 8.6 %all-to-all-start = ((bf16[8,128,128]{2,1,0:T(8,128)(2,1)}), bf16[8,128,128]{2,1,0:T(8,128)(2,1)S(1)}, u32[]{:S(2)}, u32[]{:S(2)}) async-start(bf16[8,128,128]{2,1,0:T(8,128)(2,1)} %broadcast_in_dim.4), calls=%async_computation | async-start | bytes 524288 | tf_op jit(solution)/shard_map/all_to_all | solution.py:379
  16.4 0.0 collective-permute-done.2.by3_ref
  16.4 0.0 collective-permute-done.1.by2_ref
  16.4 0.0 collective-permute-done.by1_ref
  16.5 0.7 concatenate.7
  17.2 1.8 %all-gather = f32[80,128]{1,0:T(8,128)S(1)} all-gather(f32[40,128]{1,0:T(8,128)S(1)} %concatenate.7), channel_id=2, replica_groups=mesh['y'=4,'z'=8,'x'=4,'c'=2] {'c'}, dimensions={0}, use_global_device_ids=true | all-gather | bytes 61440 | tf_op jit(solution)/shard_map/all_gather | solution.py:414
  19.0 6.9 %all-to-all-done = bf16[8,128,128]{2,1,0:T(8,128)(2,1)S(1)} async-done(((bf16[8,128,128]{2,1,0:T(8,128)(2,1)}), bf16[8,128,128]{2,1,0:T(8,128)(2,1)S(1)}, u32[]{:S(2)}, u32[]{:S(2)}) %all-to-all-start) | async-done | bytes 262176 | tf_op jit(solution)/shard_map/all_to_all | solution.py:379
  26.0 2.2 %all_gather.15.targets_ref = bf16[2048,128]{1,0:T(8,128)(2,1)S(1)} all-gather(bf16[1024,128]{1,0:T(8,128)(2,1)S(1)} %bitcast.11), channel_id=1, replica_groups=mesh['y'=4,'z'=8,'x'=4,'c'=2] {'c'}, dimensions={0}, use_global_device_ids=true | all-gather | bytes 786432 | tf_op jit(solution)/shard_map/all_gather | solution.py:415
  28.1 2.3 %shard_map.59 = (f32[16,16,128]{2,1,0:T(8,128)S(1)}, bf16[2048,128]{1,0:T(8,128)(2,1)S(1)}, f32[4,128]{1,0:T(4,128)S(1)}, f32[16,128]{1,0:T(8,128)S(1)}, f32[8,128]{1,0:T(8,128)S(1)}) custom-call(bf16[528,128]{1,0:T(8,128)(2,1)S(1)} %pad_maximum_fusion.own_ref, bf16[528,128]{1,0:T(8,128)(2,1)S(1)} %collective-permute-done.by1_ref, ...), custom_call_target="tpu_custom_call" | custom-call | flops 1073741824 | bytes 4194304 | tf_op jit(solution)/shard_map/pallas_call | solution.py:383
  30.4 14.9 %all_to_all.25.parts_ref = f32[16,16,128]{2,1,0:T(8,128)S(1)} all-to-all(f32[16,16,128]{2,1,0:T(8,128)S(1)} %get-tuple-element.17), channel_id=1, replica_groups=mesh['y'=4,'z'=8,'x'=4,'c'=2] {'y','x'}, dimensions={0} | all-to-all | bytes 262144 | tf_op jit(solution)/shard_map/all_to_all | solution.py:379
  45.3 2.1 %shard_map.60 = (f32[16,16,128]{2,1,0:T(8,128)S(1)}, f32[16,128]{1,0:T(8,128)S(1)}, f32[16,512,512]{2,1,0:T(8,128)S(1)}, f32[16,512]{1,0:T(8,128)S(1)}) custom-call(f32[8,128]{1,0:T(8,128)S(1)} %get-tuple-element.13.kept_ref, bf16[2048,128]{1,0:T(8,128)(2,1)S(1)} %get-tuple-element.14.sources_ref, bf16[2048,128]{1,0:T(8,128)(2,1)S(1)} %all_gather.15.targets_ref, ...), custom_call_target="tpu_custom_call" | custom-call | flops 1073741824 | bytes 4194304 | tf_op jit(solution)/shard_map/pallas_call | solution.py:383
  47.4 11.6 %all_to_all.26.parts_ref = f32[16,16,128]{2,1,0:T(8,128)S(1)} all-to-all(f32[16,16,128]{2,1,0:T(8,128)S(1)} %get-tuple-element.21), channel_id=1, replica_groups=mesh['y'=4,'z'=8,'x'=4,'c'=2] {'z','c'}, dimensions={0} | all-to-all | bytes 262144 | tf_op jit(solution)/shard_map/all_to_all | solution.py:379
  59.0 1.5 %shard_map.61 = f32[16,16,128]{2,1,0:T(8,128)S(1)} custom-call(f32[8,128]{1,0:T(8,128)S(1)} %get-tuple-element.13.kept_ref, bf16[2048,128]{1,0:T(8,128)(2,1)S(1)} %get-tuple-element.14.sources_ref, bf16[2048,128]{1,0:T(8,128)(2,1)S(1)} %all_gather.15.targets_ref, f32[16,128]{1,0:T(8,128)S(1)} %get-tuple-element.18.old_bias_ref, ...), custom_call_target="tpu_custom_call" | custom-call | flops 1073741824 | bytes 4194304 | tf_op jit(solution)/shard_map/pallas_call | solution.py:383
  60.4 12.0 %all_to_all.27.parts_ref = f32[16,16,128]{2,1,0:T(8,128)S(1)} all-to-all(f32[16,16,128]{2,1,0:T(8,128)S(1)} %shard_map.61), channel_id=1, replica_groups=mesh['y'=4,'z'=8,'x'=4,'c'=2] {'y','x'}, dimensions={0} | all-to-all | bytes 262144 | tf_op jit(solution)/shard_map/all_to_all | solution.py:379
  72.4 1.4 %shard_map.62 = f32[24,128]{1,0:T(8,128)S(1)} custom-call(f32[8,128]{1,0:T(8,128)S(1)} %get-tuple-element.13.kept_ref, bf16[2048,128]{1,0:T(8,128)(2,1)S(1)} %get-tuple-element.14.sources_ref, bf16[2048,128]{1,0:T(8,128)(2,1)S(1)} %all_gather.15.targets_ref, f32[4,128]{1,0:T(4,128)S(1)} %get-tuple-element.15.source_squares_ref, ...), custom_call_target="tpu_custom_call" | custom-call | flops 1073741824 | bytes 4194304 | tf_op jit(solution)/shard_map/pallas_call | solution.py:383
  73.8 1.8 %all-gather.1 = f32[48,128]{1,0:T(8,128)S(1)} all-gather(f32[24,128]{1,0:T(8,128)S(1)} %shard_map.62), channel_id=3, replica_groups=mesh['y'=4,'z'=8,'x'=4,'c'=2] {'c'}, dimensions={0}, use_global_device_ids=true | all-gather | bytes 36864 | tf_op jit(solution)/shard_map/all_gather | solution.py:450
  75.7 15.0 %all_to_all.28.parts_ref = f32[32,8,128]{2,1,0:T(8,128)S(1)} all-to-all(f32[32,8,128]{2,1,0:T(8,128)S(1)} %shard_map.63), channel_id=1, replica_groups=mesh['y'=4,'z'=8,'x'=4,'c'=2] {'y','z'}, dimensions={0} | all-to-all | bytes 262144 | tf_op jit(solution)/shard_map/all_to_all | solution.py:379
  90.7 0.7 shard_map.64
  (9 shorter events, 0.1 us)
Async XLA Ops:
  0.6 1.0 %copy-start = (bf16[1024,128]{1,0:T(8,128)(2,1)S(1)}, bf16[1024,128]{1,0:T(8,128)(2,1)}, u32[]{:S(2)}) copy-start(bf16[1024,128]{1,0:T(8,128)(2,1)} %param.5) | copy-start | bytes 786436
  1.6 14.8 %collective-permute-start.2 = (bf16[528,128]{1,0:T(8,128)(2,1)S(1)}, bf16[528,128]{1,0:T(8,128)(2,1)S(1)}, u32[]{:S(2)}, u32[]{:S(2)}) collective-permute-start(bf16[528,128]{1,0:T(8,128)(2,1)S(1)} %pad_maximum_fusion.own_ref), channel_id=1, source_target_pairs={{0,192},{64,0},{128,64},{192,128},{1,193},{65,1},{129,65},{193,129... | collective-permute-start | bytes 405512 | tf_op jit(solution)/shard_map/ppermute | solution.py:409
  4.7 11.7 %collective-permute-start.1 = (bf16[528,128]{1,0:T(8,128)(2,1)S(1)}, bf16[528,128]{1,0:T(8,128)(2,1)S(1)}, u32[]{:S(2)}, u32[]{:S(2)}) collective-permute-start(bf16[528,128]{1,0:T(8,128)(2,1)S(1)} %pad_maximum_fusion.own_ref), channel_id=1, source_target_pairs={{0,128},{64,192},{128,0},{192,64},{1,129},{65,193},{129,1},{193,65... | collective-permute-start | bytes 405512 | tf_op jit(solution)/shard_map/ppermute | solution.py:409
  5.4 11.1 %collective-permute-start = (bf16[528,128]{1,0:T(8,128)(2,1)S(1)}, bf16[528,128]{1,0:T(8,128)(2,1)S(1)}, u32[]{:S(2)}, u32[]{:S(2)}) collective-permute-start(bf16[528,128]{1,0:T(8,128)(2,1)S(1)} %pad_maximum_fusion.own_ref), channel_id=1, source_target_pairs={{0,64},{64,128},{128,192},{192,0},{1,65},{65,129},{129,193},{193,1... | collective-permute-start | bytes 405512 | tf_op jit(solution)/shard_map/ppermute | solution.py:409
  7.8 18.1 %all-to-all-start = ((bf16[8,128,128]{2,1,0:T(8,128)(2,1)}), bf16[8,128,128]{2,1,0:T(8,128)(2,1)S(1)}, u32[]{:S(2)}, u32[]{:S(2)}) async-start(bf16[8,128,128]{2,1,0:T(8,128)(2,1)} %broadcast_in_dim.4), calls=%async_computation | async-start | bytes 524288 | tf_op jit(solution)/shard_map/all_to_all | solution.py:379

commit v8 on v7

--- a/solution.py
+++ b/solution.py
@@ -97,7 +97,7 @@
 
     def where(number):
         real = number < count
-        pair = jnp.where(real, pairs_ref[jnp.minimum(number, PAIRS_MAX - 1)], 0)
+        pair = jnp.where(real, pairs_ref[jnp.clip(number, 0, PAIRS_MAX - 1)], 0)
         first, second = pair >> 2, pair & 3
         return (first, second) if kept_first else (second, first)
 
@@ -209,11 +209,16 @@
     return jnp.where(mine, jnp.left_shift(jnp.ones_like(pair), number), 0).astype(f32)
 
 
-def first_rows(own_ref, by1_ref, by2_ref, by3_ref, targets_ref, shared_ref, out_ref, sources_ref, source_squares_ref, target_squares_ref, kept_ref, *scratch):
+def packed(own_ref, by1_ref, by2_ref, by3_ref, after_ref, out_ref):
+    lists = [ref[BLOCK:BLOCK + 16, :].astype(f32)[0:1, :] for ref in (own_ref, by1_ref, by2_ref, by3_ref)]
+    out_ref[...] = jnp.concatenate(lists + [jnp.zeros((4, LANES), f32)], axis=0)
+
+
+def first_rows(own_ref, by1_ref, by2_ref, by3_ref, targets_ref, lists_ref, potential_ref, out_ref, sources_ref, source_squares_ref, target_squares_ref, kept_ref, *scratch):
     y, c = lax.axis_index("y"), lax.axis_index("c")
     kept = jnp.zeros((1, LANES), f32)
     for c_from in range(2):
-        lists = shared_ref[c_from, 32:40, :]
+        lists = lists_ref[c_from]
         for by in range(4):
             kept = kept + bits(lists[by:by + 1, :], (y + 4 - by) & 3, c_from, y, c)
     kept_ref[...] = jnp.broadcast_to(kept, kept_ref.shape)
@@ -223,7 +228,7 @@
     squared = squares(targets_ref[...])
     target_squares_ref[...] = squared
     rows = pl.ds(pl.multiple_of(y * 8, 8), 8)
-    potential = jnp.concatenate([shared_ref[0, rows, :], shared_ref[1, rows, :]], axis=0)
+    potential = jnp.concatenate([potential_ref[0, rows, :], potential_ref[1, rows, :]], axis=0)
     bias = 0.5 * (potential - squared)
     half_step(kept_ref, targets_ref, sources_ref, bias, False, *scratch)
     spread_out(out_ref, scratch)
@@ -292,9 +297,7 @@
     total = rows_ref[...]
     high = total.astype(bf16)
     rest = total - high.astype(f32)
-    middle = rest.astype(bf16)
-    low = (rest - middle.astype(f32)).astype(bf16)
-    sums = lane_sums([high, middle, low, jnp.zeros_like(low)])
+    sums = lane_sums([high, rest.astype(bf16)])
     inside = in_kept_blocks(kept)
     bad = any_of(inside & (sums < SMALLEST))
     safe = jnp.where(inside, sums, 1.0)
@@ -371,7 +374,7 @@
 
 
 VMEM = pl.BlockSpec(memory_space=pltpu.VMEM)
-PARAMS = pltpu.CompilerParams(vmem_limit_bytes=8 * 1024 * 1024)
+PARAMS = pltpu.CompilerParams(vmem_limit_bytes=24 * 1024 * 1024)
 WORK = [pltpu.VMEM((8, BLOCK), f32)] * 2 + [pltpu.VMEM((BLOCK, BLOCK), f32)] * 2 + [pltpu.SMEM((PAIRS_MAX,), jnp.int32)]
 
 
@@ -409,10 +412,9 @@
         lax.ppermute(sources, "y", [(i, (i + k) % n_y) for i in range(n_y)]) for k in range(1, n_y)
     ]
     targets = spread(jnp.broadcast_to(target_points[None], (n_z, own, EMB)), "z").reshape(n_z * own, EMB)
-    lists = [part[BLOCK:BLOCK + 1].astype(f32) for part in (sources, *by)]
-    potential = initial_potential.reshape(n_y * tgt_rows, LANES)
-    shared = lax.all_gather(jnp.concatenate([potential, *lists, jnp.zeros((4, LANES), f32)], axis=0), "c")
     targets = lax.all_gather(targets, "c", axis=0, tiled=True)
+    potential = lax.all_gather(initial_potential.reshape(n_y * tgt_rows, LANES), "c")
+    lists = lax.all_gather(call(packed, shape(8, LANES), (sources, *by, targets), []), "c")
     row_shape = shape(16, 16, LANES)
     row_parts, sources, source_squares, target_squares, kept = call(
         first_rows,
@@ -423,7 +425,7 @@
             shape(2 * tgt_rows, LANES),
             shape(8, LANES),
         ],
-        (sources, *by, targets, shared),
+        (sources, *by, targets, lists, potential),
         WORK,
     )
     row_parts = spread(row_parts, ("y", "x"))

time: 91.8 us -> 89.8 us (0.978)
  waiting for transfers between devices: 6.94 us -> 3.08 us
  Pallas kernels: 7.84 us -> 10.2 us
  local copies, waits for them, and re-layouts: 2.5 us -> 1.55 us
    all_to_all x1, waiting for transfers between devices: 6.93 us -> 3.01 us  [spread(): return lax.all_to_all(parts, axes, 0, 0, tiled=True)]
    pallas_call x6 -> x7, Pallas kernels: 7.84 us -> 10.2 us  [call(): pl.pallas_call(kernel, out_shape=out_shape, in_specs=[VMEM] * len(operand...]
    all_gather x1 -> x2, blocking collectives: 1.83 us -> 3.82 us  [the longest x1 2.03 us: per_device(): lax.all_gather(initial_potential.reshape(n_y * tgt_rows, LANES), 'c')]
    all_to_all x4, blocking collectives: 53.5 us -> 51.8 us  [spread(): return lax.all_to_all(parts, axes, 0, 0, tiled=True)]
  transfers between devices with their start and end apart: 4 -> 4, of which waited for: 1 -> 2; matrix products, arithmetic and copies ran while one was open for 2% -> 1% of each run, Pallas kernels for 0% -> 0%
where the time goes in v8:
time: 89.8 us; the launch traced here: 89.1 us
  blocking collectives  59.6 us (66%)
  starting transfers between devices  13.3 us (15%)
  Pallas kernels  10.2 us (11%)
  waiting for transfers between devices  3.08 us (3%)
  local copies, waits for them, and re-layouts  1.55 us (2%)
    all_to_all x4, blocking collectives, spread(): return lax.all_to_all(parts, axes, 0, 0, tiled=True)  51.8 us
    pallas_call x7, Pallas kernels, call(): pl.pallas_call(kernel, out_shape=out_shape, in_specs=[VMEM] * len(operand...  10.2 us
    all_to_all x1, starting transfers between devices, spread(): return lax.all_to_all(parts, axes, 0, 0, tiled=True)  8.57 us
    ppermute x3, starting transfers between devices, per_device(): lax.ppermute(sources, 'y', [(i, (i + k) % n_y) for i in range(n_y)])  4.69 us
    all_to_all x1, waiting for transfers between devices, spread(): return lax.all_to_all(parts, axes, 0, 0, tiled=True)  3.01 us
    all_gather x1, blocking collectives, per_device(): targets = lax.all_gather(targets, 'c', axis=0, tiled=True)  2.17 us
    all_gather x1, blocking collectives, per_device(): lax.all_gather(initial_potential.reshape(n_y * tgt_rows, LANES), 'c')  2.03 us
    all_gather x1, blocking collectives, per_device(): parts = lax.all_gather(parts, 'c')  1.82 us
  transfers between devices with their start and end apart: 4, of which 2 were waited for; matrix products, arithmetic and copies ran while one was open for 1% of the time, Pallas kernels for 0%

profile of v8, /device:TPU:32, one launch (start us, length us, event | category | flops | bytes accessed | tf_op | source)
XLA Modules:
  0.0 89.1 jit_solution(5394632544894990954)
XLA Ops:
  0.6 0.0 copy-start
  0.6 1.5 %broadcast_in_dim.2 = bf16[8,128,128]{2,1,0:T(8,128)(2,1)} broadcast(bf16[128,128]{1,0:T(8,128)(2,1)} %param.6), dimensions={1,2} | broadcast | bytes 294912 | tf_op jit(solution)/shard_map/broadcast_in_dim | solution.py:414
  2.2 8.6 %all-to-all-start = ((bf16[8,128,128]{2,1,0:T(8,128)(2,1)}), bf16[8,128,128]{2,1,0:T(8,128)(2,1)S(1)}, u32[]{:S(2)}, u32[]{:S(2)}) async-start(bf16[8,128,128]{2,1,0:T(8,128)(2,1)} %broadcast_in_dim.2), calls=%async_computation | async-start | bytes 524288 | tf_op jit(solution)/shard_map/all_to_all | solution.py:382
  10.7 0.0 copy-done
  10.8 0.7 convert_bitcast_fusion
  11.4 3.1 %collective-permute-start.2 = (bf16[528,128]{1,0:T(8,128)(2,1)S(1)}, bf16[528,128]{1,0:T(8,128)(2,1)S(1)}, u32[]{:S(2)}, u32[]{:S(2)}) collective-permute-start(bf16[528,128]{1,0:T(8,128)(2,1)S(1)} %fusion.1.own_ref), channel_id=1, source_target_pairs={{0,192},{64,0},{128,64},{192,128},{1,193},{65,1},{129,65},{193,129... | collective-permute-start | bytes 405512 | tf_op jit(solution)/shard_map/ppermute | solution.py:412
  14.5 0.6 collective-permute-start.1
  15.2 1.0 %collective-permute-start = (bf16[528,128]{1,0:T(8,128)(2,1)S(1)}, bf16[528,128]{1,0:T(8,128)(2,1)S(1)}, u32[]{:S(2)}, u32[]{:S(2)}) collective-permute-start(bf16[528,128]{1,0:T(8,128)(2,1)S(1)} %fusion.1.own_ref), channel_id=1, source_target_pairs={{0,64},{64,128},{128,192},{192,0},{1,65},{65,129},{129,193},{193,1... | collective-permute-start | bytes 405512 | tf_op jit(solution)/shard_map/ppermute | solution.py:412
  16.1 2.0 %all_gather.21.potential_ref = f32[2,32,128]{2,1,0:T(8,128)S(1)} all-gather(f32[1,32,128]{2,1,0:T(8,128)} %bitcast.12), channel_id=1, replica_groups=mesh['y'=4,'z'=8,'x'=4,'c'=2] {'c'}, dimensions={0}, use_global_device_ids=true | all-gather | bytes 49152 | tf_op jit(solution)/shard_map/all_gather | solution.py:416
  18.2 3.0 %all-to-all-done = bf16[8,128,128]{2,1,0:T(8,128)(2,1)S(1)} async-done(((bf16[8,128,128]{2,1,0:T(8,128)(2,1)}), bf16[8,128,128]{2,1,0:T(8,128)(2,1)S(1)}, u32[]{:S(2)}, u32[]{:S(2)}) %all-to-all-start) | async-done | bytes 262176 | tf_op jit(solution)/shard_map/all_to_all | solution.py:382
  21.2 2.2 %all_gather.18.after_ref.targets_ref = bf16[2048,128]{1,0:T(8,128)(2,1)S(1)} all-gather(bf16[1024,128]{1,0:T(8,128)(2,1)S(1)} %bitcast.11), channel_id=1, replica_groups=mesh['y'=4,'z'=8,'x'=4,'c'=2] {'c'}, dimensions={0}, use_global_device_ids=true | all-gather | bytes 786432 | tf_op jit(solution)/shard_map/all_gather | solution.py:415
  23.3 0.0 collective-permute-done.2.by3_ref
  23.3 0.0 collective-permute-done.1.by2_ref
  23.3 0.1 collective-permute-done.by1_ref
  23.4 1.8 %all-gather = f32[16,128]{1,0:T(8,128)S(1)} all-gather(f32[8,128]{1,0:T(8,128)S(1)} %shard_map.59), channel_id=2, replica_groups=mesh['y'=4,'z'=8,'x'=4,'c'=2] {'c'}, dimensions={0}, use_global_device_ids=true | all-gather | bytes 12288 | tf_op jit(solution)/shard_map/all_gather | solution.py:417
  25.2 3.2 %shard_map.60 = (f32[16,16,128]{2,1,0:T(8,128)S(1)}, bf16[2048,128]{1,0:T(8,128)(2,1)S(1)}, f32[4,128]{1,0:T(4,128)S(1)}, f32[16,128]{1,0:T(8,128)S(1)}, f32[8,128]{1,0:T(8,128)S(1)}) custom-call(bf16[528,128]{1,0:T(8,128)(2,1)S(1)} %fusion.1.own_ref, bf16[528,128]{1,0:T(8,128)(2,1)S(1)} %collective-permute-done.by1_ref, ...), custom_call_target="tpu_custom_call" | custom-call | flops 1073741824 | bytes 4194304 | tf_op jit(solution)/shard_map/pallas_call | solution.py:386
  28.4 13.8 %all_to_all.25.parts_ref = f32[16,16,128]{2,1,0:T(8,128)S(1)} all-to-all(f32[16,16,128]{2,1,0:T(8,128)S(1)} %get-tuple-element.17), channel_id=1, replica_groups=mesh['y'=4,'z'=8,'x'=4,'c'=2] {'y','x'}, dimensions={0} | all-to-all | bytes 262144 | tf_op jit(solution)/shard_map/all_to_all | solution.py:382
  42.3 3.0 %shard_map.61 = (f32[16,16,128]{2,1,0:T(8,128)S(1)}, f32[16,128]{1,0:T(8,128)S(1)}, f32[16,512,512]{2,1,0:T(8,128)S(1)}, f32[16,512]{1,0:T(8,128)S(1)}) custom-call(f32[8,128]{1,0:T(8,128)S(1)} %get-tuple-element.13.kept_ref, bf16[2048,128]{1,0:T(8,128)(2,1)S(1)} %get-tuple-element.14.sources_ref, bf16[2048,128]{1,0:T(8,128)(2,1)S(1)} %all_gather.18.after_ref.targets_ref, ...), custom_call_target="tpu_custom_call" | custom-call | flops 1073741824 | bytes 4194304 | tf_op jit(solution)/shard_map/pallas_call | solution.py:386
  45.3 11.2 %all_to_all.26.parts_ref = f32[16,16,128]{2,1,0:T(8,128)S(1)} all-to-all(f32[16,16,128]{2,1,0:T(8,128)S(1)} %get-tuple-element.21), channel_id=1, replica_groups=mesh['y'=4,'z'=8,'x'=4,'c'=2] {'z','c'}, dimensions={0} | all-to-all | bytes 262144 | tf_op jit(solution)/shard_map/all_to_all | solution.py:382
  56.4 1.5 %shard_map.62 = f32[16,16,128]{2,1,0:T(8,128)S(1)} custom-call(f32[8,128]{1,0:T(8,128)S(1)} %get-tuple-element.13.kept_ref, bf16[2048,128]{1,0:T(8,128)(2,1)S(1)} %get-tuple-element.14.sources_ref, bf16[2048,128]{1,0:T(8,128)(2,1)S(1)} %all_gather.18.after_ref.targets_ref, f32[16,128]{1,0:T(8,128)S(1)} %get-tuple-element.18.old_bias_ref, ...), custom_call_target="tpu_custom_call" | custom-call | flops 1073741824 | bytes 4194304 | tf_op jit(solution)/shard_map/pallas_call | solution.py:386
  58.0 11.9 %all_to_all.27.parts_ref = f32[16,16,128]{2,1,0:T(8,128)S(1)} all-to-all(f32[16,16,128]{2,1,0:T(8,128)S(1)} %shard_map.62), channel_id=1, replica_groups=mesh['y'=4,'z'=8,'x'=4,'c'=2] {'y','x'}, dimensions={0} | all-to-all | bytes 262144 | tf_op jit(solution)/shard_map/all_to_all | solution.py:382
  69.9 1.8 %shard_map.63 = f32[24,128]{1,0:T(8,128)S(1)} custom-call(f32[8,128]{1,0:T(8,128)S(1)} %get-tuple-element.13.kept_ref, bf16[2048,128]{1,0:T(8,128)(2,1)S(1)} %get-tuple-element.14.sources_ref, bf16[2048,128]{1,0:T(8,128)(2,1)S(1)} %all_gather.18.after_ref.targets_ref, f32[4,128]{1,0:T(4,128)S(1)} %get-tuple-element.15.source_squares_ref, ...), custom_call_target="tpu_custom_call" | custom-call | flops 1073741824 | bytes 4194304 | tf_op jit(solution)/shard_map/pallas_call | solution.py:386
  71.7 1.8 %all-gather.1 = f32[48,128]{1,0:T(8,128)S(1)} all-gather(f32[24,128]{1,0:T(8,128)S(1)} %shard_map.63), channel_id=3, replica_groups=mesh['y'=4,'z'=8,'x'=4,'c'=2] {'c'}, dimensions={0}, use_global_device_ids=true | all-gather | bytes 36864 | tf_op jit(solution)/shard_map/all_gather | solution.py:452
  73.5 14.9 %all_to_all.28.parts_ref = f32[32,8,128]{2,1,0:T(8,128)S(1)} all-to-all(f32[32,8,128]{2,1,0:T(8,128)S(1)} %shard_map.64), channel_id=1, replica_groups=mesh['y'=4,'z'=8,'x'=4,'c'=2] {'y','z'}, dimensions={0} | all-to-all | bytes 262144 | tf_op jit(solution)/shard_map/all_to_all | solution.py:382
  88.5 0.7 shard_map.65
  (4 shorter events, 0.1 us)
Async XLA Ops:
  0.6 10.1 %copy-start = (bf16[1024,128]{1,0:T(8,128)(2,1)S(1)}, bf16[1024,128]{1,0:T(8,128)(2,1)}, u32[]{:S(2)}) copy-start(bf16[1024,128]{1,0:T(8,128)(2,1)} %param.5) | copy-start | bytes 786436
  2.2 19.0 %all-to-all-start = ((bf16[8,128,128]{2,1,0:T(8,128)(2,1)}), bf16[8,128,128]{2,1,0:T(8,128)(2,1)S(1)}, u32[]{:S(2)}, u32[]{:S(2)}) async-start(bf16[8,128,128]{2,1,0:T(8,128)(2,1)} %broadcast_in_dim.2), calls=%async_computation | async-start | bytes 524288 | tf_op jit(solution)/shard_map/all_to_all | solution.py:382
  11.4 11.9 %collective-permute-start.2 = (bf16[528,128]{1,0:T(8,128)(2,1)S(1)}, bf16[528,128]{1,0:T(8,128)(2,1)S(1)}, u32[]{:S(2)}, u32[]{:S(2)}) collective-permute-start(bf16[528,128]{1,0:T(8,128)(2,1)S(1)} %fusion.1.own_ref), channel_id=1, source_target_pairs={{0,192},{64,0},{128,64},{192,128},{1,193},{65,1},{129,65},{193,129... | collective-permute-start | bytes 405512 | tf_op jit(solution)/shard_map/ppermute | solution.py:412
  14.5 8.8 %collective-permute-start.1 = (bf16[528,128]{1,0:T(8,128)(2,1)S(1)}, bf16[528,128]{1,0:T(8,128)(2,1)S(1)}, u32[]{:S(2)}, u32[]{:S(2)}) collective-permute-start(bf16[528,128]{1,0:T(8,128)(2,1)S(1)} %fusion.1.own_ref), channel_id=1, source_target_pairs={{0,128},{64,192},{128,0},{192,64},{1,129},{65,193},{129,1},{193,65... | collective-permute-start | bytes 405512 | tf_op jit(solution)/shard_map/ppermute | solution.py:412
  15.2 8.3 %collective-permute-start = (bf16[528,128]{1,0:T(8,128)(2,1)S(1)}, bf16[528,128]{1,0:T(8,128)(2,1)S(1)}, u32[]{:S(2)}, u32[]{:S(2)}) collective-permute-start(bf16[528,128]{1,0:T(8,128)(2,1)S(1)} %fusion.1.own_ref), channel_id=1, source_target_pairs={{0,64},{64,128},{128,192},{192,0},{1,65},{65,129},{129,193},{193,1... | collective-permute-start | bytes 405512 | tf_op jit(solution)/shard_map/ppermute | solution.py:412

commit v9 on v8

--- a/solution.py
+++ b/solution.py
@@ -184,16 +184,28 @@
     def turn(k, carry):
         return body(2 * k + 1, 1, body(2 * k, 0, carry))
 
-    turns = (count + 1) >> 1
+    def close(last, parity, carry):
+        *_, shift, partial = carry
+        for j in range(LAG):
+            for m in range(2):
+                pltpu.matmul_pop(mxus[m][j + CHUNKS - LAG])
+            partial = add(last, parity, j + CHUNKS - LAG, shift, partial)
+        fold(last, partial)
+        for m in range(2):
+            pltpu.matmul_acc_lhs(mxus[m][0], jnp.zeros((CHUNK, 2 * LANES), bf16), load_staged_rhs=parity)
+            pltpu.matmul_pop(mxus[m][0])
+
+    turns = count >> 1
     carry = lax.fori_loop(0, turns, turn, (*peak, nothing, nothing))
-    peak0, peak1, shift, partial = carry
-    for j in range(LAG):
-        take(0, j + CHUNKS - LAG, [peak0, peak1])
-        partial = add(2 * turns - 1, 1, j + CHUNKS - LAG, shift, partial)
-    fold(2 * turns - 1, partial)
-    for m in range(2):
-        pltpu.matmul_acc_lhs(mxus[m][0], jnp.zeros((CHUNK, 2 * LANES), bf16), load_staged_rhs=1)
-        pltpu.matmul_pop(mxus[m][0])
+    odd_count = (count & 1) == 1
+
+    @pl.when(odd_count)
+    def _():
+        close(count - 1, 0, body(count - 1, 0, carry))
+
+    @pl.when(jnp.logical_not(odd_count))
+    def _():
+        close(count - 1, 1, carry)
 
 
 def finished(acc_max, acc_sum):
@@ -209,23 +221,25 @@
     return jnp.where(mine, jnp.left_shift(jnp.ones_like(pair), number), 0).astype(f32)
 
 
-def packed(own_ref, by1_ref, by2_ref, by3_ref, after_ref, out_ref):
+def packed(own_ref, by1_ref, by2_ref, by3_ref, targets_ref, out_ref):
     lists = [ref[BLOCK:BLOCK + 16, :].astype(f32)[0:1, :] for ref in (own_ref, by1_ref, by2_ref, by3_ref)]
-    out_ref[...] = jnp.concatenate(lists + [jnp.zeros((4, LANES), f32)], axis=0)
+    out_ref[0:8, :] = jnp.concatenate(lists + [jnp.zeros((4, LANES), f32)], axis=0)
+    rows = pl.ds(pl.multiple_of(lax.axis_index("c") * 2 * BLOCK, 2 * BLOCK), 2 * BLOCK)
+    out_ref[8:16, :] = squares(targets_ref[rows, :])
 
 
 def first_rows(own_ref, by1_ref, by2_ref, by3_ref, targets_ref, lists_ref, potential_ref, out_ref, sources_ref, source_squares_ref, target_squares_ref, kept_ref, *scratch):
     y, c = lax.axis_index("y"), lax.axis_index("c")
     kept = jnp.zeros((1, LANES), f32)
     for c_from in range(2):
-        lists = lists_ref[c_from]
+        lists = lists_ref[c_from, 0:8, :]
         for by in range(4):
             kept = kept + bits(lists[by:by + 1, :], (y + 4 - by) & 3, c_from, y, c)
     kept_ref[...] = jnp.broadcast_to(kept, kept_ref.shape)
     for by, ref in enumerate((own_ref, by1_ref, by2_ref, by3_ref)):
         sources_ref[pl.ds(pl.multiple_of(((y + 4 - by) & 3) * BLOCK, BLOCK), BLOCK), :] = ref[0:BLOCK, :]
     source_squares_ref[...] = squares(own_ref[0:BLOCK, :])
-    squared = squares(targets_ref[...])
+    squared = jnp.concatenate([lists_ref[0, 8:16, :], lists_ref[1, 8:16, :]], axis=0)
     target_squares_ref[...] = squared
     rows = pl.ds(pl.multiple_of(y * 8, 8), 8)
     potential = jnp.concatenate([potential_ref[0, rows, :], potential_ref[1, rows, :]], axis=0)
@@ -414,7 +428,7 @@
     targets = spread(jnp.broadcast_to(target_points[None], (n_z, own, EMB)), "z").reshape(n_z * own, EMB)
     targets = lax.all_gather(targets, "c", axis=0, tiled=True)
     potential = lax.all_gather(initial_potential.reshape(n_y * tgt_rows, LANES), "c")
-    lists = lax.all_gather(call(packed, shape(8, LANES), (sources, *by, targets), []), "c")
+    lists = lax.all_gather(call(packed, shape(16, LANES), (sources, *by, targets), []), "c")
     row_shape = shape(16, 16, LANES)
     row_parts, sources, source_squares, target_squares, kept = call(
         first_rows,

time: 89.8 us -> 89.6 us (level)
  blocking collectives: 59.6 us -> 62.7 us
  Pallas kernels: 10.2 us -> 7.54 us
    all_to_all x4, blocking collectives: 51.8 us -> 54.9 us  [spread(): return lax.all_to_all(parts, axes, 0, 0, tiled=True)]
    pallas_call x7, Pallas kernels: 10.2 us -> 7.54 us  [call(): pl.pallas_call(kernel, out_shape=out_shape, in_specs=[VMEM] * len(operand...]
where the time goes in v9:
time: 89.6 us; the launch traced here: 89.5 us
  blocking collectives  62.7 us (70%)
  starting transfers between devices  13.3 us (15%)
  Pallas kernels  7.54 us (8%)
  waiting for transfers between devices  3.08 us (3%)
  local copies, waits for them, and re-layouts  1.55 us (2%)
    all_to_all x4, blocking collectives, spread(): return lax.all_to_all(parts, axes, 0, 0, tiled=True)  54.9 us
    all_to_all x1, starting transfers between devices, spread(): return lax.all_to_all(parts, axes, 0, 0, tiled=True)  8.57 us
    pallas_call x7, Pallas kernels, call(): pl.pallas_call(kernel, out_shape=out_shape, in_specs=[VMEM] * len(operand...  7.54 us
    ppermute x3, starting transfers between devices, per_device(): lax.ppermute(sources, 'y', [(i, (i + k) % n_y) for i in range(n_y)])  4.69 us
    all_to_all x1, waiting for transfers between devices, spread(): return lax.all_to_all(parts, axes, 0, 0, tiled=True)  3.01 us
    all_gather x1, blocking collectives, per_device(): targets = lax.all_gather(targets, 'c', axis=0, tiled=True)  2.17 us
    all_gather x1, blocking collectives, per_device(): lax.all_gather(initial_potential.reshape(n_y * tgt_rows, LANES), 'c')  2.03 us
    all_gather x1, blocking collectives, per_device(): parts = lax.all_gather(parts, 'c')  1.82 us
  transfers between devices with their start and end apart: 4, of which 2 were waited for; matrix products, arithmetic and copies ran while one was open for 1% of the time, Pallas kernels for 0%

profile of v9, /device:TPU:32, one launch (start us, length us, event | category | flops | bytes accessed | tf_op | source)
XLA Modules:
  0.0 89.5 jit_solution(3862126917634297195)
XLA Ops:
  0.6 0.0 copy-start
  0.6 1.5 %broadcast_in_dim.2 = bf16[8,128,128]{2,1,0:T(8,128)(2,1)} broadcast(bf16[128,128]{1,0:T(8,128)(2,1)} %param.6), dimensions={1,2} | broadcast | bytes 294912 | tf_op jit(solution)/shard_map/broadcast_in_dim | solution.py:428
  2.2 8.6 %all-to-all-start = ((bf16[8,128,128]{2,1,0:T(8,128)(2,1)}), bf16[8,128,128]{2,1,0:T(8,128)(2,1)S(1)}, u32[]{:S(2)}, u32[]{:S(2)}) async-start(bf16[8,128,128]{2,1,0:T(8,128)(2,1)} %broadcast_in_dim.2), calls=%async_computation | async-start | bytes 524288 | tf_op jit(solution)/shard_map/all_to_all | solution.py:396
  10.7 0.0 copy-done
  10.8 0.7 convert_bitcast_fusion
  11.4 3.1 %collective-permute-start.2 = (bf16[528,128]{1,0:T(8,128)(2,1)S(1)}, bf16[528,128]{1,0:T(8,128)(2,1)S(1)}, u32[]{:S(2)}, u32[]{:S(2)}) collective-permute-start(bf16[528,128]{1,0:T(8,128)(2,1)S(1)} %fusion.1.own_ref), channel_id=1, source_target_pairs={{0,192},{64,0},{128,64},{192,128},{1,193},{65,1},{129,65},{193,129... | collective-permute-start | bytes 405512 | tf_op jit(solution)/shard_map/ppermute | solution.py:426
  14.5 0.6 collective-permute-start.1
  15.2 1.0 %collective-permute-start = (bf16[528,128]{1,0:T(8,128)(2,1)S(1)}, bf16[528,128]{1,0:T(8,128)(2,1)S(1)}, u32[]{:S(2)}, u32[]{:S(2)}) collective-permute-start(bf16[528,128]{1,0:T(8,128)(2,1)S(1)} %fusion.1.own_ref), channel_id=1, source_target_pairs={{0,64},{64,128},{128,192},{192,0},{1,65},{65,129},{129,193},{193,1... | collective-permute-start | bytes 405512 | tf_op jit(solution)/shard_map/ppermute | solution.py:426
  16.1 2.0 %all_gather.21.potential_ref = f32[2,32,128]{2,1,0:T(8,128)S(1)} all-gather(f32[1,32,128]{2,1,0:T(8,128)} %bitcast.12), channel_id=1, replica_groups=mesh['y'=4,'z'=8,'x'=4,'c'=2] {'c'}, dimensions={0}, use_global_device_ids=true | all-gather | bytes 49152 | tf_op jit(solution)/shard_map/all_gather | solution.py:430
  18.2 3.0 %all-to-all-done = bf16[8,128,128]{2,1,0:T(8,128)(2,1)S(1)} async-done(((bf16[8,128,128]{2,1,0:T(8,128)(2,1)}), bf16[8,128,128]{2,1,0:T(8,128)(2,1)S(1)}, u32[]{:S(2)}, u32[]{:S(2)}) %all-to-all-start) | async-done | bytes 262176 | tf_op jit(solution)/shard_map/all_to_all | solution.py:396
  21.2 2.2 %all_gather.18.targets_ref = bf16[2048,128]{1,0:T(8,128)(2,1)S(1)} all-gather(bf16[1024,128]{1,0:T(8,128)(2,1)S(1)} %bitcast.11), channel_id=1, replica_groups=mesh['y'=4,'z'=8,'x'=4,'c'=2] {'c'}, dimensions={0}, use_global_device_ids=true | all-gather | bytes 786432 | tf_op jit(solution)/shard_map/all_gather | solution.py:429
  23.3 0.0 collective-permute-done.2.by3_ref
  23.3 0.0 collective-permute-done.1.by2_ref
  23.3 0.1 collective-permute-done.by1_ref
  23.4 0.2 shard_map.59
  23.7 1.8 %all-gather = f32[32,128]{1,0:T(8,128)S(1)} all-gather(f32[16,128]{1,0:T(8,128)S(1)} %shard_map.59), channel_id=2, replica_groups=mesh['y'=4,'z'=8,'x'=4,'c'=2] {'c'}, dimensions={0}, use_global_device_ids=true | all-gather | bytes 24576 | tf_op jit(solution)/shard_map/all_gather | solution.py:431
  25.5 2.0 %shard_map.60 = (f32[16,16,128]{2,1,0:T(8,128)S(1)}, bf16[2048,128]{1,0:T(8,128)(2,1)S(1)}, f32[4,128]{1,0:T(4,128)S(1)}, f32[16,128]{1,0:T(8,128)S(1)}, f32[8,128]{1,0:T(8,128)S(1)}) custom-call(bf16[528,128]{1,0:T(8,128)(2,1)S(1)} %fusion.1.own_ref, bf16[528,128]{1,0:T(8,128)(2,1)S(1)} %collective-permute-done.by1_ref, ...), custom_call_target="tpu_custom_call" | custom-call | flops 1073741824 | bytes 4194304 | tf_op jit(solution)/shard_map/pallas_call | solution.py:400
  27.5 14.5 %all_to_all.25.parts_ref = f32[16,16,128]{2,1,0:T(8,128)S(1)} all-to-all(f32[16,16,128]{2,1,0:T(8,128)S(1)} %get-tuple-element.17), channel_id=1, replica_groups=mesh['y'=4,'z'=8,'x'=4,'c'=2] {'y','x'}, dimensions={0} | all-to-all | bytes 262144 | tf_op jit(solution)/shard_map/all_to_all | solution.py:396
  42.0 2.0 %shard_map.61 = (f32[16,16,128]{2,1,0:T(8,128)S(1)}, f32[16,128]{1,0:T(8,128)S(1)}, f32[16,512,512]{2,1,0:T(8,128)S(1)}, f32[16,512]{1,0:T(8,128)S(1)}) custom-call(f32[8,128]{1,0:T(8,128)S(1)} %get-tuple-element.13.kept_ref, bf16[2048,128]{1,0:T(8,128)(2,1)S(1)} %get-tuple-element.14.sources_ref, bf16[2048,128]{1,0:T(8,128)(2,1)S(1)} %all_gather.18.targets_ref, ...), custom_call_target="tpu_custom_call" | custom-call | flops 1073741824 | bytes 4194304 | tf_op jit(solution)/shard_map/pallas_call | solution.py:400
  44.1 12.7 %all_to_all.26.parts_ref = f32[16,16,128]{2,1,0:T(8,128)S(1)} all-to-all(f32[16,16,128]{2,1,0:T(8,128)S(1)} %get-tuple-element.21), channel_id=1, replica_groups=mesh['y'=4,'z'=8,'x'=4,'c'=2] {'z','c'}, dimensions={0} | all-to-all | bytes 262144 | tf_op jit(solution)/shard_map/all_to_all | solution.py:396
  56.8 1.2 %shard_map.62 = f32[16,16,128]{2,1,0:T(8,128)S(1)} custom-call(f32[8,128]{1,0:T(8,128)S(1)} %get-tuple-element.13.kept_ref, bf16[2048,128]{1,0:T(8,128)(2,1)S(1)} %get-tuple-element.14.sources_ref, bf16[2048,128]{1,0:T(8,128)(2,1)S(1)} %all_gather.18.targets_ref, f32[16,128]{1,0:T(8,128)S(1)} %get-tuple-element.18.old_bias_ref, ...), custom_call_target="tpu_custom_call" | custom-call | flops 1073741824 | bytes 4194304 | tf_op jit(solution)/shard_map/pallas_call | solution.py:400
  57.9 12.4 %all_to_all.27.parts_ref = f32[16,16,128]{2,1,0:T(8,128)S(1)} all-to-all(f32[16,16,128]{2,1,0:T(8,128)S(1)} %shard_map.62), channel_id=1, replica_groups=mesh['y'=4,'z'=8,'x'=4,'c'=2] {'y','x'}, dimensions={0} | all-to-all | bytes 262144 | tf_op jit(solution)/shard_map/all_to_all | solution.py:396
  70.4 1.4 %shard_map.63 = f32[24,128]{1,0:T(8,128)S(1)} custom-call(f32[8,128]{1,0:T(8,128)S(1)} %get-tuple-element.13.kept_ref, bf16[2048,128]{1,0:T(8,128)(2,1)S(1)} %get-tuple-element.14.sources_ref, bf16[2048,128]{1,0:T(8,128)(2,1)S(1)} %all_gather.18.targets_ref, f32[4,128]{1,0:T(4,128)S(1)} %get-tuple-element.15.source_squares_ref, ...), custom_call_target="tpu_custom_call" | custom-call | flops 1073741824 | bytes 4194304 | tf_op jit(solution)/shard_map/pallas_call | solution.py:400
  71.8 1.8 %all-gather.1 = f32[48,128]{1,0:T(8,128)S(1)} all-gather(f32[24,128]{1,0:T(8,128)S(1)} %shard_map.63), channel_id=3, replica_groups=mesh['y'=4,'z'=8,'x'=4,'c'=2] {'c'}, dimensions={0}, use_global_device_ids=true | all-gather | bytes 36864 | tf_op jit(solution)/shard_map/all_gather | solution.py:466
  73.6 15.2 %all_to_all.28.parts_ref = f32[32,8,128]{2,1,0:T(8,128)S(1)} all-to-all(f32[32,8,128]{2,1,0:T(8,128)S(1)} %shard_map.64), channel_id=1, replica_groups=mesh['y'=4,'z'=8,'x'=4,'c'=2] {'y','z'}, dimensions={0} | all-to-all | bytes 262144 | tf_op jit(solution)/shard_map/all_to_all | solution.py:396
  88.8 0.7 shard_map.65
  (3 shorter events, 0.0 us)
Async XLA Ops:
  0.6 10.1 %copy-start = (bf16[1024,128]{1,0:T(8,128)(2,1)S(1)}, bf16[1024,128]{1,0:T(8,128)(2,1)}, u32[]{:S(2)}) copy-start(bf16[1024,128]{1,0:T(8,128)(2,1)} %param.5) | copy-start | bytes 786436
  2.2 19.0 %all-to-all-start = ((bf16[8,128,128]{2,1,0:T(8,128)(2,1)}), bf16[8,128,128]{2,1,0:T(8,128)(2,1)S(1)}, u32[]{:S(2)}, u32[]{:S(2)}) async-start(bf16[8,128,128]{2,1,0:T(8,128)(2,1)} %broadcast_in_dim.2), calls=%async_computation | async-start | bytes 524288 | tf_op jit(solution)/shard_map/all_to_all | solution.py:396
  11.4 11.9 %collective-permute-start.2 = (bf16[528,128]{1,0:T(8,128)(2,1)S(1)}, bf16[528,128]{1,0:T(8,128)(2,1)S(1)}, u32[]{:S(2)}, u32[]{:S(2)}) collective-permute-start(bf16[528,128]{1,0:T(8,128)(2,1)S(1)} %fusion.1.own_ref), channel_id=1, source_target_pairs={{0,192},{64,0},{128,64},{192,128},{1,193},{65,1},{129,65},{193,129... | collective-permute-start | bytes 405512 | tf_op jit(solution)/shard_map/ppermute | solution.py:426
  14.5 8.8 %collective-permute-start.1 = (bf16[528,128]{1,0:T(8,128)(2,1)S(1)}, bf16[528,128]{1,0:T(8,128)(2,1)S(1)}, u32[]{:S(2)}, u32[]{:S(2)}) collective-permute-start(bf16[528,128]{1,0:T(8,128)(2,1)S(1)} %fusion.1.own_ref), channel_id=1, source_target_pairs={{0,128},{64,192},{128,0},{192,64},{1,129},{65,193},{129,1},{193,65... | collective-permute-start | bytes 405512 | tf_op jit(solution)/shard_map/ppermute | solution.py:426
  15.2 8.3 %collective-permute-start = (bf16[528,128]{1,0:T(8,128)(2,1)S(1)}, bf16[528,128]{1,0:T(8,128)(2,1)S(1)}, u32[]{:S(2)}, u32[]{:S(2)}) collective-permute-start(bf16[528,128]{1,0:T(8,128)(2,1)S(1)} %fusion.1.own_ref), channel_id=1, source_target_pairs={{0,64},{64,128},{128,192},{192,0},{1,65},{65,129},{129,193},{193,1... | collective-permute-start | bytes 405512 | tf_op jit(solution)/shard_map/ppermute | solution.py:426

commit v10 on v9

--- a/solution.py
+++ b/solution.py
@@ -221,25 +221,23 @@
     return jnp.where(mine, jnp.left_shift(jnp.ones_like(pair), number), 0).astype(f32)
 
 
-def packed(own_ref, by1_ref, by2_ref, by3_ref, targets_ref, out_ref):
+def packed(own_ref, by1_ref, by2_ref, by3_ref, after_ref, out_ref):
     lists = [ref[BLOCK:BLOCK + 16, :].astype(f32)[0:1, :] for ref in (own_ref, by1_ref, by2_ref, by3_ref)]
-    out_ref[0:8, :] = jnp.concatenate(lists + [jnp.zeros((4, LANES), f32)], axis=0)
-    rows = pl.ds(pl.multiple_of(lax.axis_index("c") * 2 * BLOCK, 2 * BLOCK), 2 * BLOCK)
-    out_ref[8:16, :] = squares(targets_ref[rows, :])
+    out_ref[...] = jnp.concatenate(lists + [jnp.zeros((4, LANES), f32)], axis=0)
 
 
 def first_rows(own_ref, by1_ref, by2_ref, by3_ref, targets_ref, lists_ref, potential_ref, out_ref, sources_ref, source_squares_ref, target_squares_ref, kept_ref, *scratch):
     y, c = lax.axis_index("y"), lax.axis_index("c")
     kept = jnp.zeros((1, LANES), f32)
     for c_from in range(2):
-        lists = lists_ref[c_from, 0:8, :]
+        lists = lists_ref[c_from]
         for by in range(4):
             kept = kept + bits(lists[by:by + 1, :], (y + 4 - by) & 3, c_from, y, c)
     kept_ref[...] = jnp.broadcast_to(kept, kept_ref.shape)
     for by, ref in enumerate((own_ref, by1_ref, by2_ref, by3_ref)):
         sources_ref[pl.ds(pl.multiple_of(((y + 4 - by) & 3) * BLOCK, BLOCK), BLOCK), :] = ref[0:BLOCK, :]
     source_squares_ref[...] = squares(own_ref[0:BLOCK, :])
-    squared = jnp.concatenate([lists_ref[0, 8:16, :], lists_ref[1, 8:16, :]], axis=0)
+    squared = squares(targets_ref[...])
     target_squares_ref[...] = squared
     rows = pl.ds(pl.multiple_of(y * 8, 8), 8)
     potential = jnp.concatenate([potential_ref[0, rows, :], potential_ref[1, rows, :]], axis=0)
@@ -381,9 +379,8 @@
 def last_potentials(parts_ref, cores_ref, source_ref, target_ref):
     for b in range(2):
         source_ref[b * GROUPS:(b + 1) * GROUPS, :] = cores_ref[b, 16:16 + GROUPS, :]
-    count = parts_ref.shape[0] // 4
     for y in range(4):
-        lse = combined(parts_ref[y * count:(y + 1) * count])
+        lse = combined(jnp.stack([parts_ref[k] for k in range(y, parts_ref.shape[0], 4)]))
         target_ref[y * 8:(y + 1) * 8, :] = 2.0 * half_bias(lse)
 
 
@@ -428,7 +425,7 @@
     targets = spread(jnp.broadcast_to(target_points[None], (n_z, own, EMB)), "z").reshape(n_z * own, EMB)
     targets = lax.all_gather(targets, "c", axis=0, tiled=True)
     potential = lax.all_gather(initial_potential.reshape(n_y * tgt_rows, LANES), "c")
-    lists = lax.all_gather(call(packed, shape(16, LANES), (sources, *by, targets), []), "c")
+    lists = lax.all_gather(call(packed, shape(8, LANES), (sources, *by, targets), []), "c")
     row_shape = shape(16, 16, LANES)
     row_parts, sources, source_squares, target_squares, kept = call(
         first_rows,
@@ -465,7 +462,7 @@
     )
     parts = lax.all_gather(parts, "c")
     col_parts = call(both_cores, shape(n_y * n_z, tgt_rows, LANES), (parts,), [])
-    col_parts = spread(col_parts, ("y", "z"))
+    col_parts = spread(col_parts, ("z", "y"))
     source_potential, target_potential = call(
         last_potentials, [shape(2 * GROUPS, LANES), shape(n_y * tgt_rows, LANES)], (col_parts, parts), []
     )

time: 89.6 us -> 89.9 us (level)
  Pallas kernels: 7.54 us -> 9.66 us
  blocking collectives: 62.7 us -> 60.8 us
    pallas_call x7, Pallas kernels: 7.54 us -> 9.66 us  [call(): pl.pallas_call(kernel, out_shape=out_shape, in_specs=[VMEM] * len(operand...]
    all_to_all x4, blocking collectives: 54.9 us -> 53 us  [spread(): return lax.all_to_all(parts, axes, 0, 0, tiled=True)]
where the time goes in v10:
time: 89.9 us; the launch traced here: 89.8 us
  blocking collectives  60.8 us (68%)
  starting transfers between devices  13.3 us (15%)
  Pallas kernels  9.66 us (11%)
  waiting for transfers between devices  3.08 us (3%)
  local copies, waits for them, and re-layouts  1.55 us (2%)
    all_to_all x4, blocking collectives, spread(): return lax.all_to_all(parts, axes, 0, 0, tiled=True)  53 us
    pallas_call x7, Pallas kernels, call(): pl.pallas_call(kernel, out_shape=out_shape, in_specs=[VMEM] * len(operand...  9.66 us
    all_to_all x1, starting transfers between devices, spread(): return lax.all_to_all(parts, axes, 0, 0, tiled=True)  8.57 us
    ppermute x3, starting transfers between devices, per_device(): lax.ppermute(sources, 'y', [(i, (i + k) % n_y) for i in range(n_y)])  4.69 us
    all_to_all x1, waiting for transfers between devices, spread(): return lax.all_to_all(parts, axes, 0, 0, tiled=True)  3.01 us
    all_gather x1, blocking collectives, per_device(): targets = lax.all_gather(targets, 'c', axis=0, tiled=True)  2.17 us
    all_gather x1, blocking collectives, per_device(): lax.all_gather(initial_potential.reshape(n_y * tgt_rows, LANES), 'c')  2.03 us
    all_gather x1, blocking collectives, per_device(): parts = lax.all_gather(parts, 'c')  1.82 us
  transfers between devices with their start and end apart: 4, of which 2 were waited for; matrix products, arithmetic and copies ran while one was open for 1% of the time, Pallas kernels for 0%

profile of v10, /device:TPU:32, one launch (start us, length us, event | category | flops | bytes accessed | tf_op | source)
XLA Modules:
  0.0 89.8 jit_solution(7599620912322703136)
XLA Ops:
  0.6 0.0 copy-start
  0.6 1.5 %broadcast_in_dim.2 = bf16[8,128,128]{2,1,0:T(8,128)(2,1)} broadcast(bf16[128,128]{1,0:T(8,128)(2,1)} %param.6), dimensions={1,2} | broadcast | bytes 294912 | tf_op jit(solution)/shard_map/broadcast_in_dim | solution.py:425
  2.2 8.6 %all-to-all-start = ((bf16[8,128,128]{2,1,0:T(8,128)(2,1)}), bf16[8,128,128]{2,1,0:T(8,128)(2,1)S(1)}, u32[]{:S(2)}, u32[]{:S(2)}) async-start(bf16[8,128,128]{2,1,0:T(8,128)(2,1)} %broadcast_in_dim.2), calls=%async_computation | async-start | bytes 524288 | tf_op jit(solution)/shard_map/all_to_all | solution.py:393
  10.7 0.0 copy-done
  10.8 0.7 convert_bitcast_fusion
  11.4 3.1 %collective-permute-start.2 = (bf16[528,128]{1,0:T(8,128)(2,1)S(1)}, bf16[528,128]{1,0:T(8,128)(2,1)S(1)}, u32[]{:S(2)}, u32[]{:S(2)}) collective-permute-start(bf16[528,128]{1,0:T(8,128)(2,1)S(1)} %fusion.1.own_ref), channel_id=1, source_target_pairs={{0,192},{64,0},{128,64},{192,128},{1,193},{65,1},{129,65},{193,129... | collective-permute-start | bytes 405512 | tf_op jit(solution)/shard_map/ppermute | solution.py:423
  14.5 0.6 collective-permute-start.1
  15.2 1.0 %collective-permute-start = (bf16[528,128]{1,0:T(8,128)(2,1)S(1)}, bf16[528,128]{1,0:T(8,128)(2,1)S(1)}, u32[]{:S(2)}, u32[]{:S(2)}) collective-permute-start(bf16[528,128]{1,0:T(8,128)(2,1)S(1)} %fusion.1.own_ref), channel_id=1, source_target_pairs={{0,64},{64,128},{128,192},{192,0},{1,65},{65,129},{129,193},{193,1... | collective-permute-start | bytes 405512 | tf_op jit(solution)/shard_map/ppermute | solution.py:423
  16.1 2.0 %all_gather.21.potential_ref = f32[2,32,128]{2,1,0:T(8,128)S(1)} all-gather(f32[1,32,128]{2,1,0:T(8,128)} %bitcast.12), channel_id=1, replica_groups=mesh['y'=4,'z'=8,'x'=4,'c'=2] {'c'}, dimensions={0}, use_global_device_ids=true | all-gather | bytes 49152 | tf_op jit(solution)/shard_map/all_gather | solution.py:427
  18.2 3.0 %all-to-all-done = bf16[8,128,128]{2,1,0:T(8,128)(2,1)S(1)} async-done(((bf16[8,128,128]{2,1,0:T(8,128)(2,1)}), bf16[8,128,128]{2,1,0:T(8,128)(2,1)S(1)}, u32[]{:S(2)}, u32[]{:S(2)}) %all-to-all-start) | async-done | bytes 262176 | tf_op jit(solution)/shard_map/all_to_all | solution.py:393
  21.2 2.2 %all_gather.18.after_ref.targets_ref = bf16[2048,128]{1,0:T(8,128)(2,1)S(1)} all-gather(bf16[1024,128]{1,0:T(8,128)(2,1)S(1)} %bitcast.11), channel_id=1, replica_groups=mesh['y'=4,'z'=8,'x'=4,'c'=2] {'c'}, dimensions={0}, use_global_device_ids=true | all-gather | bytes 786432 | tf_op jit(solution)/shard_map/all_gather | solution.py:426
  23.3 0.0 collective-permute-done.2.by3_ref
  23.3 0.0 collective-permute-done.1.by2_ref
  23.3 0.1 collective-permute-done.by1_ref
  23.4 1.8 %all-gather = f32[16,128]{1,0:T(8,128)S(1)} all-gather(f32[8,128]{1,0:T(8,128)S(1)} %shard_map.59), channel_id=2, replica_groups=mesh['y'=4,'z'=8,'x'=4,'c'=2] {'c'}, dimensions={0}, use_global_device_ids=true | all-gather | bytes 12288 | tf_op jit(solution)/shard_map/all_gather | solution.py:428
  25.2 3.1 %shard_map.60 = (f32[16,16,128]{2,1,0:T(8,128)S(1)}, bf16[2048,128]{1,0:T(8,128)(2,1)S(1)}, f32[4,128]{1,0:T(4,128)S(1)}, f32[16,128]{1,0:T(8,128)S(1)}, f32[8,128]{1,0:T(8,128)S(1)}) custom-call(bf16[528,128]{1,0:T(8,128)(2,1)S(1)} %fusion.1.own_ref, bf16[528,128]{1,0:T(8,128)(2,1)S(1)} %collective-permute-done.by1_ref, ...), custom_call_target="tpu_custom_call" | custom-call | flops 1073741824 | bytes 4194304 | tf_op jit(solution)/shard_map/pallas_call | solution.py:397
  28.3 15.0 %all_to_all.25.parts_ref = f32[16,16,128]{2,1,0:T(8,128)S(1)} all-to-all(f32[16,16,128]{2,1,0:T(8,128)S(1)} %get-tuple-element.17), channel_id=1, replica_groups=mesh['y'=4,'z'=8,'x'=4,'c'=2] {'y','x'}, dimensions={0} | all-to-all | bytes 262144 | tf_op jit(solution)/shard_map/all_to_all | solution.py:393
  43.3 2.8 %shard_map.61 = (f32[16,16,128]{2,1,0:T(8,128)S(1)}, f32[16,128]{1,0:T(8,128)S(1)}, f32[16,512,512]{2,1,0:T(8,128)S(1)}, f32[16,512]{1,0:T(8,128)S(1)}) custom-call(f32[8,128]{1,0:T(8,128)S(1)} %get-tuple-element.13.kept_ref, bf16[2048,128]{1,0:T(8,128)(2,1)S(1)} %get-tuple-element.14.sources_ref, bf16[2048,128]{1,0:T(8,128)(2,1)S(1)} %all_gather.18.after_ref.targets_ref, ...), custom_call_target="tpu_custom_call" | custom-call | flops 1073741824 | bytes 4194304 | tf_op jit(solution)/shard_map/pallas_call | solution.py:397
  46.1 11.4 %all_to_all.26.parts_ref = f32[16,16,128]{2,1,0:T(8,128)S(1)} all-to-all(f32[16,16,128]{2,1,0:T(8,128)S(1)} %get-tuple-element.21), channel_id=1, replica_groups=mesh['y'=4,'z'=8,'x'=4,'c'=2] {'z','c'}, dimensions={0} | all-to-all | bytes 262144 | tf_op jit(solution)/shard_map/all_to_all | solution.py:393
  57.5 1.4 %shard_map.62 = f32[16,16,128]{2,1,0:T(8,128)S(1)} custom-call(f32[8,128]{1,0:T(8,128)S(1)} %get-tuple-element.13.kept_ref, bf16[2048,128]{1,0:T(8,128)(2,1)S(1)} %get-tuple-element.14.sources_ref, bf16[2048,128]{1,0:T(8,128)(2,1)S(1)} %all_gather.18.after_ref.targets_ref, f32[16,128]{1,0:T(8,128)S(1)} %get-tuple-element.18.old_bias_ref, ...), custom_call_target="tpu_custom_call" | custom-call | flops 1073741824 | bytes 4194304 | tf_op jit(solution)/shard_map/pallas_call | solution.py:397
  59.0 11.8 %all_to_all.27.parts_ref = f32[16,16,128]{2,1,0:T(8,128)S(1)} all-to-all(f32[16,16,128]{2,1,0:T(8,128)S(1)} %shard_map.62), channel_id=1, replica_groups=mesh['y'=4,'z'=8,'x'=4,'c'=2] {'y','x'}, dimensions={0} | all-to-all | bytes 262144 | tf_op jit(solution)/shard_map/all_to_all | solution.py:393
  70.8 1.7 %shard_map.63 = f32[24,128]{1,0:T(8,128)S(1)} custom-call(f32[8,128]{1,0:T(8,128)S(1)} %get-tuple-element.13.kept_ref, bf16[2048,128]{1,0:T(8,128)(2,1)S(1)} %get-tuple-element.14.sources_ref, bf16[2048,128]{1,0:T(8,128)(2,1)S(1)} %all_gather.18.after_ref.targets_ref, f32[4,128]{1,0:T(4,128)S(1)} %get-tuple-element.15.source_squares_ref, ...), custom_call_target="tpu_custom_call" | custom-call | flops 1073741824 | bytes 4194304 | tf_op jit(solution)/shard_map/pallas_call | solution.py:397
  72.5 1.8 %all-gather.1 = f32[48,128]{1,0:T(8,128)S(1)} all-gather(f32[24,128]{1,0:T(8,128)S(1)} %shard_map.63), channel_id=3, replica_groups=mesh['y'=4,'z'=8,'x'=4,'c'=2] {'c'}, dimensions={0}, use_global_device_ids=true | all-gather | bytes 36864 | tf_op jit(solution)/shard_map/all_gather | solution.py:463
  74.4 14.7 %all_to_all.28.parts_ref = f32[32,8,128]{2,1,0:T(8,128)S(1)} all-to-all(f32[32,8,128]{2,1,0:T(8,128)S(1)} %shard_map.64), channel_id=1, replica_groups=mesh['y'=4,'z'=8,'x'=4,'c'=2] {'z','y'}, dimensions={0} | all-to-all | bytes 262144 | tf_op jit(solution)/shard_map/all_to_all | solution.py:393
  89.1 0.7 shard_map.65
  (4 shorter events, 0.1 us)
Async XLA Ops:
  0.6 10.1 %copy-start = (bf16[1024,128]{1,0:T(8,128)(2,1)S(1)}, bf16[1024,128]{1,0:T(8,128)(2,1)}, u32[]{:S(2)}) copy-start(bf16[1024,128]{1,0:T(8,128)(2,1)} %param.5) | copy-start | bytes 786436
  2.2 19.0 %all-to-all-start = ((bf16[8,128,128]{2,1,0:T(8,128)(2,1)}), bf16[8,128,128]{2,1,0:T(8,128)(2,1)S(1)}, u32[]{:S(2)}, u32[]{:S(2)}) async-start(bf16[8,128,128]{2,1,0:T(8,128)(2,1)} %broadcast_in_dim.2), calls=%async_computation | async-start | bytes 524288 | tf_op jit(solution)/shard_map/all_to_all | solution.py:393
  11.4 11.9 %collective-permute-start.2 = (bf16[528,128]{1,0:T(8,128)(2,1)S(1)}, bf16[528,128]{1,0:T(8,128)(2,1)S(1)}, u32[]{:S(2)}, u32[]{:S(2)}) collective-permute-start(bf16[528,128]{1,0:T(8,128)(2,1)S(1)} %fusion.1.own_ref), channel_id=1, source_target_pairs={{0,192},{64,0},{128,64},{192,128},{1,193},{65,1},{129,65},{193,129... | collective-permute-start | bytes 405512 | tf_op jit(solution)/shard_map/ppermute | solution.py:423
  14.5 8.8 %collective-permute-start.1 = (bf16[528,128]{1,0:T(8,128)(2,1)S(1)}, bf16[528,128]{1,0:T(8,128)(2,1)S(1)}, u32[]{:S(2)}, u32[]{:S(2)}) collective-permute-start(bf16[528,128]{1,0:T(8,128)(2,1)S(1)} %fusion.1.own_ref), channel_id=1, source_target_pairs={{0,128},{64,192},{128,0},{192,64},{1,129},{65,193},{129,1},{193,65... | collective-permute-start | bytes 405512 | tf_op jit(solution)/shard_map/ppermute | solution.py:423
  15.2 8.3 %collective-permute-start = (bf16[528,128]{1,0:T(8,128)(2,1)S(1)}, bf16[528,128]{1,0:T(8,128)(2,1)S(1)}, u32[]{:S(2)}, u32[]{:S(2)}) collective-permute-start(bf16[528,128]{1,0:T(8,128)(2,1)S(1)} %fusion.1.own_ref), channel_id=1, source_target_pairs={{0,64},{64,128},{128,192},{192,0},{1,65},{65,129},{129,193},{193,1... | collective-permute-start | bytes 405512 | tf_op jit(solution)/shard_map/ppermute | solution.py:423

commit v11 on v10

--- a/solution.py
+++ b/solution.py
@@ -379,8 +379,9 @@
 def last_potentials(parts_ref, cores_ref, source_ref, target_ref):
     for b in range(2):
         source_ref[b * GROUPS:(b + 1) * GROUPS, :] = cores_ref[b, 16:16 + GROUPS, :]
+    count = parts_ref.shape[0] // 4
     for y in range(4):
-        lse = combined(jnp.stack([parts_ref[k] for k in range(y, parts_ref.shape[0], 4)]))
+        lse = combined(parts_ref[y * count:(y + 1) * count])
         target_ref[y * 8:(y + 1) * 8, :] = 2.0 * half_bias(lse)
 
 
@@ -462,7 +463,7 @@
     )
     parts = lax.all_gather(parts, "c")
     col_parts = call(both_cores, shape(n_y * n_z, tgt_rows, LANES), (parts,), [])
-    col_parts = spread(col_parts, ("z", "y"))
+    col_parts = spread(col_parts, ("y", "z"))
     source_potential, target_potential = call(
         last_potentials, [shape(2 * GROUPS, LANES), shape(n_y * tgt_rows, LANES)], (col_parts, parts), []
     )

time: 89.9 us -> 89.8 us (level)
  no operation moved by 1% of the time
where the time goes in v11:
time: 89.8 us; the launch traced here: 89 us
  blocking collectives  60.7 us (68%)
  starting transfers between devices  13.3 us (15%)
  Pallas kernels  8.98 us (10%)
  waiting for transfers between devices  3.08 us (3%)
  local copies, waits for them, and re-layouts  1.55 us (2%)
    all_to_all x4, blocking collectives, spread(): return lax.all_to_all(parts, axes, 0, 0, tiled=True)  52.9 us
    pallas_call x7, Pallas kernels, call(): pl.pallas_call(kernel, out_shape=out_shape, in_specs=[VMEM] * len(operand...  8.98 us
    all_to_all x1, starting transfers between devices, spread(): return lax.all_to_all(parts, axes, 0, 0, tiled=True)  8.57 us
    ppermute x3, starting transfers between devices, per_device(): lax.ppermute(sources, 'y', [(i, (i + k) % n_y) for i in range(n_y)])  4.69 us
    all_to_all x1, waiting for transfers between devices, spread(): return lax.all_to_all(parts, axes, 0, 0, tiled=True)  3.01 us
    all_gather x1, blocking collectives, per_device(): targets = lax.all_gather(targets, 'c', axis=0, tiled=True)  2.17 us
    all_gather x1, blocking collectives, per_device(): lax.all_gather(initial_potential.reshape(n_y * tgt_rows, LANES), 'c')  2.03 us
    all_gather x1, blocking collectives, per_device(): parts = lax.all_gather(parts, 'c')  1.82 us
  transfers between devices with their start and end apart: 4, of which 2 were waited for; matrix products, arithmetic and copies ran while one was open for 1% of the time, Pallas kernels for 0%

profile of v11, /device:TPU:32, one launch (start us, length us, event | category | flops | bytes accessed | tf_op | source)
XLA Modules:
  0.0 89.0 jit_solution(18071526980635192463)
XLA Ops:
  0.6 0.0 copy-start
  0.6 1.5 %broadcast_in_dim.2 = bf16[8,128,128]{2,1,0:T(8,128)(2,1)} broadcast(bf16[128,128]{1,0:T(8,128)(2,1)} %param.6), dimensions={1,2} | broadcast | bytes 294912 | tf_op jit(solution)/shard_map/broadcast_in_dim | solution.py:426
  2.2 8.6 %all-to-all-start = ((bf16[8,128,128]{2,1,0:T(8,128)(2,1)}), bf16[8,128,128]{2,1,0:T(8,128)(2,1)S(1)}, u32[]{:S(2)}, u32[]{:S(2)}) async-start(bf16[8,128,128]{2,1,0:T(8,128)(2,1)} %broadcast_in_dim.2), calls=%async_computation | async-start | bytes 524288 | tf_op jit(solution)/shard_map/all_to_all | solution.py:394
  10.7 0.0 copy-done
  10.8 0.7 convert_bitcast_fusion
  11.4 3.1 %collective-permute-start.2 = (bf16[528,128]{1,0:T(8,128)(2,1)S(1)}, bf16[528,128]{1,0:T(8,128)(2,1)S(1)}, u32[]{:S(2)}, u32[]{:S(2)}) collective-permute-start(bf16[528,128]{1,0:T(8,128)(2,1)S(1)} %fusion.1.own_ref), channel_id=1, source_target_pairs={{0,192},{64,0},{128,64},{192,128},{1,193},{65,1},{129,65},{193,129... | collective-permute-start | bytes 405512 | tf_op jit(solution)/shard_map/ppermute | solution.py:424
  14.5 0.6 collective-permute-start.1
  15.2 1.0 %collective-permute-start = (bf16[528,128]{1,0:T(8,128)(2,1)S(1)}, bf16[528,128]{1,0:T(8,128)(2,1)S(1)}, u32[]{:S(2)}, u32[]{:S(2)}) collective-permute-start(bf16[528,128]{1,0:T(8,128)(2,1)S(1)} %fusion.1.own_ref), channel_id=1, source_target_pairs={{0,64},{64,128},{128,192},{192,0},{1,65},{65,129},{129,193},{193,1... | collective-permute-start | bytes 405512 | tf_op jit(solution)/shard_map/ppermute | solution.py:424
  16.1 2.0 %all_gather.21.potential_ref = f32[2,32,128]{2,1,0:T(8,128)S(1)} all-gather(f32[1,32,128]{2,1,0:T(8,128)} %bitcast.12), channel_id=1, replica_groups=mesh['y'=4,'z'=8,'x'=4,'c'=2] {'c'}, dimensions={0}, use_global_device_ids=true | all-gather | bytes 49152 | tf_op jit(solution)/shard_map/all_gather | solution.py:428
  18.2 3.0 %all-to-all-done = bf16[8,128,128]{2,1,0:T(8,128)(2,1)S(1)} async-done(((bf16[8,128,128]{2,1,0:T(8,128)(2,1)}), bf16[8,128,128]{2,1,0:T(8,128)(2,1)S(1)}, u32[]{:S(2)}, u32[]{:S(2)}) %all-to-all-start) | async-done | bytes 262176 | tf_op jit(solution)/shard_map/all_to_all | solution.py:394
  21.2 2.2 %all_gather.18.after_ref.targets_ref = bf16[2048,128]{1,0:T(8,128)(2,1)S(1)} all-gather(bf16[1024,128]{1,0:T(8,128)(2,1)S(1)} %bitcast.11), channel_id=1, replica_groups=mesh['y'=4,'z'=8,'x'=4,'c'=2] {'c'}, dimensions={0}, use_global_device_ids=true | all-gather | bytes 786432 | tf_op jit(solution)/shard_map/all_gather | solution.py:427
  23.3 0.0 collective-permute-done.2.by3_ref
  23.3 0.0 collective-permute-done.1.by2_ref
  23.3 0.1 collective-permute-done.by1_ref
  23.4 1.8 %all-gather = f32[16,128]{1,0:T(8,128)S(1)} all-gather(f32[8,128]{1,0:T(8,128)S(1)} %shard_map.59), channel_id=2, replica_groups=mesh['y'=4,'z'=8,'x'=4,'c'=2] {'c'}, dimensions={0}, use_global_device_ids=true | all-gather | bytes 12288 | tf_op jit(solution)/shard_map/all_gather | solution.py:429
  25.2 2.8 %shard_map.60 = (f32[16,16,128]{2,1,0:T(8,128)S(1)}, bf16[2048,128]{1,0:T(8,128)(2,1)S(1)}, f32[4,128]{1,0:T(4,128)S(1)}, f32[16,128]{1,0:T(8,128)S(1)}, f32[8,128]{1,0:T(8,128)S(1)}) custom-call(bf16[528,128]{1,0:T(8,128)(2,1)S(1)} %fusion.1.own_ref, bf16[528,128]{1,0:T(8,128)(2,1)S(1)} %collective-permute-done.by1_ref, ...), custom_call_target="tpu_custom_call" | custom-call | flops 1073741824 | bytes 4194304 | tf_op jit(solution)/shard_map/pallas_call | solution.py:398
  28.0 15.3 %all_to_all.25.parts_ref = f32[16,16,128]{2,1,0:T(8,128)S(1)} all-to-all(f32[16,16,128]{2,1,0:T(8,128)S(1)} %get-tuple-element.17), channel_id=1, replica_groups=mesh['y'=4,'z'=8,'x'=4,'c'=2] {'y','x'}, dimensions={0} | all-to-all | bytes 262144 | tf_op jit(solution)/shard_map/all_to_all | solution.py:394
  43.4 2.5 %shard_map.61 = (f32[16,16,128]{2,1,0:T(8,128)S(1)}, f32[16,128]{1,0:T(8,128)S(1)}, f32[16,512,512]{2,1,0:T(8,128)S(1)}, f32[16,512]{1,0:T(8,128)S(1)}) custom-call(f32[8,128]{1,0:T(8,128)S(1)} %get-tuple-element.13.kept_ref, bf16[2048,128]{1,0:T(8,128)(2,1)S(1)} %get-tuple-element.14.sources_ref, bf16[2048,128]{1,0:T(8,128)(2,1)S(1)} %all_gather.18.after_ref.targets_ref, ...), custom_call_target="tpu_custom_call" | custom-call | flops 1073741824 | bytes 4194304 | tf_op jit(solution)/shard_map/pallas_call | solution.py:398
  45.9 10.9 %all_to_all.26.parts_ref = f32[16,16,128]{2,1,0:T(8,128)S(1)} all-to-all(f32[16,16,128]{2,1,0:T(8,128)S(1)} %get-tuple-element.21), channel_id=1, replica_groups=mesh['y'=4,'z'=8,'x'=4,'c'=2] {'z','c'}, dimensions={0} | all-to-all | bytes 262144 | tf_op jit(solution)/shard_map/all_to_all | solution.py:394
  56.8 1.4 %shard_map.62 = f32[16,16,128]{2,1,0:T(8,128)S(1)} custom-call(f32[8,128]{1,0:T(8,128)S(1)} %get-tuple-element.13.kept_ref, bf16[2048,128]{1,0:T(8,128)(2,1)S(1)} %get-tuple-element.14.sources_ref, bf16[2048,128]{1,0:T(8,128)(2,1)S(1)} %all_gather.18.after_ref.targets_ref, f32[16,128]{1,0:T(8,128)S(1)} %get-tuple-element.18.old_bias_ref, ...), custom_call_target="tpu_custom_call" | custom-call | flops 1073741824 | bytes 4194304 | tf_op jit(solution)/shard_map/pallas_call | solution.py:398
  58.2 11.9 %all_to_all.27.parts_ref = f32[16,16,128]{2,1,0:T(8,128)S(1)} all-to-all(f32[16,16,128]{2,1,0:T(8,128)S(1)} %shard_map.62), channel_id=1, replica_groups=mesh['y'=4,'z'=8,'x'=4,'c'=2] {'y','x'}, dimensions={0} | all-to-all | bytes 262144 | tf_op jit(solution)/shard_map/all_to_all | solution.py:394
  70.1 1.6 %shard_map.63 = f32[24,128]{1,0:T(8,128)S(1)} custom-call(f32[8,128]{1,0:T(8,128)S(1)} %get-tuple-element.13.kept_ref, bf16[2048,128]{1,0:T(8,128)(2,1)S(1)} %get-tuple-element.14.sources_ref, bf16[2048,128]{1,0:T(8,128)(2,1)S(1)} %all_gather.18.after_ref.targets_ref, f32[4,128]{1,0:T(4,128)S(1)} %get-tuple-element.15.source_squares_ref, ...), custom_call_target="tpu_custom_call" | custom-call | flops 1073741824 | bytes 4194304 | tf_op jit(solution)/shard_map/pallas_call | solution.py:398
  71.7 1.8 %all-gather.1 = f32[48,128]{1,0:T(8,128)S(1)} all-gather(f32[24,128]{1,0:T(8,128)S(1)} %shard_map.63), channel_id=3, replica_groups=mesh['y'=4,'z'=8,'x'=4,'c'=2] {'c'}, dimensions={0}, use_global_device_ids=true | all-gather | bytes 36864 | tf_op jit(solution)/shard_map/all_gather | solution.py:464
  73.5 14.8 %all_to_all.28.parts_ref = f32[32,8,128]{2,1,0:T(8,128)S(1)} all-to-all(f32[32,8,128]{2,1,0:T(8,128)S(1)} %shard_map.64), channel_id=1, replica_groups=mesh['y'=4,'z'=8,'x'=4,'c'=2] {'y','z'}, dimensions={0} | all-to-all | bytes 262144 | tf_op jit(solution)/shard_map/all_to_all | solution.py:394
  88.3 0.7 shard_map.65
  (4 shorter events, 0.1 us)
Async XLA Ops:
  0.6 10.1 %copy-start = (bf16[1024,128]{1,0:T(8,128)(2,1)S(1)}, bf16[1024,128]{1,0:T(8,128)(2,1)}, u32[]{:S(2)}) copy-start(bf16[1024,128]{1,0:T(8,128)(2,1)} %param.5) | copy-start | bytes 786436
  2.2 19.0 %all-to-all-start = ((bf16[8,128,128]{2,1,0:T(8,128)(2,1)}), bf16[8,128,128]{2,1,0:T(8,128)(2,1)S(1)}, u32[]{:S(2)}, u32[]{:S(2)}) async-start(bf16[8,128,128]{2,1,0:T(8,128)(2,1)} %broadcast_in_dim.2), calls=%async_computation | async-start | bytes 524288 | tf_op jit(solution)/shard_map/all_to_all | solution.py:394
  11.4 11.9 %collective-permute-start.2 = (bf16[528,128]{1,0:T(8,128)(2,1)S(1)}, bf16[528,128]{1,0:T(8,128)(2,1)S(1)}, u32[]{:S(2)}, u32[]{:S(2)}) collective-permute-start(bf16[528,128]{1,0:T(8,128)(2,1)S(1)} %fusion.1.own_ref), channel_id=1, source_target_pairs={{0,192},{64,0},{128,64},{192,128},{1,193},{65,1},{129,65},{193,129... | collective-permute-start | bytes 405512 | tf_op jit(solution)/shard_map/ppermute | solution.py:424
  14.5 8.8 %collective-permute-start.1 = (bf16[528,128]{1,0:T(8,128)(2,1)S(1)}, bf16[528,128]{1,0:T(8,128)(2,1)S(1)}, u32[]{:S(2)}, u32[]{:S(2)}) collective-permute-start(bf16[528,128]{1,0:T(8,128)(2,1)S(1)} %fusion.1.own_ref), channel_id=1, source_target_pairs={{0,128},{64,192},{128,0},{192,64},{1,129},{65,193},{129,1},{193,65... | collective-permute-start | bytes 405512 | tf_op jit(solution)/shard_map/ppermute | solution.py:424
  15.2 8.3 %collective-permute-start = (bf16[528,128]{1,0:T(8,128)(2,1)S(1)}, bf16[528,128]{1,0:T(8,128)(2,1)S(1)}, u32[]{:S(2)}, u32[]{:S(2)}) collective-permute-start(bf16[528,128]{1,0:T(8,128)(2,1)S(1)} %fusion.1.own_ref), channel_id=1, source_target_pairs={{0,64},{64,128},{128,192},{192,0},{1,65},{65,129},{129,193},{193,1... | collective-permute-start | bytes 405512 | tf_op jit(solution)/shard_map/ppermute | solution.py:424
